TPU v7x, 128 devices: a whole 4x4x4 slice. The times are simulated.
128 devices in a mesh: tm: 4 (over z), row: 4 (over y), col: 8 (over x, core).
Axes of the slice: x: 4, y: 4, z: 4, core: 2. Of those that a mesh axis runs over, the one named last changes fastest.
Arguments:
- features: bfloat16 [8, 32, 256, 384], P('tm', 'row', 'col'), may hold values from -6 to 6
- conv_first: bfloat16 [3, 3, 3, 384, 192], replicated, may hold values from -0.0625 to 0.0625
- conv_second: bfloat16 [3, 3, 3, 192, 192], replicated, may hold values from -0.078125 to 0.078125
- shortcut_weight: bfloat16 [384, 192], replicated, may hold values from -0.3125 to 0.3125
- head_weight: bfloat16 [192, 3], replicated, may hold values from -0.4375 to 0.4375
- target_frames: float32 [3, 8, 32, 256], P(None, 'tm', 'row', 'col'), may hold values from -4 to 4
Outputs:
- grad_first: float32 [3, 3, 3, 384, 192], replicated
- grad_second: float32 [3, 3, 3, 192, 192], replicated
- grad_shortcut: float32 [384, 192], replicated
- grad_head: float32 [192, 3], replicated
- loss_mean: float32 [], replicated
All inputs are finite; a program needn't handle non-finite values.
Results may differ from a plain program's by a relative error of at most 0.0038.
Values may be sent and summed in bfloat16 or wider, within the bound.
A program may use at most 128 MiB of HBM per device.

v0:
```python
import jax
import jax.numpy as jnp
from jax import lax
from jax.sharding import PartitionSpec as P

EPSILON = 1e-06
HUBER_BETA = 0.05
SSIM_CONST_A = 0.0004
SSIM_CONST_B = 0.0036


def shifted(value, axis, steps):
    count = lax.axis_size(axis)
    initial, last = (max(0, -steps), min(count, count - steps))
    return lax.ppermute(value, axis, [(source, source + steps) for source in range(initial, last)])


def padded_2(cells, sides, width):
    for axis, dim in sides:
        count = lax.axis_size(axis)
        ends = count - 1
        head = lax.slice_in_dim(cells, 0, width, axis=dim)
        tail = lax.slice_in_dim(cells, cells.shape[dim] - width, cells.shape[dim], axis=dim)
        cells = jnp.concatenate(
            [
                lax.ppermute(tail, axis, [(i, (i + 1) % count) for i in range(ends)]),
                cells,
                lax.ppermute(head, axis, [((i + 1) % count, i) for i in range(ends)]),
            ],
            axis=dim,
        )
    return cells


def normed_silu(values):
    inverse = lax.rsqrt(jnp.mean(values * values, axis=-1, keepdims=True) + EPSILON)
    return jax.nn.silu(values * inverse)


def gauss_weights():
    offsets = jnp.arange(11, dtype=jnp.float32) - 5.0
    kernel_taps = jnp.exp(-offsets * offsets / 4.5)
    return kernel_taps / jnp.sum(kernel_taps)


def blur_valid(padded, height, tile_width):
    kernel_taps = gauss_weights()
    row_pass = kernel_taps[0] * padded[..., 0:height, :]
    for offset in range(1, 11):
        row_pass = row_pass + kernel_taps[offset] * padded[..., offset : offset + height, :]
    result = kernel_taps[0] * row_pass[..., 0:tile_width]
    for offset in range(1, 11):
        result = result + kernel_taps[offset] * row_pass[..., offset : offset + tile_width]
    return result


def huber_loss(diff):
    magnitude = jnp.abs(diff)
    return jnp.where(
        magnitude < HUBER_BETA, 0.5 * diff * diff / HUBER_BETA, magnitude - 0.5 * HUBER_BETA
    )


def causal_pad(values):
    prior = shifted(values, "tm", 1)
    joined = jnp.concatenate([prior, values], axis=0)
    return padded_2(joined, (("row", 1), ("col", 2)), 1)


def future_pad(values):
    later = shifted(values, "tm", -1)
    joined = jnp.concatenate([values, later], axis=0)
    return padded_2(joined, (("row", 1), ("col", 2)), 1)


def gather_patches(padded, frames, height, tile_width):
    pieces = []
    for depth_at in range(3):
        for row_at in range(3):
            for col_at in range(3):
                pieces.append(
                    padded[
                        depth_at : depth_at + frames,
                        row_at : row_at + height,
                        col_at : col_at + tile_width,
                        :,
                    ]
                )
    joined = jnp.concatenate(pieces, axis=-1)
    return joined.reshape(frames * height * tile_width, -1)


def ssim_terms(picture, target, pix_dev):
    height, tile_width = (picture.shape[2], picture.shape[3])
    stacked = jnp.stack([picture, target])
    rimmed = padded_2(stacked, (("row", 3), ("col", 4)), 5)
    pic_rim, tgt_rim = (rimmed[0], rimmed[1])
    mean_x = blur_valid(pic_rim, height, tile_width)
    mean_y = blur_valid(tgt_rim, height, tile_width)
    var_x = blur_valid(pic_rim * pic_rim, height, tile_width) - mean_x * mean_x
    var_y = blur_valid(tgt_rim * tgt_rim, height, tile_width) - mean_y * mean_y
    covar = blur_valid(pic_rim * tgt_rim, height, tile_width) - mean_x * mean_y
    numer_a = 2.0 * mean_x * mean_y + SSIM_CONST_A
    numer_b = 2.0 * covar + SSIM_CONST_B
    denom_a = mean_x * mean_x + mean_y * mean_y + SSIM_CONST_A
    denom_b = var_x + var_y + SSIM_CONST_B
    denom_all = denom_a * denom_b
    ssim_map = numer_a * numer_b / denom_all
    diff = picture - target
    loss_local = (jnp.sum(huber_loss(diff)) + jnp.sum(1.0 - ssim_map)) / pix_dev
    slope_mean = (2.0 * mean_y * numer_b - 2.0 * mean_y * numer_a) / denom_all - ssim_map * (
        2.0 * mean_x / denom_a - 2.0 * mean_x / denom_b
    )
    slope_square = -ssim_map / denom_b
    slope_cross = 2.0 * numer_a / denom_all
    adjoint = jnp.stack([slope_mean, slope_square, slope_cross]) * (-1.0 / pix_dev)
    spread = padded_2(adjoint, (("row", 3), ("col", 4)), 5)
    pulled = blur_valid(spread, height, tile_width)
    gradient = (
        jnp.clip(diff / HUBER_BETA, -1.0, 1.0) / pix_dev
        + pulled[0]
        + 2.0 * picture * pulled[1]
        + target * pulled[2]
    )
    return (loss_local, gradient)


def body(features, conv_first, conv_second, shortcut_weight, head_weight, target_frames):
    frames, rows_tile, cols_tile, chan_in = features.shape
    chan_mid = conv_second.shape[-1]
    colors = head_weight.shape[1]
    voxels = frames * rows_tile * cols_tile
    pix_dev = 1.0 * colors * voxels
    contract = (((0,), (0,)), ((), ()))
    act_zero = normed_silu(features.astype(jnp.float32)).astype(jnp.bfloat16)
    patch_zero = gather_patches(causal_pad(act_zero), frames, rows_tile, cols_tile)
    pre_first = jnp.dot(
        patch_zero, conv_first.reshape(-1, chan_mid), preferred_element_type=jnp.float32
    )
    act_first = normed_silu(pre_first).astype(jnp.bfloat16)
    padded_first = causal_pad(act_first.reshape(frames, rows_tile, cols_tile, chan_mid))
    patch_first = gather_patches(padded_first, frames, rows_tile, cols_tile)
    pre_second = jnp.dot(
        patch_first, conv_second.reshape(-1, chan_mid), preferred_element_type=jnp.float32
    )
    flat_features = features.reshape(voxels, chan_in)
    shortcut_out = jnp.dot(flat_features, shortcut_weight, preferred_element_type=jnp.float32)
    block_sum = pre_second + shortcut_out
    act_block = normed_silu(block_sum).astype(jnp.bfloat16)
    image_rgb = jnp.dot(act_block, head_weight, preferred_element_type=jnp.float32)
    image_first = image_rgb.reshape(frames, rows_tile, cols_tile, colors).transpose(3, 0, 1, 2)
    loss_local, grad_first_axis = ssim_terms(image_first, target_frames, pix_dev)
    grad_image = grad_first_axis.transpose(1, 2, 3, 0).reshape(voxels, colors)
    grad_head = lax.dot_general(
        act_block.astype(jnp.float32), grad_image, contract, precision=lax.Precision.HIGHEST
    )
    grad_act_block = jnp.dot(
        grad_image, head_weight.astype(jnp.float32).T, precision=lax.Precision.HIGHEST
    )
    grad_block = jax.vjp(normed_silu, block_sum)[1](grad_act_block)[0].astype(jnp.bfloat16)
    grad_shortcut = lax.dot_general(
        flat_features, grad_block, contract, preferred_element_type=jnp.float32
    )
    grad_second = lax.dot_general(
        patch_first, grad_block, contract, preferred_element_type=jnp.float32
    ).reshape(conv_second.shape)
    padded_grad = future_pad(grad_block.reshape(frames, rows_tile, cols_tile, chan_mid))
    patch_grad = gather_patches(padded_grad, frames, rows_tile, cols_tile)
    flipped = conv_second[::-1, ::-1, ::-1].transpose(0, 1, 2, 4, 3).reshape(-1, chan_mid)
    grad_act_first = jnp.dot(patch_grad, flipped, preferred_element_type=jnp.float32)
    grad_pre_first = jax.vjp(normed_silu, pre_first)[1](grad_act_first)[0].astype(jnp.bfloat16)
    grad_first = lax.dot_general(
        patch_zero, grad_pre_first, contract, preferred_element_type=jnp.float32
    ).reshape(conv_first.shape)
    grad_first, grad_second, grad_shortcut, grad_head, loss_total = lax.psum(
        (grad_first, grad_second, grad_shortcut, grad_head, loss_local), ("tm", "row", "col")
    )
    devices_all = lax.axis_size("tm") * lax.axis_size("row") * lax.axis_size("col")
    loss_mean = loss_total / devices_all
    return (grad_first, grad_second, grad_shortcut, grad_head, loss_mean)


def solution(mesh):
    return jax.shard_map(
        body,
        mesh=mesh,
        in_specs=(P("tm", "row", "col", None), P(), P(), P(), P(), P(None, "tm", "row", "col")),
        out_specs=(P(), P(), P(), P(), P()),
        check_vma=False,
    )
```

profile of v0, /device:TPU:1, one launch (start us, length us, event | category | flops | bytes accessed | tf_op | source)
XLA Modules:
  0.0 567.4 jit_solution(3778551931624395523)
XLA Ops:
  9.7 4.4 collective-permute-start
  14.1 7.7 %collective-permute-done = bf16[2,8,32,384]{3,2,1,0:T(8,128)(2,1)S(1)} collective-permute-done((bf16[2,8,32,384]{3,2,1,0:T(8,128)(2,1)S(1)}, bf16[2,8,32,384]{3,2,1,0:T(8,128)(2,1)S(1)}, u32[]{:S(2)}, u32[]{:S(2)}) %collective-permute-start) | collective-permute-done | bytes 393248 | tf_op jit(solution)/shard_map/ppermute | solution.py:15
  21.9 3.2 collective-permute-start.1
  26.4 7.9 %copy.13 = bf16[3,3,3,384,192]{3,2,1,0,4:T(4,128)(2,1)} copy(bf16[3,3,3,384,192]{3,4,2,1,0:T(8,128)(2,1)} %param.7) | data formatting | bytes 7962624 | tf_op args[1]
  34.3 10.0 %reshape.140 = bf16[10368,192]{0,1:T(8,128)(2,1)} reshape(bf16[3,3,3,384,192]{3,2,1,0,4:T(4,128)(2,1)} %copy.13) | data formatting | bytes 7962624 | tf_op jit(solution)/shard_map/reshape | solution.py:138
  44.5 4.8 collective-permute-start.3
  49.3 1.9 collective-permute-start.4
  51.4 3.4 collective-permute-done.4
  59.8 3.6 multiply_reduce_fusion.3
  64.0 4.1 collective-permute-start.5
  68.8 3.5 collective-permute-done.5
  72.4 4.3 collective-permute-start.6
  79.6 2.1 collective-permute-done.7
  81.7 5.7 collective-permute-start.8
  87.4 2.1 collective-permute-start.9
  96.8 1.8 copy.15
  100.2 1.8 copy.17
  101.9 1.8 copy.18
  103.7 1.8 copy.20
  105.4 1.8 copy.21
  107.2 1.7 copy.23
  109.0 1.8 copy.24
  110.7 1.7 copy.26
  146.7 4.6 fusion.184
  152.7 3.2 collective-permute-start.10
  157.9 2.9 collective-permute-done.11
  160.9 5.1 collective-permute-start.12
  166.0 1.9 collective-permute-start.13
  168.6 3.8 collective-permute-done.13
  172.7 7.2 %fusion.85 = f32[3,2,8,42]{3,2,1,0:T(8,128)S(1)} fusion(f32[3,2,18,42]{3,2,1,0:T(8,128)S(1)} %get-tuple-element.92, f32[]{:T(128)} %bitcast.46, f32[]{:T(128)} %bitcast.45, f32[]{:T(128)} %bitcast.44, f32[]{:T(128)} %bitcast.43, f32[]{:T(128)} %bitcast.42, f32[]{:T(128)} %bitcast.41, f32[]{:T(128)} %bitcast.40, f32[]{:T(128)} %bitcast.39, f32[]{:T(128)} %bitcast.38, ...), kind=kLoop, calls=%fused_computation.282 | loop fusion | flops 42336 | bytes 96812 | tf_op jit(solution)/shard_map/add | solution.py:50
  179.8 7.2 %fusion.64 = f32[3,2,8,42]{3,2,1,0:T(8,128)S(1)} fusion(f32[3,2,18,42]{3,2,1,0:T(8,128)S(1)} %get-tuple-element.93, f32[]{:T(128)} %bitcast.46, f32[]{:T(128)} %bitcast.45, f32[]{:T(128)} %bitcast.44, f32[]{:T(128)} %bitcast.43, f32[]{:T(128)} %bitcast.42, f32[]{:T(128)} %bitcast.41, f32[]{:T(128)} %bitcast.40, f32[]{:T(128)} %bitcast.39, f32[]{:T(128)} %bitcast.38, ...), kind=kLoop, calls=%fused_computation.239 | loop fusion | flops 42336 | bytes 96812 | tf_op jit(solution)/shard_map/add | solution.py:50
  187.0 7.2 %fusion.128 = f32[3,2,8,42]{3,2,1,0:T(8,128)S(1)} fusion(f32[3,2,18,42]{3,2,1,0:T(8,128)S(1)} %get-tuple-element.94, f32[]{:T(128)} %bitcast.46, f32[]{:T(128)} %bitcast.45, f32[]{:T(128)} %bitcast.44, f32[]{:T(128)} %bitcast.43, f32[]{:T(128)} %bitcast.42, f32[]{:T(128)} %bitcast.41, f32[]{:T(128)} %bitcast.40, f32[]{:T(128)} %bitcast.39, f32[]{:T(128)} %bitcast.38, ...), kind=kLoop, calls=%fused_computation.369 | loop fusion | flops 42336 | bytes 96812 | tf_op jit(solution)/shard_map/add | solution.py:50
  194.2 7.2 %fusion.105 = f32[3,2,8,42]{3,2,1,0:T(8,128)S(1)} fusion(f32[3,2,18,42]{3,2,1,0:T(8,128)S(1)} %get-tuple-element.91, f32[]{:T(128)} %bitcast.46, f32[]{:T(128)} %bitcast.45, f32[]{:T(128)} %bitcast.44, f32[]{:T(128)} %bitcast.43, f32[]{:T(128)} %bitcast.42, f32[]{:T(128)} %bitcast.41, f32[]{:T(128)} %bitcast.40, f32[]{:T(128)} %bitcast.39, f32[]{:T(128)} %bitcast.38, ...), kind=kLoop, calls=%fused_computation.324 | loop fusion | flops 42336 | bytes 96812 | tf_op jit(solution)/shard_map/add | solution.py:50
  201.3 7.2 %fusion.148 = f32[3,2,8,42]{3,2,1,0:T(8,128)S(1)} fusion(f32[3,2,18,42]{3,2,1,0:T(8,128)S(1)} %get-tuple-element.90, f32[]{:T(128)} %bitcast.46, f32[]{:T(128)} %bitcast.45, f32[]{:T(128)} %bitcast.44, f32[]{:T(128)} %bitcast.43, f32[]{:T(128)} %bitcast.42, f32[]{:T(128)} %bitcast.41, f32[]{:T(128)} %bitcast.40, f32[]{:T(128)} %bitcast.39, f32[]{:T(128)} %bitcast.38, ...), kind=kLoop, calls=%fused_computation.411 | loop fusion | flops 42336 | bytes 96812 | tf_op jit(solution)/shard_map/add | solution.py:50
  208.5 8.2 %subtract_reduce_fusion = (f32[]{:T(128)}, f32[3,2,8,32]{3,2,1,0:T(8,128)S(1)}, f32[3,2,8,32]{3,2,1,0:T(8,128)S(1)}, f32[3,2,8,32]{3,2,1,0:T(8,128)S(1)}, f32[3,...) fusion(f32[3,2,8,42]{3,2,1,0:T(8,128)S(1)} %fusion.128, f32[]{:T(128)} %bitcast.46, f32[]{:T(128)} %bitcast.45, ...), kind=kLoop, calls=%fused_computation.433 | loop fusion | flops 191999 | bytes 368688 | tf_op jit(solution)/shard_map/reduce_sum | solution.py:110
  216.7 2.9 collective-permute-start.14
  221.0 3.7 collective-permute-done.15
  225.6 3.4 collective-permute-start.16
  229.0 1.9 collective-permute-start.17
  231.0 1.9 reverse_bitcast_fusion
  232.9 3.5 copy.68
  236.3 14.5 %copy.12 = bf16[512,10368]{0,1:T(8,128)(2,1)} copy(bf16[512,10368]{1,0:T(8,128)(2,1)} %bitcast.173) | data formatting | bytes 21233664 | tf_op jit(solution)/shard_map/reshape | solution.py:90
  252.1 7.2 %fusion.32 = f32[3,3,2,8,42]{4,3,2,1,0:T(8,128)S(1)} fusion(f32[3,3,2,18,42]{4,3,2,1,0:T(8,128)S(1)} %pad_maximum_fusion.10, f32[]{:T(128)} %bitcast.46, f32[]{:T(128)} %bitcast.45, f32[]{:T(128)} %bitcast.44, f32[]{:T(128)} %bitcast.43, f32[]{:T(128)} %bitcast.42, f32[]{:T(128)} %bitcast.41, f32[]{:T(128)} %bitcast.40, f32[]{:T(128)} %bitcast.39, ...), kind=kLoop, calls=%fused_computation.160 | loop fusion | flops 127008 | bytes 290348 | tf_op jit(solution)/shard_map/add | solution.py:50
  259.3 7.4 %fusion.22 = f32[3,3,2,8,32]{4,3,2,1,0:T(8,128)S(1)} fusion(f32[3,3,2,8,42]{4,3,2,1,0:T(8,128)S(1)} %fusion.32, f32[]{:T(128)} %bitcast.46, f32[]{:T(128)} %bitcast.45, f32[]{:T(128)} %bitcast.44, f32[]{:T(128)} %bitcast.43, f32[]{:T(128)} %bitcast.42, f32[]{:T(128)} %bitcast.41, f32[]{:T(128)} %bitcast.40, f32[]{:T(128)} %bitcast.39, f32[]{:T(128)} %bitcast.38, ...), kind=kLoop, calls=%fused_computation.139 | loop fusion | flops 96768 | bytes 221228 | tf_op jit(solution)/shard_map/add | solution.py:53
  268.2 6.4 %fusion.17 = f32[3,3,3,192,192]{4,3,2,1,0:T(8,128)} fusion(bf16[3,3,3,192,512]{4,3,2,1,0:T(8,128)(2,1)} %bitcast.190, bf16[512,192]{0,1:T(8,128)(2,1)S(1)} %fusion.9), kind=kOutput, calls=%fused_computation.74 | convolution fusion | flops 1019215872 | bytes 9486336 | tf_op jit(solution)/shard_map/dot_general | solution.py:164
  277.0 7.5 %collective-permute-done.18 = bf16[2,8,32,192]{3,2,1,0:T(8,128)(2,1)S(1)} collective-permute-done((bf16[2,8,32,192]{3,2,1,0:T(8,128)(2,1)S(1)}, bf16[2,8,32,192]{3,2,1,0:T(8,128)(2,1)S(1)}, u32[]{:S(2)}, u32[]{:S(2)}) %collective-permute-start.18) | collective-permute-done | bytes 196640 | tf_op jit(solution)/shard_map/ppermute | solution.py:15
  284.5 1.9 collective-permute-start.19
  289.4 2.0 collective-permute-done.20
  291.8 5.7 %collective-permute-start.21 = (bf16[4,10,1,192]{3,2,1,0:T(2,128)(2,1)S(1)}, bf16[4,10,1,192]{3,2,1,0:T(2,128)(2,1)S(1)}, u32[]{:S(2)}, u32[]{:S(2)}) collective-permute-start(bf16[4,10,1,192]{3,2,1,0:T(2,128)(2,1)S(1)} %get-tuple-element.63), channel_id=1, source_target_pairs={{0,1},{1,2},{2,3},{3,4},{4,5},{5,6},{6,7},{8,9},{9,10},{10,11},{11... | collective-permute-start | bytes 46088 | tf_op jit(solution)/shard_map/ppermute | solution.py:26
  297.6 1.9 collective-permute-start.22
  305.9 1.7 copy.42
  311.0 1.8 copy.44
  323.6 1.8 copy.52
  329.4 1.7 copy.61
  331.1 1.8 copy.62
  332.9 1.8 copy.64
  336.6 1.8 constant_dynamic-update-slice_fusion.50
  356.2 1.8 constant_dynamic-update-slice_fusion.38
  367.9 4.1 multiply_reduce_fusion
  372.0 6.9 %fusion.15 = f32[3,3,3,384,192]{3,4,2,1,0:T(8,128)} fusion(bf16[3,3,3,384,512]{4,3,2,1,0:T(8,128)(2,1)S(1)} %bitcast.171, f32[512,192]{0,1:T(8,128)S(1)} %copy-done.9, f32[512]{0:T(512)S(1)} %multiply_multiply_fusion.1, f32[512]{0:T(512)S(1)} %copy-done.26, f32[512,192]{0,1:T(8,128)S(1)} %get-tuple-element.124), kind=kOutput, calls=%fused_computation.73 | convolution fusion | flops 2039906304 | bytes 19369984 | tf_op jit(solution)/shard_map/dot_general | solution.py:172
  380.4 64.2 %all-reduce = (f32[192,3]{0,1:T(4,128)}, f32[]{:T(128)}) all-reduce(f32[192,3]{0,1:T(4,128)S(1)} %fusion.186, f32[]{:T(128)S(6)} %div.132), channel_id=1, replica_groups=mesh['tm'=4,'row'=4,'col'=8] {'tm','row','col'}, use_global_device_ids=true, to_apply=%region_9.10 | all-reduce | flops 577 | bytes 4616 | tf_op jit(solution)/shard_map/psum | solution.py:175
  445.2 103.6 %all-reduce.4.cloned.1.call-done = (f32[3,3,3,384,192]{3,4,2,1,0:T(8,128)}, f32[3,3,3,192,192]{4,3,2,1,0:T(8,128)}, f32[384,192]{0,1:T(8,128)}) async-done(((f32[3,3,3,384,192]{3,4,2,1,0:T(8,128)}, f32[3,3,3,192,192]{4,3,2,1,0:T(8,128)}, f32[384,192]{0,1:T(8,128)}), (f32[3,3,3,384,192]{3,4,2,1,0:T(8,128)}, f32[3,3,3,192,192]{4,3,2,1,0:T(8,128)}, f32[384,192]{0,1:T(8,128)})) %all-reduce.4.cloned.1.call-update) | async-done | bytes 12238864 | tf_op jit(solution)/shard_map/psum | solution.py:175
  548.8 7.5 %copy.152 = f32[3,3,3,384,192]{3,4,2,1,0:T(8,128)} copy(f32[3,3,3,384,192]{3,4,2,1,0:T(8,128)} %get-tuple-element.137) | data formatting | bytes 15925248
  556.4 2.4 copy.153
  (262 shorter events, 126.4 us)
Async XLA Ops:
  7.2 144.1 %copy-start = (bf16[384,192]{0,1:T(8,128)(2,1)S(1)}, bf16[384,192]{0,1:T(8,128)(2,1)}, u32[]{:S(2)}) copy-start(bf16[384,192]{0,1:T(8,128)(2,1)} %param.9) | copy-start | bytes 442372
  7.2 541.7 %all-reduce.4.cloned.1.call-start = ((), (), s32[]{:S(2)}) async-start(), calls=%async_computation | async-start | bytes 27131904 | tf_op jit(solution)/shard_map/psum | solution.py:175
  9.7 12.1 %collective-permute-start = (bf16[2,8,32,384]{3,2,1,0:T(8,128)(2,1)S(1)}, bf16[2,8,32,384]{3,2,1,0:T(8,128)(2,1)S(1)}, u32[]{:S(2)}, u32[]{:S(2)}) collective-permute-start(bf16[2,8,32,384]{3,2,1,0:T(8,128)(2,1)S(1)} %fusion.5), channel_id=1, source_target_pairs={{0,32},{32,64},{64,96},{1,33},{33,65},{65,97},{2,34},{34,66},{66,9... | collective-permute-start | bytes 1179656 | tf_op jit(solution)/shard_map/ppermute | solution.py:15
  21.9 22.5 %collective-permute-start.1 = (bf16[4,1,32,384]{3,2,1,0:T(8,128)(2,1)S(1)}, bf16[4,1,32,384]{3,2,1,0:T(8,128)(2,1)S(1)}, u32[]{:S(2)}, u32[]{:S(2)}) collective-permute-start(bf16[4,1,32,384]{3,2,1,0:T(8,128)(2,1)S(1)} %get-tuple-element.58), channel_id=1, source_target_pairs={{0,8},{8,16},{16,24},{1,9},{9,17},{17,25},{2,10},{10,18},{18,26},{... | collective-permute-start | bytes 294920 | tf_op jit(solution)/shard_map/ppermute | solution.py:26
  25.1 19.3 %collective-permute-start.2 = (bf16[4,1,32,384]{3,2,1,0:T(8,128)(2,1)S(1)}, bf16[4,1,32,384]{3,2,1,0:T(8,128)(2,1)S(1)}, u32[]{:S(2)}, u32[]{:S(2)}) collective-permute-start(bf16[4,1,32,384]{3,2,1,0:T(8,128)(2,1)S(1)} %get-tuple-element.59), channel_id=1, source_target_pairs={{8,0},{16,8},{24,16},{9,1},{17,9},{25,17},{10,2},{18,10},{26,18},{... | collective-permute-start | bytes 294920 | tf_op jit(solution)/shard_map/ppermute | solution.py:28
  44.5 6.9 %collective-permute-start.3 = (bf16[4,10,1,384]{3,2,1,0:T(2,128)(2,1)S(1)}, bf16[4,10,1,384]{3,2,1,0:T(2,128)(2,1)S(1)}, u32[]{:S(2)}, u32[]{:S(2)}) collective-permute-start(bf16[4,10,1,384]{3,2,1,0:T(2,128)(2,1)S(1)} %get-tuple-element.19), channel_id=1, source_target_pairs={{0,1},{1,2},{2,3},{3,4},{4,5},{5,6},{6,7},{8,9},{9,10},{10,11},{11... | collective-permute-start | bytes 92168 | tf_op jit(solution)/shard_map/ppermute | solution.py:26
  49.3 5.5 collective-permute-start.4
  57.2 1.3 copy-start.3
  57.6 2.2 copy-start.5
  59.3 4.1 copy-start.2
  63.4 0.6 copy-start.27
  63.4 79.3 %copy-start.8 = (f32[512,192]{0,1:T(8,128)}, f32[512,192]{0,1:T(8,128)S(1)}, u32[]{:S(2)}) copy-start(f32[512,192]{0,1:T(8,128)S(1)} %get-tuple-element.118) | copy-start | bytes 1179652
  63.4 0.6 copy-start.25
  64.0 8.3 %collective-permute-start.5 = (bf16[2,8,32,192]{3,2,1,0:T(8,128)(2,1)S(1)}, bf16[2,8,32,192]{3,2,1,0:T(8,128)(2,1)S(1)}, u32[]{:S(2)}, u32[]{:S(2)}) collective-permute-start(bf16[2,8,32,192]{3,2,1,0:T(8,128)(2,1)S(1)} %bitcast.182), channel_id=1, source_target_pairs={{0,32},{32,64},{64,96},{1,33},{33,65},{65,97},{2,34},{34,66},{66,9... | collective-permute-start | bytes 589832 | tf_op jit(solution)/shard_map/ppermute | solution.py:15
  72.4 7.2 %collective-permute-start.6 = (bf16[4,1,32,192]{3,2,1,0:T(8,128)(2,1)S(1)}, bf16[4,1,32,192]{3,2,1,0:T(8,128)(2,1)S(1)}, u32[]{:S(2)}, u32[]{:S(2)}) collective-permute-start(bf16[4,1,32,192]{3,2,1,0:T(8,128)(2,1)S(1)} %get-tuple-element.86), channel_id=1, source_target_pairs={{0,8},{8,16},{16,24},{1,9},{9,17},{17,25},{2,10},{10,18},{18,26},{... | collective-permute-start | bytes 147464 | tf_op jit(solution)/shard_map/ppermute | solution.py:26
  76.6 5.0 collective-permute-start.7
  81.7 13.0 %collective-permute-start.8 = (bf16[4,10,1,192]{3,2,1,0:T(2,128)(2,1)S(1)}, bf16[4,10,1,192]{3,2,1,0:T(2,128)(2,1)S(1)}, u32[]{:S(2)}, u32[]{:S(2)}) collective-permute-start(bf16[4,10,1,192]{3,2,1,0:T(2,128)(2,1)S(1)} %get-tuple-element.67), channel_id=1, source_target_pairs={{0,1},{1,2},{2,3},{3,4},{4,5},{5,6},{6,7},{8,9},{9,10},{10,11},{11... | collective-permute-start | bytes 46088 | tf_op jit(solution)/shard_map/ppermute | solution.py:26
  87.4 7.4 %collective-permute-start.9 = (bf16[4,10,1,192]{3,2,1,0:T(2,128)(2,1)S(1)}, bf16[4,10,1,192]{3,2,1,0:T(2,128)(2,1)S(1)}, u32[]{:S(2)}, u32[]{:S(2)}) collective-permute-start(bf16[4,10,1,192]{3,2,1,0:T(2,128)(2,1)S(1)} %get-tuple-element.66), channel_id=1, source_target_pairs={{1,0},{2,1},{3,2},{4,3},{5,4},{6,5},{7,6},{9,8},{10,9},{11,10},{12... | collective-permute-start | bytes 46088 | tf_op jit(solution)/shard_map/ppermute | solution.py:28
  113.3 22.3 %copy-start.13 = (bf16[512,192]{0,1:T(8,128)(2,1)S(1)}, bf16[512,192]{0,1:T(8,128)(2,1)}, u32[]{:S(2)}) copy-start(bf16[512,192]{0,1:T(8,128)(2,1)} %copy.28) | copy-start | bytes 589828
  114.1 26.6 %copy-start.15 = (bf16[512,192]{0,1:T(8,128)(2,1)S(1)}, bf16[512,192]{0,1:T(8,128)(2,1)}, u32[]{:S(2)}) copy-start(bf16[512,192]{0,1:T(8,128)(2,1)} %copy.34) | copy-start | bytes 589828
  114.1 28.6 %copy-start.26 = (f32[512]{0:T(512)S(1)}, f32[512]{0:T(512)}, u32[]{:S(2)}) copy-start(f32[512]{0:T(512)} %copy-done.25) | copy-start | bytes 6148
  114.9 23.7 %copy-start.16 = (bf16[512,192]{0,1:T(8,128)(2,1)S(1)}, bf16[512,192]{0,1:T(8,128)(2,1)}, u32[]{:S(2)}) copy-start(bf16[512,192]{0,1:T(8,128)(2,1)} %copy.31) | copy-start | bytes 589828
  116.0 21.8 %copy-start.22 = (bf16[512,192]{0,1:T(8,128)(2,1)S(1)}, bf16[512,192]{0,1:T(8,128)(2,1)}, u32[]{:S(2)}) copy-start(bf16[512,192]{0,1:T(8,128)(2,1)} %copy.30) | copy-start | bytes 589828
  116.1 23.2 %copy-start.21 = (bf16[512,192]{0,1:T(8,128)(2,1)S(1)}, bf16[512,192]{0,1:T(8,128)(2,1)}, u32[]{:S(2)}) copy-start(bf16[512,192]{0,1:T(8,128)(2,1)} %copy.32) | copy-start | bytes 589828
  117.7 27.5 %copy-start.14 = (bf16[512,192]{0,1:T(8,128)(2,1)S(1)}, bf16[512,192]{0,1:T(8,128)(2,1)}, u32[]{:S(2)}) copy-start(bf16[512,192]{0,1:T(8,128)(2,1)} %copy.39) | copy-start | bytes 589828
  146.7 5.8 %copy-start.29 = (bf16[192,3]{0,1:T(4,128)(2,1)S(1)}, bf16[192,3]{0,1:T(4,128)(2,1)}, u32[]{:S(2)}) copy-start(bf16[192,3]{0,1:T(4,128)(2,1)} %param.10) | copy-start | bytes 3460
  146.7 6.0 %copy-start.23 = (f32[3,2,8,32]{3,2,1,0:T(8,128)S(1)}, f32[3,2,8,32]{3,2,1,0:T(8,128)}, u32[]{:S(2)}) copy-start(f32[3,2,8,32]{3,2,1,0:T(8,128)} %param.11) | copy-start | bytes 18436
  151.6 0.7 copy-start.6
  152.7 5.2 collective-permute-start.10
  155.9 4.8 collective-permute-start.11
  160.9 7.7 %collective-permute-start.12 = (f32[2,3,2,18,5]{4,3,2,1,0:T(8,128)S(1)}, f32[2,3,2,18,5]{4,3,2,1,0:T(8,128)S(1)}, u32[]{:S(2)}, u32[]{:S(2)}) collective-permute-start(f32[2,3,2,18,5]{4,3,2,1,0:T(8,128)S(1)} %get-tuple-element.95), channel_id=1, source_target_pairs={{0,1},{1,2},{2,3},{3,4},{4,5},{5,6},{6,7},{8,9},{9,10},{10,11},{11... | collective-permute-start | bytes 12968 | tf_op jit(solution)/shard_map/ppermute | solution.py:26
  166.0 6.5 %collective-permute-start.13 = (f32[2,3,2,18,5]{4,3,2,1,0:T(8,128)S(1)}, f32[2,3,2,18,5]{4,3,2,1,0:T(8,128)S(1)}, u32[]{:S(2)}, u32[]{:S(2)}) collective-permute-start(f32[2,3,2,18,5]{4,3,2,1,0:T(8,128)S(1)} %get-tuple-element.96), channel_id=1, source_target_pairs={{1,0},{2,1},{3,2},{4,3},{5,4},{6,5},{7,6},{9,8},{10,9},{11,10},{12... | collective-permute-start | bytes 12968 | tf_op jit(solution)/shard_map/ppermute | solution.py:28
  216.7 4.3 collective-permute-start.14
  219.7 5.1 collective-permute-start.15
  225.6 25.2 %collective-permute-start.16 = (f32[3,3,2,18,5]{4,3,2,1,0:T(8,128)}, f32[3,3,2,18,5]{4,3,2,1,0:T(8,128)}, u32[]{:S(2)}, u32[]{:S(2)}) collective-permute-start(f32[3,3,2,18,5]{4,3,2,1,0:T(8,128)} %get-tuple-element.88), channel_id=1, source_target_pairs={{0,1},{1,2},{2,3},{3,4},{4,5},{5,6},{6,7},{8,9},{9,10},{10,11},{11... | collective-permute-start | bytes 19448 | tf_op jit(solution)/shard_map/ppermute | solution.py:26
  229.0 21.8 %collective-permute-start.17 = (f32[3,3,2,18,5]{4,3,2,1,0:T(8,128)}, f32[3,3,2,18,5]{4,3,2,1,0:T(8,128)}, u32[]{:S(2)}, u32[]{:S(2)}) collective-permute-start(f32[3,3,2,18,5]{4,3,2,1,0:T(8,128)} %get-tuple-element.89), channel_id=1, source_target_pairs={{1,0},{2,1},{3,2},{4,3},{5,4},{6,5},{7,6},{9,8},{10,9},{11,10},{12... | collective-permute-start | bytes 19448 | tf_op jit(solution)/shard_map/ppermute | solution.py:28
  236.3 31.1 %copy-start.7 = (f32[512,192]{0,1:T(8,128)S(1)}, f32[512,192]{0,1:T(8,128)}, u32[]{:S(2)}) copy-start(f32[512,192]{0,1:T(8,128)} %copy-done.6) | copy-start | bytes 1179652
  274.5 9.9 %collective-permute-start.18 = (bf16[2,8,32,192]{3,2,1,0:T(8,128)(2,1)S(1)}, bf16[2,8,32,192]{3,2,1,0:T(8,128)(2,1)S(1)}, u32[]{:S(2)}, u32[]{:S(2)}) collective-permute-start(bf16[2,8,32,192]{3,2,1,0:T(8,128)(2,1)S(1)} %bitcast.176), channel_id=1, source_target_pairs={{32,0},{64,32},{96,64},{33,1},{65,33},{97,65},{34,2},{66,34},{98,6... | collective-permute-start | bytes 589832 | tf_op jit(solution)/shard_map/ppermute | solution.py:15
  284.5 4.9 collective-permute-start.19
  286.4 5.0 collective-permute-start.20
  291.8 12.5 %collective-permute-start.21 = (bf16[4,10,1,192]{3,2,1,0:T(2,128)(2,1)S(1)}, bf16[4,10,1,192]{3,2,1,0:T(2,128)(2,1)S(1)}, u32[]{:S(2)}, u32[]{:S(2)}) collective-permute-start(bf16[4,10,1,192]{3,2,1,0:T(2,128)(2,1)S(1)} %get-tuple-element.63), channel_id=1, source_target_pairs={{0,1},{1,2},{2,3},{3,4},{4,5},{5,6},{6,7},{8,9},{9,10},{10,11},{11... | collective-permute-start | bytes 46088 | tf_op jit(solution)/shard_map/ppermute | solution.py:26
  297.6 6.8 %collective-permute-start.22 = (bf16[4,10,1,192]{3,2,1,0:T(2,128)(2,1)S(1)}, bf16[4,10,1,192]{3,2,1,0:T(2,128)(2,1)S(1)}, u32[]{:S(2)}, u32[]{:S(2)}) collective-permute-start(bf16[4,10,1,192]{3,2,1,0:T(2,128)(2,1)S(1)} %get-tuple-element.62), channel_id=1, source_target_pairs={{1,0},{2,1},{3,2},{4,3},{5,4},{6,5},{7,6},{9,8},{10,9},{11,10},{12... | collective-permute-start | bytes 46088 | tf_op jit(solution)/shard_map/ppermute | solution.py:28
  311.0 15.2 %copy-start.12 = (bf16[2,8,32,192]{3,2,1,0:T(8,128)(2,1)S(1)}, bf16[2,8,32,192]{3,2,1,0:T(8,128)(2,1)}, u32[]{:S(2)}) copy-start(bf16[2,8,32,192]{3,2,1,0:T(8,128)(2,1)} %get-tuple-element.24) | copy-start | bytes 589828
  311.0 16.8 %copy-start.11 = (bf16[2,8,32,192]{3,2,1,0:T(8,128)(2,1)S(1)}, bf16[2,8,32,192]{3,2,1,0:T(8,128)(2,1)}, u32[]{:S(2)}) copy-start(bf16[2,8,32,192]{3,2,1,0:T(8,128)(2,1)} %get-tuple-element.23) | copy-start | bytes 589828
  328.5 43.4 %slice-start = ((s8[10616832]{0:T(1024)(128)(4,1)}), s8[2228224]{0:T(1024)(128)(4,1)S(1)}, s32[]{:S(2)}) async-start(s8[10616832]{0:T(1024)(128)(4,1)} %bitcast.169), calls=%async_computation.1 | async-start | bytes 4456448
  331.1 36.8 %copy-start.9 = (f32[512,192]{0,1:T(8,128)S(1)}, f32[512,192]{0,1:T(8,128)}, u32[]{:S(2)}) copy-start(f32[512,192]{0,1:T(8,128)} %copy-done.8) | copy-start | bytes 1179652
  335.5 28.7 %copy-start.17 = (bf16[512,192]{0,1:T(8,128)(2,1)S(1)}, bf16[512,192]{0,1:T(8,128)(2,1)}, u32[]{:S(2)}) copy-start(bf16[512,192]{0,1:T(8,128)(2,1)} %copy.64) | copy-start | bytes 589828
  336.6 24.6 %copy-start.20 = (bf16[512,192]{0,1:T(8,128)(2,1)S(1)}, bf16[512,192]{0,1:T(8,128)(2,1)}, u32[]{:S(2)}) copy-start(bf16[512,192]{0,1:T(8,128)(2,1)} %copy.61) | copy-start | bytes 589828
  336.6 25.3 %copy-start.19 = (bf16[512,192]{0,1:T(8,128)(2,1)S(1)}, bf16[512,192]{0,1:T(8,128)(2,1)}, u32[]{:S(2)}) copy-start(bf16[512,192]{0,1:T(8,128)(2,1)} %copy.62) | copy-start | bytes 589828
  336.6 28.3 %copy-start.18 = (bf16[512,192]{0,1:T(8,128)(2,1)S(1)}, bf16[512,192]{0,1:T(8,128)(2,1)}, u32[]{:S(2)}) copy-start(bf16[512,192]{0,1:T(8,128)(2,1)} %copy.65) | copy-start | bytes 589828
  336.6 31.3 %copy-start.10 = (bf16[3,3,3,192,192]{4,3,2,1,0:T(8,128)(2,1)S(1)}, bf16[3,3,3,192,192]{4,3,2,1,0:T(8,128)(2,1)}, u32[]{:S(2)}) copy-start(bf16[3,3,3,192,192]{4,3,2,1,0:T(8,128)(2,1)} %copy.68) | copy-start | bytes 5971972
  356.2 15.8 %slice-start.1 = ((s8[10616832]{0:T(1024)(128)(4,1)}), s8[4194304]{0:T(1024)(128)(4,1)S(1)}, s32[]{:S(2)}) async-start(s8[10616832]{0:T(1024)(128)(4,1)} %bitcast.169), calls=%async_computation.2 | async-start | bytes 8388608
  367.9 4.1 copy-start.28
  367.9 4.1 slice-start.2
  548.8 7.5 %copy-start.4 = (f32[3,3,3,192,192]{4,3,2,1,0:T(8,128)S(1)}, f32[3,3,3,192,192]{4,3,2,1,0:T(8,128)}, u32[]{:S(2)}) copy-start(f32[3,3,3,192,192]{4,3,2,1,0:T(8,128)} %get-tuple-element.138) | copy-start | bytes 11943940
  548.8 10.6 %copy-start.1 = (bf16[384,192]{0,1:T(8,128)(2,1)S(1)}, bf16[384,192]{0,1:T(8,128)(2,1)}, u32[]{:S(2)}) copy-start(bf16[384,192]{0,1:T(8,128)(2,1)} %param.9) | copy-start | bytes 442372
  556.4 2.4 copy-start.24
Sparse Core Ops, SparseCore 0:
  379.1 169.7 all-reduce.3
where the time goes:
time: 571 us; the launch traced here: 567 us
  local copies, waits for them, and re-layouts  181 us (32%)
  waiting for transfers between devices  140 us (25%)
  other arithmetic  69.4 us (12%)
  starting transfers between devices  66.5 us (12%)
  blocking collectives  64.2 us (11%)
  matrix products  27.7 us (5%)
  between operations  18.1 us (3%)
    psum x1, waiting for transfers between devices, body(): lax.psum((grad_first, grad_second, grad_shortcut, grad_head, loss_local),...  104 us
    unnamed x145, local copies, waits for them, and re-layouts  89.5 us
    psum x1, blocking collectives, body(): lax.psum((grad_first, grad_second, grad_shortcut, grad_head, loss_local),...  64.2 us
    concatenate x55, local copies, waits for them, and re-layouts, gather_patches(): joined = jnp.concatenate(pieces, axis=-1)  55 us
    add x6, other arithmetic, blur_valid(): row_pass + kernel_taps[offset] * padded[..., offset:offset + height, :]  43 us
    ppermute x10, starting transfers between devices, padded_2(): lax.ppermute(tail, axis, [(i, (i + 1) % count) for i in range(ends)])  40.2 us
    ppermute x3, waiting for transfers between devices, shifted(): lax.ppermute(value, axis, [(source, source + steps) for source in range(i...  18.7 us
    ppermute x10, waiting for transfers between devices, padded_2(): lax.ppermute(head, axis, [((i + 1) % count, i) for i in range(ends)])  17.9 us
  transfers between devices with their start and end apart: 24, of which 11 were waited for; matrix products, arithmetic and copies ran while one was open for 10% of the time, Pallas kernels for 0%

commit v1 on v0

v1 whole, which is shorter than its diff:
```python
import functools
import math
import types

import jax
import jax.numpy as jnp
from jax import lax
from jax.experimental import pallas as pl
from jax.experimental.pallas import tpu as pltpu
from jax.sharding import PartitionSpec as P

MESH = pl.DeviceIdType.MESH
F32, BF16 = jnp.float32, jnp.bfloat16
HIGH = lax.Precision.HIGHEST
EPSILON = 1e-06
HUBER_BETA = 0.05
SSIM_CONST_A = 0.0004
SSIM_CONST_B = 0.0036
N_TM, N_ROW, N_COL = 4, 4, 8
FR, TH, TW = 2, 8, 32
VOX = FR * TH * TW
C_IN, C_MID = 384, 192
PIX = 1.0 * 3 * VOX
RAW = [math.exp(-o * o / 4.5) for o in range(6)]
TAPS = [v / (RAW[0] + 2.0 * sum(RAW[1:])) for v in RAW]
NT = (((1,), (1,)), ((), ()))
NN = (((1,), (0,)), ((), ()))
TN = (((0,), (0,)), ((), ()))
HALO = [(0, -1, 0), (0, 1, 0)]
SIDES = [(-1, -1), (0, -1), (1, -1), (-1, 1), (0, 1), (1, 1)]


def band(distance, keep):
    total = jnp.zeros(distance.shape, F32)
    gap = jnp.abs(distance)
    for offset in range(6):
        total = total + jnp.where(gap == offset, TAPS[offset], 0.0)
    return jnp.where(keep, total, 0.0)


def iota(shape, dim):
    return lax.broadcasted_iota(jnp.int32, shape, dim)


def silu_forward(values):
    inverse = lax.rsqrt(jnp.mean(values * values, axis=-1, keepdims=True) + EPSILON)
    unit = values * inverse
    return unit / (1.0 + jnp.exp(-unit))


def silu_backward(values, grad):
    inverse = lax.rsqrt(jnp.mean(values * values, axis=-1, keepdims=True) + EPSILON)
    unit = values * inverse
    gate = 1.0 / (1.0 + jnp.exp(-unit))
    slope = grad * (gate * (1.0 + unit * (1.0 - gate)))
    return inverse * (slope - unit * jnp.mean(slope * unit, axis=-1, keepdims=True))


def wrap(index, step, count):
    return lax.rem(index + (step + count), count)


class Halo:
    def __init__(self, place, ahead, own, other, rims, edges, lines, send, recv):
        self.place, self.ahead = place, ahead
        self.tiles, self.rims, self.edges, self.lines = (own, other), rims, edges, lines
        self.send, self.recv = send, recv

    def copies(self, group):
        t, r, c = self.place
        own, target = self.tiles[0], self.tiles[group]
        there = wrap(t, self.ahead * group, N_TM)
        items = []

        def add(number, src, dst, dr, dc):
            items.append(
                pltpu.make_async_remote_copy(
                    src_ref=src,
                    dst_ref=dst,
                    send_sem=self.send.at[9 * group + number],
                    recv_sem=self.recv.at[9 * group + number],
                    device_id=(there, wrap(r, dr, N_ROW), wrap(c, dc, N_COL)),
                    device_id_type=MESH,
                )
            )

        add(0, own.at[:, 1], target.at[:, 9], -1, 0)
        add(1, own.at[:, 8], target.at[:, 0], 1, 0)
        for number, (dr, dc) in enumerate(SIDES):
            side = 0 if dc == 1 else 1
            add(2 + number, self.edges.at[1 - side], self.rims.at[group, side, 1 - dr], dr, dc)
        if group == 1:
            add(8, own.at[:, pl.ds(1, TH)], target.at[:, pl.ds(1, TH)], 0, 0)
        return items

    def start(self, edges_ref):
        chan = self.edges.shape[-1]
        self.edges[...] = edges_ref[:, :, 0:chan].astype(BF16)
        for group in (0, 1):
            for copy in self.copies(group):
                copy.start()

    def arrived(self, group):
        for copy in self.copies(group):
            copy.wait_recv()

    def sent(self):
        for group in (0, 1):
            for copy in self.copies(group):
                copy.wait_send()

    def shift(self, group, shifted, frame_at):
        t, r, c = self.place
        tile, lines = self.tiles[group], self.lines
        chan = tile.shape[-1]
        for side in (0, 1):
            for frame in range(FR):
                at = slice(frame * TH, frame * TH + TH)
                middle = self.rims[group, side, 1].astype(F32)
                lines[side, frame, 1 : TH + 1] = middle[at]
                lines[side, frame, 0:1] = self.rims[group, side, 0].astype(F32)[frame * TH + TH - 1 : frame * TH + TH]
                lines[side, frame, TH + 1 : TH + 2] = self.rims[group, side, 2].astype(F32)[frame * TH : frame * TH + 1]
        edge_t = jnp.where(self.ahead == 1, t == 0, t == N_TM - 1)
        live = 1.0 if group == 0 else jnp.where(edge_t, 0.0, 1.0)
        top = jnp.where(r == 0, 0.0, 1.0)
        bottom = jnp.where(r == N_ROW - 1, 0.0, 1.0)
        left = jnp.where(c == 0, 0.0, 1.0)
        right = jnp.where(c == N_COL - 1, 0.0, 1.0)
        column = iota((TW, chan), 0)

        def one(step, carry):
            frame, row = step // (TH + 2), lax.rem(step, TH + 2)
            scale = live * jnp.where(row == 0, top, jnp.where(row == TH + 1, bottom, 1.0))
            base = tile[frame, row].astype(F32) * scale
            first = lines[0, frame, pl.ds(row, 1), :] * (scale * left)
            last = lines[1, frame, pl.ds(row, 1), :] * (scale * right)
            shifted[0, frame_at + frame, row] = jnp.where(column == 0, first, pltpu.roll(base, 1, 0)).astype(BF16)
            shifted[1, frame_at + frame, row] = base.astype(BF16)
            shifted[2, frame_at + frame, row] = jnp.where(column == TW - 1, last, pltpu.roll(base, TW - 1, 0)).astype(BF16)
            return carry

        lax.fori_loop(0, FR * (TH + 2), one, 0)


def convolve(shifted, weights, total, full_at, full_tap, half_at, half_out, dims, flip, first):
    half = VOX // FR

    def one(row, carry):
        def tap(time, col):
            if flip:
                return weights[(time * 3 + 2 - row) * 3 + 2 - col]
            return weights[(time * 3 + row) * 3 + col]

        chan = shifted.shape[-1]
        full = None
        part = None
        for col in range(3):
            data = shifted[col, pl.ds(full_at, FR), pl.ds(row, TH)].reshape(VOX, chan)
            term = lax.dot_general(data, tap(full_tap, col), dims, preferred_element_type=F32)
            full = term if full is None else full + term
        total[...] += full
        for col in range(3):
            data = shifted[col, half_at, pl.ds(row, TH)].reshape(half, chan)
            term = lax.dot_general(data, tap(1, col), dims, preferred_element_type=F32)
            part = term if part is None else part + term
        total[pl.ds(half_out * half, half), :] += part
        return carry

    if first:
        total[...] = jnp.zeros(total.shape, F32)
    lax.fori_loop(0, 3, one, 0)


CHUNK = 128


def chunks(body):
    def one(step, carry):
        body(pl.ds(pl.multiple_of(step * CHUNK, CHUNK), CHUNK), step)
        return carry

    lax.fori_loop(0, VOX // CHUNK, one, 0)


def put_tile(tile, edges, step, values):
    rows = CHUNK // TW
    chan = values.shape[-1]
    for at in range(rows):
        edges[0, pl.ds(step * rows + at, 1), 0:chan] = values[at * TW : at * TW + 1]
        edges[1, pl.ds(step * rows + at, 1), 0:chan] = values[at * TW + TW - 1 : at * TW + TW]
    values = values.astype(BF16)
    frame, row = step // (TH // rows), lax.rem(step, TH // rows) * rows
    tile[frame, pl.ds(row + 1, rows)] = values.reshape(rows, TW, values.shape[-1])


def picture_copies(place, tile, field, send, recv):
    t, r, c = place
    items = []
    number = 0
    for dr in range(N_ROW):
        for dc in (-1, 0, 1):
            if dr == 0 and dc == 0:
                continue
            items.append(
                pltpu.make_async_remote_copy(
                    src_ref=tile,
                    dst_ref=field.at[1 - dc, :, pl.ds(pl.multiple_of(r * TH, TH), TH), :],
                    send_sem=send.at[number],
                    recv_sem=recv.at[number],
                    device_id=(t, wrap(r, dr, N_ROW), wrap(c, dc, N_COL)),
                    device_id_type=MESH,
                )
            )
            number += 1
    return items


def canvas(place, tile, field):
    t, r, c = place
    field[1, :, pl.ds(pl.multiple_of(r * TH, TH), TH), :] = tile[...]
    flat = [field[side].reshape(6 * N_ROW * TH, 128) for side in range(3)]
    left = flat[0] * jnp.where(c == 0, 0.0, 1.0)
    right = flat[2] * jnp.where(c == N_COL - 1, 0.0, 1.0)
    return left + pltpu.roll(flat[1], TW, 1) + pltpu.roll(right, 2 * TW, 1)


def high_dot(a, b):
    return jnp.dot(a, b, precision=HIGH, preferred_element_type=F32)


def picture_loss(place, x_tile, y_tile, x_field, y_field, spread):
    t, r, c = place
    rows = 6 * N_ROW * TH
    x, y = canvas(place, x_tile, x_field), canvas(place, y_tile, y_field)
    across = band(iota((128, 128), 0) - iota((128, 128), 1), True)
    row_a, row_b = iota((rows, rows), 0), iota((rows, rows), 1)
    down = band(row_a - row_b, (row_a >> 5) == (row_b >> 5))
    own_a, own_b = iota((48, rows), 0), iota((48, rows), 1)
    down_own = band((own_a & 7) + r * TH - (own_b & 31), (own_a >> 3) == (own_b >> 5))
    wide = high_dot(jnp.concatenate([x, y, x * x, y * y, x * y], axis=0), across)
    mean_x, mean_y, square_x, square_y, cross = [
        high_dot(down, wide[m * rows : (m + 1) * rows]) for m in range(5)
    ]
    var_x = square_x - mean_x * mean_x
    var_y = square_y - mean_y * mean_y
    covar = cross - mean_x * mean_y
    numer_a = 2.0 * mean_x * mean_y + SSIM_CONST_A
    numer_b = 2.0 * covar + SSIM_CONST_B
    denom_a = mean_x * mean_x + mean_y * mean_y + SSIM_CONST_A
    denom_b = var_x + var_y + SSIM_CONST_B
    denom_all = denom_a * denom_b
    ssim = numer_a * numer_b / denom_all
    slope_mean = (2.0 * mean_y * numer_b - 2.0 * mean_y * numer_a) / denom_all - ssim * (
        2.0 * mean_x / denom_a - 2.0 * mean_x / denom_b
    )
    slope_square = -ssim / denom_b
    slope_cross = 2.0 * numer_a / denom_all
    lane, line = iota((rows, 128), 1), iota((rows, 128), 0) & 31
    low = jnp.where(c == 0, TW, TW - 5)
    high = jnp.where(c == N_COL - 1, 2 * TW, 2 * TW + 5)
    inside = (lane >= low) & (lane < high)
    mine = (lane >= TW) & (lane < 2 * TW) & (line >= r * TH) & (line < r * TH + TH)
    loss = jnp.sum(jnp.where(mine, 1.0 - ssim, 0.0), axis=0, keepdims=True)
    adjoint = jnp.concatenate(
        [jnp.where(inside, slope * (-1.0 / PIX), 0.0) for slope in (slope_mean, slope_square, slope_cross)], axis=0
    )
    wide = high_dot(adjoint, across)
    pulled = [high_dot(down_own, wide[m * rows : (m + 1) * rows]) for m in range(3)]
    x_own = pltpu.roll(x_tile[...].reshape(48, 128), TW, 1)
    y_own = pltpu.roll(y_tile[...].reshape(48, 128), TW, 1)
    lane = iota((48, 128), 1)
    mine = (lane >= TW) & (lane < 2 * TW)
    diff = x_own - y_own
    size = jnp.abs(diff)
    huber = jnp.where(size < HUBER_BETA, 0.5 * diff * diff / HUBER_BETA, size - 0.5 * HUBER_BETA)
    loss = (loss + jnp.sum(jnp.where(mine, huber, 0.0), axis=0, keepdims=True)) / PIX
    grad = jnp.clip(diff / HUBER_BETA, -1.0, 1.0) / PIX + pulled[0] + 2.0 * x_own * pulled[1] + y_own * pulled[2]
    grad = pltpu.roll(jnp.where(mine, grad, 0.0), 128 - TW, 1)
    spread[...] = jnp.zeros(spread.shape, F32)
    for color in range(3):
        for frame in range(FR):
            at = (color * FR + frame) * TH
            spread[pl.ds(frame * 64 + color, TH, stride=8), :] = grad[at : at + TH]
    return loss


def kernel(feat, w1, w2, ws, head, targ, g1, g2, gh, loss_out, *scratch):
    s = types.SimpleNamespace(**dict(zip(SCRATCH_NAMES, scratch)))
    t, r, c = lax.axis_index("tm"), lax.axis_index("row"), lax.axis_index("col")
    place = (t, r, c)

    barrier = pltpu.get_barrier_semaphore()
    around = [
        (dt, dr, dc)
        for dt in (-1, 0, 1)
        for dr in (-1, 0, 1, 2)
        for dc in (-1, 0, 1)
        if (dt, dr, dc) != (0, 0, 0) and (dt == 0 or dr < 2)
    ]
    for dt, dr, dc in around:
        pl.semaphore_signal(
            barrier,
            inc=1,
            device_id=(wrap(t, dt, N_TM), wrap(r, dr, N_ROW), wrap(c, dc, N_COL)),
            device_id_type=MESH,
        )

    def act(rows, step):
        values = silu_forward(feat[rows, :].astype(F32))
        put_tile(s.own0, s.columns, step, values)

    chunks(act)
    s.target[...] = jnp.zeros(s.target.shape, F32)
    s.target[:, :, 0:TW] = targ[...]
    pl.semaphore_wait(barrier, len(around))

    halo0 = Halo(place, 1, s.own0, s.other0, s.rims0, s.edges0, s.lines0, s.send0, s.recv0)
    halo1 = Halo(place, 1, s.own1, s.other1, s.rims1, s.edges1, s.lines1, s.send1, s.recv1)
    halo2 = Halo(place, -1, s.own2, s.other2, s.rims2, s.edges2, s.lines1, s.send2, s.recv2)
    halo0.start(s.columns)
    y_copies = picture_copies(place, s.target, s.y_field, s.send_y, s.recv_y)
    for copy in y_copies:
        copy.start()

    halo0.arrived(0)
    halo0.shift(0, s.shift0, FR)
    convolve(s.shift0, w1, s.pre, FR, 2, FR, 1, NT, False, True)
    halo0.arrived(1)
    halo0.shift(1, s.shift0, 0)
    convolve(s.shift0, w1, s.pre, 0, 0, 1, 0, NT, False, False)

    def act_first(rows, step):
        values = silu_forward(s.pre[rows, :])
        put_tile(s.own1, s.columns, step, values)

    chunks(act_first)
    halo1.start(s.columns)
    halo1.arrived(0)
    halo1.shift(0, s.shift1, FR)
    convolve(s.shift1, w2, s.block, FR, 2, FR, 1, NN, False, True)

    def shortcut(rows, step):
        s.block[rows, :] += lax.dot_general(feat[rows, :], ws[...], NT, preferred_element_type=F32)

    chunks(shortcut)
    halo1.arrived(1)
    halo1.shift(1, s.shift1, 0)
    convolve(s.shift1, w2, s.block, 0, 0, 1, 0, NN, False, False)

    s.headf[...] = jnp.zeros(s.headf.shape, F32)
    s.headf[0:3, :] = head[...].astype(F32)

    def act_block(rows, step):
        s.values1[rows, :] = silu_forward(s.block[rows, :]).astype(BF16).astype(F32)

    chunks(act_block)
    lane = iota((8, 128), 1)
    for part in range(4):
        rows = slice(part * 128, part * 128 + 128)
        color = lax.dot_general(
            s.headf[...].astype(BF16), s.values1[rows, :].astype(BF16), NT, preferred_element_type=F32
        )
        for piece in range(4):
            moved = color if piece == 0 else pltpu.roll(color, 128 - TW * piece, 1)
            at = (4 * part + piece) * 8
            s.spread[at : at + 8, :] = jnp.where(lane < TW, moved, 0.0)
    for color in range(3):
        for frame in range(FR):
            s.image[color * FR + frame] = s.spread[pl.ds(frame * 64 + color, TH, stride=8), :]

    x_copies = picture_copies(place, s.image, s.x_field, s.send_x, s.recv_x)
    for copy in x_copies:
        copy.start()
    for copy in y_copies:
        copy.wait_recv()
    for copy in x_copies:
        copy.wait_recv()
    loss = picture_loss(place, s.image, s.target, s.x_field, s.y_field, s.spread)
    loss_out[...] = jnp.broadcast_to(loss, loss_out.shape)

    grad_head = None
    for part in range(4):
        rows = slice(part * 128, part * 128 + 128)
        color = None
        for piece in range(4):
            at = (4 * part + piece) * 8
            held = s.spread[at : at + 8, :]
            color = held if piece == 0 else color + pltpu.roll(held, TW * piece, 1)
        s.colors[part] = color
        term = high_dot(color, s.values1[rows, :])
        grad_head = term if grad_head is None else grad_head + term
    gh[...] = grad_head

    def back_block(rows, step):
        grad = lax.dot_general(s.colors[step], s.headf[...], TN, precision=HIGH, preferred_element_type=F32)
        values = silu_backward(s.block[rows, :], grad)
        s.values1[rows, :] = values
        put_tile(s.own2, s.columns, step, values)

    chunks(back_block)
    halo2.start(s.columns)
    block_t = s.values1[...].T.astype(BF16)
    s.block_t[...] = block_t
    halo2.arrived(0)
    halo2.shift(0, s.shift2, 0)
    convolve(s.shift2, w2, s.back, 0, 2, 1, 0, NT, True, True)

    def second(step, carry):
        time, row = step // 3, lax.rem(step, 3)
        for col in range(3):
            data = s.shift1[col, pl.ds(time, FR), pl.ds(row, TH)].reshape(VOX, C_MID)
            result = lax.dot_general(s.block_t[...], data, NN, preferred_element_type=F32)
            g2[step * 3 + col] = result.T
        return carry

    lax.fori_loop(0, 9, second, 0)
    g1[27] = lax.dot_general(s.block_t[...], feat[...], NN, preferred_element_type=F32)
    halo2.arrived(1)
    halo2.shift(1, s.shift2, FR)
    convolve(s.shift2, w2, s.back, FR, 0, FR, 1, NT, True, False)

    def back_first(rows, step):
        s.values1[rows, :] = silu_backward(s.pre[rows, :], s.back[rows, :])

    chunks(back_first)
    s.block_t[...] = s.values1[...].T.astype(BF16)

    def first(step, carry):
        time, row = step // 3, lax.rem(step, 3)
        for col in range(3):
            data = s.shift0[col, pl.ds(time, FR), pl.ds(row, TH)].reshape(VOX, C_IN)
            g1[step * 3 + col] = lax.dot_general(s.block_t[...], data, NN, preferred_element_type=F32)
        return carry

    lax.fori_loop(0, 9, first, 0)
    for halo in (halo0, halo1, halo2):
        halo.sent()
    for copy in x_copies + y_copies:
        copy.wait_send()


def halo_scratch(number, chan):
    return [
        (f"own{number}", pltpu.VMEM((FR, TH + 2, TW, chan), BF16)),
        (f"other{number}", pltpu.VMEM((FR, TH + 2, TW, chan), BF16)),
        (f"rims{number}", pltpu.VMEM((2, 2, 3, FR * TH, chan), BF16)),
        (f"edges{number}", pltpu.VMEM((2, FR * TH, chan), BF16)),
        (f"shift{number}", pltpu.VMEM((3, 2 * FR, TH + 2, TW, chan), BF16)),
        (f"send{number}", pltpu.SemaphoreType.DMA((18,))),
        (f"recv{number}", pltpu.SemaphoreType.DMA((18,))),
    ]


SCRATCH = (
    halo_scratch(0, C_IN)
    + halo_scratch(1, C_MID)
    + halo_scratch(2, C_MID)
    + [
        ("lines0", pltpu.VMEM((2, FR, 16, C_IN), F32)),
        ("lines1", pltpu.VMEM((2, FR, 16, C_MID), F32)),
        ("columns", pltpu.VMEM((2, FR * TH, C_IN), F32)),
        ("values1", pltpu.VMEM((VOX, C_MID), F32)),
        ("pre", pltpu.VMEM((VOX, C_MID), F32)),
        ("block", pltpu.VMEM((VOX, C_MID), F32)),
        ("back", pltpu.VMEM((VOX, C_MID), F32)),
        ("block_t", pltpu.VMEM((C_MID, VOX), BF16)),
        ("headf", pltpu.VMEM((8, C_MID), F32)),
        ("spread", pltpu.VMEM((128, 128), F32)),
        ("colors", pltpu.VMEM((4, 8, 128), F32)),
        ("image", pltpu.VMEM((6, TH, 128), F32)),
        ("target", pltpu.VMEM((6, TH, 128), F32)),
        ("x_field", pltpu.VMEM((3, 6, N_ROW * TH, 128), F32)),
        ("y_field", pltpu.VMEM((3, 6, N_ROW * TH, 128), F32)),
        ("send_x", pltpu.SemaphoreType.DMA((11,))),
        ("recv_x", pltpu.SemaphoreType.DMA((11,))),
        ("send_y", pltpu.SemaphoreType.DMA((11,))),
        ("recv_y", pltpu.SemaphoreType.DMA((11,))),
    ]
)
SCRATCH_NAMES = [name for name, _ in SCRATCH]


def body(features, conv_first, conv_second, shortcut_weight, head_weight, target_frames):
    vmem = pl.BlockSpec(memory_space=pltpu.VMEM)
    g1, g2, gh, loss = pl.pallas_call(
        kernel,
        out_shape=[
            jax.ShapeDtypeStruct((28, C_MID, C_IN), F32),
            jax.ShapeDtypeStruct((27, C_MID, C_MID), F32),
            jax.ShapeDtypeStruct((8, C_MID), F32),
            jax.ShapeDtypeStruct((8, 128), F32),
        ],
        in_specs=[vmem] * 6,
        out_specs=[vmem] * 4,
        scratch_shapes=[shape for _, shape in SCRATCH],
        compiler_params=pltpu.CompilerParams(
            collective_id=0, has_side_effects=True, vmem_limit_bytes=60 * 1024 * 1024
        ),
    )(
        features.reshape(VOX, C_IN),
        conv_first.transpose(0, 1, 2, 4, 3).reshape(27, C_MID, C_IN),
        conv_second.reshape(27, C_MID, C_MID),
        shortcut_weight.T,
        head_weight.T,
        target_frames.reshape(6, TH, TW),
    )
    g1, g2, gh, loss = lax.psum((g1, g2, gh[:3], jnp.sum(loss[0])), ("tm", "row", "col"))
    return (
        g1[:27].reshape(3, 3, 3, C_MID, C_IN).transpose(0, 1, 2, 4, 3),
        g2.reshape(3, 3, 3, C_MID, C_MID),
        g1[27].T,
        gh.T,
        loss / (N_TM * N_ROW * N_COL),
    )


def solution(mesh):
    return jax.shard_map(
        body,
        mesh=mesh,
        in_specs=(P("tm", "row", "col", None), P(), P(), P(), P(), P(None, "tm", "row", "col")),
        out_specs=(P(), P(), P(), P(), P()),
        check_vma=False,
    )
```

time: 571 us -> 273 us (0.48)
  local copies, waits for them, and re-layouts: 181 us -> 11.7 us
  Pallas kernels: 0 us -> 76.1 us
  other arithmetic: 69.4 us -> 1.28 us
  starting transfers between devices: 66.5 us -> 0.04 us
  waiting for transfers between devices: 140 us -> 104 us
  matrix products: 27.7 us -> 0 us
    unnamed x145 -> x7, local copies, waits for them, and re-layouts: 89.5 us -> 2.39 us
    pallas_call x0 -> x1, Pallas kernels: none -> 76.1 us  [body(): pl.pallas_call(kernel, out_shape=[jax.ShapeDtypeStruct((28, C_MID, C_IN),...]
    ppermute x23 -> x0, starting transfers between devices: 66.4 us -> none  [the longest x10 40.2 us: padded_2(): lax.ppermute(tail, axis, [(i, (i + 1) % count) for i in range(ends)])]
    concatenate x55 -> x0, local copies, waits for them, and re-layouts: 55 us -> none  [gather_patches(): joined = jnp.concatenate(pieces, axis=-1)]
    add x7 -> x0, other arithmetic: 50.4 us -> none  [the longest x6 43 us: blur_valid(): row_pass + kernel_taps[offset] * padded[..., offset:offset + height, :]]
    ppermute x23 -> x0, waiting for transfers between devices: 36.8 us -> none  [the longest x3 18.7 us: shifted(): lax.ppermute(value, axis, [(source, source + steps) for source in range(i...]
    dot_general x10 -> x0, matrix products: 27.7 us -> none  [the longest x1 6.88 us: body(): lax.dot_general(patch_zero, grad_pre_first, contract, preferred_element_t...]
    reshape x4 -> x0, local copies, waits for them, and re-layouts: 24.7 us -> none  [the longest x1 14.5 us: gather_patches(): return joined.reshape(frames * height * tile_width, -1)]
  transfers between devices with their start and end apart: 24 -> 1, of which waited for: 11 -> 1; matrix products, arithmetic and copies ran while one was open for 10% -> 0% of each run, Pallas kernels for 0% -> 0%
where the time goes in v1:
time: 273 us
  waiting for transfers between devices  104 us (38%)
  Pallas kernels  76.1 us (28%)
  blocking collectives  64.5 us (24%)
  between operations  15.8 us (6%)
  local copies, waits for them, and re-layouts  11.7 us (4%)
    psum x1, waiting for transfers between devices, body(): lax.psum((g1, g2, gh[:3], jnp.sum(loss[0])), ('tm', 'row', 'col'))  104 us
    pallas_call x1, Pallas kernels, body(): pl.pallas_call(kernel, out_shape=[jax.ShapeDtypeStruct((28, C_MID, C_IN),...  76.1 us
    psum x1, blocking collectives, body(): lax.psum((g1, g2, gh[:3], jnp.sum(loss[0])), ('tm', 'row', 'col'))  64.5 us
    slice x1, local copies, waits for them, and re-layouts, body(): g1[:27].reshape(3, 3, 3, C_MID, C_IN).transpose(0, 1, 2, 4, 3)  7.46 us
  transfers between devices with their start and end apart: 1, of which 1 were waited for; matrix products, arithmetic and copies ran while one was open for 0% of the time, Pallas kernels for 0%

profile of v1, /device:TPU:1, one launch (start us, length us, event | category | flops | bytes accessed | tf_op | source)
XLA Modules:
  0.0 273.0 jit_solution(1209886796480172263)
XLA Ops:
  7.2 0.0 all-reduce.4.cloned.1.call-start
  7.2 76.1 %shard_map.101 = (f32[28,192,384]{2,1,0:T(8,128)}, f32[27,192,192]{2,1,0:T(8,128)}, f32[8,192]{1,0:T(8,128)}, f32[8,128]{1,0:T(8,128)}) custom-call(bf16[512,384]{1,0:T(8,128)(2,1)} %bitcast.24, bf16[27,192,384]{2,1,0:T(8,128)(2,1)} %bitcast.22, bf16[27,192,192]{2,1,0:T(8,128)(2,1)} %bitcast.23, bf16[192,384]{1,0:T(8,128)(2,1)} %bitcast.25, ...), custom_call_target="tpu_custom_call" | custom-call | tf_op jit(solution)/shard_map/pallas_call | solution.py:485
  83.3 0.0 copy-start
  83.3 0.0 all-reduce.4.cloned.1.call-update
  83.3 1.3 slice_reduce_fusion
  84.6 0.0 copy-done
  84.6 64.5 %all-reduce = (f32[192,3]{0,1:T(4,128)}, f32[]{:T(128)}) all-reduce(f32[192,3]{0,1:T(4,128)S(1)} %slice_bitcast_fusion.1, f32[]{:T(128)} %slice_reduce_fusion), channel_id=1, replica_groups=mesh['tm'=4,'row'=4,'col'=8] {'tm','row','col'}, use_global_device_ids=true, to_apply=%region_2.0 | all-reduce | flops 577 | bytes 4616 | tf_op jit(solution)/shard_map/psum | solution.py:507
  149.7 103.6 %all-reduce.4.cloned.1.call-done = (f32[28,192,384]{2,1,0:T(8,128)}, f32[3,3,3,192,192]{4,3,2,1,0:T(8,128)}) async-done(((f32[28,192,384]{2,1,0:T(8,128)}, f32[3,3,3,192,192]{4,3,2,1,0:T(8,128)}), (f32[28,192,384]{2,1,0:T(8,128)}, f32[3,3,3,192,192]{4,3,2,1,0:T(8,128)})) %all-reduce.4.cloned.1.call-update) | async-done | bytes 12238864 | tf_op jit(solution)/shard_map/psum | solution.py:507
  253.3 0.0 slice-start
  253.3 1.8 slice_bitcast_fusion
  255.2 0.0 slice-start.1
  255.2 7.5 %slice.16 = f32[27,192,384]{2,1,0:T(8,128)} slice(f32[28,192,384]{2,1,0:T(8,128)} %get-tuple-element.15), slice={[0:27], [0:192], [0:384]} | slice | bytes 15925248 | tf_op jit(solution)/shard_map/slice | solution.py:509
  262.6 0.0 slice-done
  262.6 0.0 slice-done.1
  262.6 2.4 copy.14
  (2 shorter events, 0.0 us)
Async XLA Ops:
  7.2 246.2 %all-reduce.4.cloned.1.call-start = ((), (), s32[]{:S(2)}) async-start(), calls=%async_computation | async-start | bytes 27131904 | tf_op jit(solution)/shard_map/psum | solution.py:507
  83.3 1.3 copy-start
  253.3 9.3 %slice-start = ((s8[5308416]{0:T(1024)(128)(4,1)}), s8[4194304]{0:T(1024)(128)(4,1)S(1)}, s32[]{:S(2)}) async-start(s8[5308416]{0:T(1024)(128)(4,1)} %bitcast.20), calls=%async_computation.1 | async-start | bytes 8388608
  255.2 7.5 %slice-start.1 = ((s8[5308416]{0:T(1024)(128)(4,1)}), s8[1114112]{0:T(1024)(128)(4,1)S(1)}, s32[]{:S(2)}) async-start(s8[5308416]{0:T(1024)(128)(4,1)} %bitcast.20), calls=%async_computation.2 | async-start | bytes 2228224
Sparse Core Ops, SparseCore 0:
  83.4 169.8 all-reduce.3

commit v2 on v1

--- a/solution.py
+++ b/solution.py
@@ -26,7 +26,12 @@
 NT = (((1,), (1,)), ((), ()))
 NN = (((1,), (0,)), ((), ()))
 TN = (((0,), (0,)), ((), ()))
-HALO = [(0, -1, 0), (0, 1, 0)]
+PARTS, SPAN = 3, 4096
+SIZES = (1024, 256, 64)
+AXES = ("yzx", "zxy", "xyz")
+SLOTS = 14
+LINES = PARTS * SPAN
+SECOND_AT = SLOTS * 3 * C_MID
 SIDES = [(-1, -1), (0, -1), (1, -1), (-1, 1), (0, 1), (1, 1)]
 
 
@@ -284,7 +289,203 @@
     return loss
 
 
-def kernel(feat, w1, w2, ws, head, targ, g1, g2, gh, loss_out, *scratch):
+def axis_line(place, axis):
+    t, r, c = place
+    if axis == "z":
+        return t, lambda step: (wrap(t, step, N_TM), r, c)
+    if axis == "y":
+        return r, lambda step: (t, wrap(r, step, N_ROW), c)
+    return c >> 1, lambda step: (t, r, wrap(c, 2 * step, N_COL))
+
+
+class Reduce:
+    def __init__(self, s, place, part, result):
+        self.s, self.part, self.result = s, part, result
+        self.core = place[2] & 1
+        self.mate = (place[0], place[1], place[2] + 1 - 2 * self.core)
+        lines = [axis_line(place, axis) for axis in AXES[part]]
+        self.at = [line[0] for line in lines]
+        self.there = [line[1] for line in lines]
+
+    def held(self, phase, chunk, half):
+        size = SIZES[phase]
+        index = lax.rem(self.at[phase] + (chunk + 4), 4)
+        base = self.part * SPAN if phase == 0 else 0
+        at = pl.multiple_of(base + index * size + half * (size // 2), 32)
+        ref = (self.s.flat, self.s.sum1.at[self.part], self.s.sum2.at[self.part])[phase]
+        return ref.at[pl.ds(at, size // 2), :]
+
+    def inbox(self, phase):
+        return (self.s.inbox0, self.s.inbox1, self.s.inbox2)[phase].at[self.part]
+
+    def stage(self, phase):
+        return (self.s.stage0, self.s.stage1, self.s.stage2)[phase].at[self.part]
+
+    def scatter_copy(self, phase, number):
+        if phase == 0 or number >= 4:
+            src = self.stage(phase).at[number if phase == 0 else number - 4]
+        else:
+            src = self.held(phase, *((2, 0), (2, 1), (1, 1), (-1, 0))[number])
+        sem = (self.part * 3 + phase) * 6 + number
+        return pltpu.make_async_remote_copy(
+            src_ref=src,
+            dst_ref=self.inbox(phase).at[number],
+            send_sem=self.s.scatter_send.at[sem],
+            recv_sem=self.s.scatter_recv.at[sem],
+            device_id=self.there[phase](1 if number % 2 == 0 else -1),
+            device_id_type=MESH,
+        )
+
+    def scatter_start(self, phase):
+        for number, (chunk, half) in enumerate(((2, 0), (2, 1), (1, 1), (-1, 0))):
+            if phase == 0:
+                self.stage(0)[number] = self.held(0, chunk, half)[...].astype(BF16)
+            self.scatter_copy(phase, number).start()
+
+    def scatter_middle(self, phase):
+        for number, (chunk, half) in ((4, (1, 0)), (5, (-1, 1))):
+            self.scatter_copy(phase, number - 4).wait_recv()
+            stage = self.stage(phase).at[number if phase == 0 else number - 4]
+            total = self.held(phase, chunk, half)[...] + self.inbox(phase)[number - 4].astype(F32)
+            stage[...] = total.astype(stage.dtype)
+            self.scatter_copy(phase, number).start()
+
+    def scatter_finish(self, phase):
+        for number in (2, 3, 4, 5):
+            self.scatter_copy(phase, number).wait_recv()
+        half_size = SIZES[phase] // 2
+        for half, (first, second) in ((0, (4, 3)), (1, (2, 5))):
+            total = self.held(phase, 0, half)[...] + (
+                self.inbox(phase)[first].astype(F32) + self.inbox(phase)[second].astype(F32)
+            )
+            if phase == 0:
+                self.s.sum1[self.part, half * half_size : (half + 1) * half_size, :] = total
+            elif phase == 1:
+                self.s.sum2[self.part, half * half_size : (half + 1) * half_size, :] = total
+            else:
+                self.region(2, 0, half, self.core)[...] = total.astype(BF16)
+
+    def region(self, phase, chunk, half, core):
+        size = SIZES[phase]
+        base = self.part * SPAN
+        for outer in range(phase):
+            base = base + self.at[outer] * SIZES[outer]
+        base = base + lax.rem(self.at[phase] + (chunk + 4), 4) * size
+        if half is None:
+            return self.result.at[core, pl.ds(pl.multiple_of(base, 32), size), :]
+        return self.result.at[core, pl.ds(pl.multiple_of(base + half * (size // 2), 32), size // 2), :]
+
+    def gather_copy(self, phase, number, arriving):
+        chunk, half = ((0, 0), (0, 1), (0, 1), (0, 0), (-1, 0), (1, 1))[number]
+        way = 1 if number % 2 == 0 else -1
+        block = self.region(phase, chunk - way if arriving else chunk, half, self.core)
+        sem = (self.part * 3 + phase) * 6 + number
+        return pltpu.make_async_remote_copy(
+            src_ref=block,
+            dst_ref=block,
+            send_sem=self.s.gather_send.at[sem],
+            recv_sem=self.s.gather_recv.at[sem],
+            device_id=self.there[phase](way),
+            device_id_type=MESH,
+        )
+
+    def gather_start(self, phase):
+        for number in range(4):
+            self.gather_copy(phase, number, False).start()
+        if phase == 0:
+            self.share(0).start()
+
+    def gather_middle(self, phase):
+        for number in (4, 5):
+            self.gather_copy(phase, number - 4, True).wait_recv()
+            self.gather_copy(phase, number, False).start()
+
+    def gather_finish(self, phase):
+        for number in (2, 3):
+            self.gather_copy(phase, number, True).wait_recv()
+        if phase == 0:
+            self.share(1).start()
+            self.share(-1).start()
+        for number in (4, 5):
+            self.gather_copy(phase, number, True).wait_recv()
+        if phase == 0:
+            self.share(2).start()
+
+    def share(self, chunk, arriving=False):
+        block = self.region(0, chunk, None, 1 - self.core if arriving else self.core)
+        sem = self.part * 4 + chunk % 4
+        return pltpu.make_async_remote_copy(
+            src_ref=block,
+            dst_ref=block,
+            send_sem=self.s.share_send.at[sem],
+            recv_sem=self.s.share_recv.at[sem],
+            device_id=self.mate,
+            device_id_type=MESH,
+        )
+
+    def settle(self):
+        for chunk in range(4):
+            self.share(chunk, True).wait_recv()
+        for phase in range(3):
+            for number in range(6):
+                self.scatter_copy(phase, number).wait_send()
+                self.gather_copy(phase, number, False).wait_send()
+        for chunk in range(4):
+            self.share(chunk).wait_send()
+
+
+class Small:
+    def __init__(self, s, place):
+        self.s = s
+        core = place[2] & 1
+        self.lines = [axis_line(place, axis) for axis in "zyx"]
+        self.lines.append((core, lambda step: (place[0], place[1], place[2] + 1 - 2 * core)))
+
+    def copies(self, stage):
+        at, there = self.lines[stage]
+        mine = self.s.small.at[stage, at]
+        return [
+            pltpu.make_async_remote_copy(
+                src_ref=mine,
+                dst_ref=mine,
+                send_sem=self.s.small_send.at[stage * 3 + step - 1],
+                recv_sem=self.s.small_recv.at[stage * 3 + step - 1],
+                device_id=there(step),
+                device_id_type=MESH,
+            )
+            for step in ((1, 2, 3) if stage < 3 else (1,))
+        ]
+
+    def start(self, stage, value):
+        self.s.small[stage, self.lines[stage][0]] = value
+        for copy in self.copies(stage):
+            copy.start()
+
+    def finish(self, stage):
+        at, there = self.lines[stage]
+        count = 4 if stage < 3 else 2
+        for step in range(1, count):
+            block = self.s.small.at[stage, lax.rem(at + (count - step), count)]
+            pltpu.make_async_remote_copy(
+                src_ref=block,
+                dst_ref=block,
+                send_sem=self.s.small_send.at[stage * 3 + step - 1],
+                recv_sem=self.s.small_recv.at[stage * 3 + step - 1],
+                device_id=there(step),
+                device_id_type=MESH,
+            ).wait_recv()
+        value = self.s.small[stage, 0]
+        for index in range(1, count):
+            value = value + self.s.small[stage, index]
+        return value
+
+    def settle(self):
+        for stage in range(4):
+            for copy in self.copies(stage):
+                copy.wait_send()
+
+
+def kernel(feat, w1, w2, ws, head, targ, result, small_out, *scratch):
     s = types.SimpleNamespace(**dict(zip(SCRATCH_NAMES, scratch)))
     t, r, c = lax.axis_index("tm"), lax.axis_index("row"), lax.axis_index("col")
     place = (t, r, c)
@@ -296,7 +497,7 @@
         for dr in (-1, 0, 1, 2)
         for dc in (-1, 0, 1)
         if (dt, dr, dc) != (0, 0, 0) and (dt == 0 or dr < 2)
-    ]
+    ] + [(2, 0, 0), (0, 0, -2), (0, 0, 2), (0, 0, 4)]
     for dt, dr, dc in around:
         pl.semaphore_signal(
             barrier,
@@ -305,8 +506,42 @@
             device_id_type=MESH,
         )
 
+    core = c & 1
+    mate = (t, r, c + 1 - 2 * core)
+
+    def to_mate(number, src, dst):
+        return pltpu.make_async_remote_copy(
+            src_ref=src,
+            dst_ref=dst,
+            send_sem=s.mate_send.at[number],
+            recv_sem=s.mate_recv.at[number],
+            device_id=mate,
+            device_id_type=MESH,
+        )
+
+    mates = [
+        to_mate(0, feat, s.mate0.at[3, pl.ds(FR, FR), pl.ds(1, TH)]),
+        to_mate(1, s.shift0.at[pl.ds(0, 3), pl.ds(FR, FR)], s.mate0.at[pl.ds(0, 3), pl.ds(FR, FR)]),
+        to_mate(2, s.shift0.at[pl.ds(0, 3), pl.ds(0, FR)], s.mate0.at[pl.ds(0, 3), pl.ds(0, FR)]),
+        to_mate(3, s.shift1.at[:, pl.ds(FR, FR)], s.mate1.at[:, pl.ds(FR, FR)]),
+        to_mate(4, s.shift1.at[:, pl.ds(0, FR)], s.mate1.at[:, pl.ds(0, FR)]),
+        to_mate(5, s.grads.at[1], s.mate_grads.at[1]),
+        to_mate(6, s.grads.at[0], s.mate_grads.at[0]),
+    ]
+
+    def tile_rows(step):
+        rows = CHUNK // TW
+        return step // (TH // rows), lax.rem(step, TH // rows) * rows
+
+    def features(step):
+        frame, row = tile_rows(step)
+        return feat[frame, pl.ds(row, CHUNK // TW)].reshape(CHUNK, C_IN)
+
     def act(rows, step):
-        values = silu_forward(feat[rows, :].astype(F32))
+        raw = features(step)
+        frame, row = tile_rows(step)
+        s.shift0[3, FR + frame, pl.ds(row + 1, CHUNK // TW)] = raw.reshape(CHUNK // TW, TW, C_IN)
+        values = silu_forward(raw.astype(F32))
         put_tile(s.own0, s.columns, step, values)
 
     chunks(act)
@@ -321,12 +556,15 @@
     y_copies = picture_copies(place, s.target, s.y_field, s.send_y, s.recv_y)
     for copy in y_copies:
         copy.start()
+    mates[0].start()
 
     halo0.arrived(0)
     halo0.shift(0, s.shift0, FR)
+    mates[1].start()
     convolve(s.shift0, w1, s.pre, FR, 2, FR, 1, NT, False, True)
     halo0.arrived(1)
     halo0.shift(1, s.shift0, 0)
+    mates[2].start()
     convolve(s.shift0, w1, s.pre, 0, 0, 1, 0, NT, False, False)
 
     def act_first(rows, step):
@@ -337,14 +575,16 @@
     halo1.start(s.columns)
     halo1.arrived(0)
     halo1.shift(0, s.shift1, FR)
+    mates[3].start()
     convolve(s.shift1, w2, s.block, FR, 2, FR, 1, NN, False, True)
 
     def shortcut(rows, step):
-        s.block[rows, :] += lax.dot_general(feat[rows, :], ws[...], NT, preferred_element_type=F32)
+        s.block[rows, :] += lax.dot_general(features(step), ws[...], NT, preferred_element_type=F32)
 
     chunks(shortcut)
     halo1.arrived(1)
     halo1.shift(1, s.shift1, 0)
+    mates[4].start()
     convolve(s.shift1, w2, s.block, 0, 0, 1, 0, NN, False, False)
 
     s.headf[...] = jnp.zeros(s.headf.shape, F32)
@@ -376,7 +616,6 @@
     for copy in x_copies:
         copy.wait_recv()
     loss = picture_loss(place, s.image, s.target, s.x_field, s.y_field, s.spread)
-    loss_out[...] = jnp.broadcast_to(loss, loss_out.shape)
 
     grad_head = None
     for part in range(4):
@@ -389,7 +628,12 @@
         s.colors[part] = color
         term = high_dot(color, s.values1[rows, :])
         grad_head = term if grad_head is None else grad_head + term
-    gh[...] = grad_head
+    tail = jnp.concatenate([grad_head[:, 128:], jnp.zeros((8, 64), F32)], axis=1)
+    small = Small(s, place)
+    small.start(
+        0,
+        jnp.concatenate([grad_head[0:3, 0:128], tail[0:3], jnp.zeros((1, 128), F32), loss], axis=0),
+    )
 
     def back_block(rows, step):
         grad = lax.dot_general(s.colors[step], s.headf[...], TN, precision=HIGH, preferred_element_type=F32)
@@ -399,22 +643,35 @@
 
     chunks(back_block)
     halo2.start(s.columns)
-    block_t = s.values1[...].T.astype(BF16)
-    s.block_t[...] = block_t
+    s.grads[1] = s.values1[...].T.astype(BF16)
+    mates[5].start()
+    parts = [Reduce(s, place, part, result) for part in range(PARTS)]
+    s.flat[LINES - C_MID :, :] = jnp.zeros((C_MID, 128), F32)
+    small.start(1, small.finish(0))
     halo2.arrived(0)
     halo2.shift(0, s.shift2, 0)
     convolve(s.shift2, w2, s.back, 0, 2, 1, 0, NT, True, True)
-
-    def second(step, carry):
-        time, row = step // 3, lax.rem(step, 3)
-        for col in range(3):
+    for number in (3, 4, 5):
+        mates[number].wait_recv()
+
+    def second(pair, carry):
+        halves = []
+        for which in range(2):
+            slot = jnp.minimum(core * SLOTS + pair * 2 + which, 26)
+            time, row, col = slot // 9, lax.rem(slot // 3, 3), lax.rem(slot, 3)
             data = s.shift1[col, pl.ds(time, FR), pl.ds(row, TH)].reshape(VOX, C_MID)
-            result = lax.dot_general(s.block_t[...], data, NN, preferred_element_type=F32)
-            g2[step * 3 + col] = result.T
+            term = lax.dot_general(s.grads[1], data, NN, preferred_element_type=F32)
+            data = s.mate1[col, pl.ds(time, FR), pl.ds(row, TH)].reshape(VOX, C_MID)
+            term = term + lax.dot_general(s.mate_grads[1], data, NN, preferred_element_type=F32)
+            halves.append(term.T)
+        at = pl.multiple_of(SECOND_AT + pair * (3 * C_MID), C_MID)
+        s.flat[pl.ds(at, C_MID), :] = halves[0][:, 0:128]
+        s.flat[pl.ds(at + C_MID, C_MID), :] = halves[1][:, 0:128]
+        s.flat[pl.ds(at + 2 * C_MID, C_MID), :] = jnp.concatenate([halves[0][:, 128:], halves[1][:, 128:]], axis=1)
         return carry
 
-    lax.fori_loop(0, 9, second, 0)
-    g1[27] = lax.dot_general(s.block_t[...], feat[...], NN, preferred_element_type=F32)
+    lax.fori_loop(0, SLOTS // 2, second, 0)
+    parts[2].scatter_start(0)
     halo2.arrived(1)
     halo2.shift(1, s.shift2, FR)
     convolve(s.shift2, w2, s.back, FR, 0, FR, 1, NT, True, False)
@@ -423,38 +680,102 @@
         s.values1[rows, :] = silu_backward(s.pre[rows, :], s.back[rows, :])
 
     chunks(back_first)
-    s.block_t[...] = s.values1[...].T.astype(BF16)
+    s.grads[0] = s.values1[...].T.astype(BF16)
+    mates[6].start()
+    parts[2].scatter_middle(0)
+    small.start(2, small.finish(1))
+    for number in (0, 1, 2, 6):
+        mates[number].wait_recv()
 
     def first(step, carry):
-        time, row = step // 3, lax.rem(step, 3)
-        for col in range(3):
-            data = s.shift0[col, pl.ds(time, FR), pl.ds(row, TH)].reshape(VOX, C_IN)
-            g1[step * 3 + col] = lax.dot_general(s.block_t[...], data, NN, preferred_element_type=F32)
+        slot = core * SLOTS + step
+        extra = (slot == 27).astype(jnp.int32)
+        time, row, col = slot // 9 - extra, lax.rem(slot // 3, 3) + extra, lax.rem(slot, 3) + 3 * extra
+        data = s.shift0[col, pl.ds(time, FR), pl.ds(row, TH)].reshape(VOX, C_IN)
+        term = lax.dot_general(s.grads[extra], data, NN, preferred_element_type=F32)
+        data = s.mate0[col, pl.ds(time, FR), pl.ds(row, TH)].reshape(VOX, C_IN)
+        term = term + lax.dot_general(s.mate_grads[extra], data, NN, preferred_element_type=F32)
+        at = pl.multiple_of(step * (3 * C_MID), C_MID)
+        for block in range(3):
+            s.flat[pl.ds(at + block * C_MID, C_MID), :] = term[:, block * 128 : block * 128 + 128]
         return carry
 
-    lax.fori_loop(0, 9, first, 0)
+    lax.fori_loop(0, 8, first, 0)
+    parts[0].scatter_start(0)
+    lax.fori_loop(8, SLOTS, first, 0)
+    parts[1].scatter_start(0)
+    small.start(3, small.finish(2))
+    parts[2].scatter_finish(0)
+    parts[2].scatter_start(1)
+    for part in (0, 1):
+        parts[part].scatter_middle(0)
+    parts[2].scatter_middle(1)
+    small_out[...] = small.finish(3)
+    for part in (0, 1):
+        parts[part].scatter_finish(0)
+        parts[part].scatter_start(1)
+    parts[2].scatter_finish(1)
+    parts[2].scatter_start(2)
+    for part in (0, 1):
+        parts[part].scatter_middle(1)
+    parts[2].scatter_middle(2)
+    for part in (0, 1):
+        parts[part].scatter_finish(1)
+        parts[part].scatter_start(2)
+    parts[2].scatter_finish(2)
+    parts[2].gather_start(2)
+    for part in (0, 1):
+        parts[part].scatter_middle(2)
+    parts[2].gather_middle(2)
+    for part in (0, 1):
+        parts[part].scatter_finish(2)
+        parts[part].gather_start(2)
+    parts[2].gather_finish(2)
+    parts[2].gather_start(1)
+    for part in (0, 1):
+        parts[part].gather_middle(2)
+    parts[2].gather_middle(1)
+    for part in (0, 1):
+        parts[part].gather_finish(2)
+        parts[part].gather_start(1)
+    parts[2].gather_finish(1)
+    parts[2].gather_start(0)
+    for part in (0, 1):
+        parts[part].gather_middle(1)
+    parts[2].gather_middle(0)
+    for part in (0, 1):
+        parts[part].gather_finish(1)
+        parts[part].gather_start(0)
+    parts[2].gather_finish(0)
+    for part in (0, 1):
+        parts[part].gather_middle(0)
+    for part in (0, 1):
+        parts[part].gather_finish(0)
+    for part in parts:
+        part.settle()
     for halo in (halo0, halo1, halo2):
         halo.sent()
-    for copy in x_copies + y_copies:
+    for copy in x_copies + y_copies + mates:
         copy.wait_send()
-
-
-def halo_scratch(number, chan):
+    small.settle()
+
+
+def halo_scratch(number, chan, copies):
     return [
         (f"own{number}", pltpu.VMEM((FR, TH + 2, TW, chan), BF16)),
         (f"other{number}", pltpu.VMEM((FR, TH + 2, TW, chan), BF16)),
         (f"rims{number}", pltpu.VMEM((2, 2, 3, FR * TH, chan), BF16)),
         (f"edges{number}", pltpu.VMEM((2, FR * TH, chan), BF16)),
-        (f"shift{number}", pltpu.VMEM((3, 2 * FR, TH + 2, TW, chan), BF16)),
+        (f"shift{number}", pltpu.VMEM((copies, 2 * FR, TH + 2, TW, chan), BF16)),
         (f"send{number}", pltpu.SemaphoreType.DMA((18,))),
         (f"recv{number}", pltpu.SemaphoreType.DMA((18,))),
     ]
 
 
 SCRATCH = (
-    halo_scratch(0, C_IN)
-    + halo_scratch(1, C_MID)
-    + halo_scratch(2, C_MID)
+    halo_scratch(0, C_IN, 4)
+    + halo_scratch(1, C_MID, 3)
+    + halo_scratch(2, C_MID, 3)
     + [
         ("lines0", pltpu.VMEM((2, FR, 16, C_IN), F32)),
         ("lines1", pltpu.VMEM((2, FR, 16, C_MID), F32)),
@@ -463,7 +784,30 @@
         ("pre", pltpu.VMEM((VOX, C_MID), F32)),
         ("block", pltpu.VMEM((VOX, C_MID), F32)),
         ("back", pltpu.VMEM((VOX, C_MID), F32)),
-        ("block_t", pltpu.VMEM((C_MID, VOX), BF16)),
+        ("grads", pltpu.VMEM((2, C_MID, VOX), BF16)),
+        ("mate_grads", pltpu.VMEM((2, C_MID, VOX), BF16)),
+        ("mate0", pltpu.VMEM((4, 2 * FR, TH + 2, TW, C_IN), BF16)),
+        ("mate1", pltpu.VMEM((3, 2 * FR, TH + 2, TW, C_MID), BF16)),
+        ("mate_send", pltpu.SemaphoreType.DMA((7,))),
+        ("mate_recv", pltpu.SemaphoreType.DMA((7,))),
+        ("flat", pltpu.VMEM((LINES, 128), F32)),
+        ("sum1", pltpu.VMEM((PARTS, SIZES[0], 128), F32)),
+        ("sum2", pltpu.VMEM((PARTS, SIZES[1], 128), F32)),
+        ("stage0", pltpu.VMEM((PARTS, 6, SIZES[0] // 2, 128), BF16)),
+        ("stage1", pltpu.VMEM((PARTS, 2, SIZES[1] // 2, 128), F32)),
+        ("stage2", pltpu.VMEM((PARTS, 2, SIZES[2] // 2, 128), F32)),
+        ("inbox0", pltpu.VMEM((PARTS, 6, SIZES[0] // 2, 128), BF16)),
+        ("inbox1", pltpu.VMEM((PARTS, 6, SIZES[1] // 2, 128), F32)),
+        ("inbox2", pltpu.VMEM((PARTS, 6, SIZES[2] // 2, 128), F32)),
+        ("scatter_send", pltpu.SemaphoreType.DMA((54,))),
+        ("scatter_recv", pltpu.SemaphoreType.DMA((54,))),
+        ("gather_send", pltpu.SemaphoreType.DMA((54,))),
+        ("gather_recv", pltpu.SemaphoreType.DMA((54,))),
+        ("share_send", pltpu.SemaphoreType.DMA((12,))),
+        ("share_recv", pltpu.SemaphoreType.DMA((12,))),
+        ("small", pltpu.VMEM((4, 4, 8, 128), F32)),
+        ("small_send", pltpu.SemaphoreType.DMA((12,))),
+        ("small_recv", pltpu.SemaphoreType.DMA((12,))),
         ("headf", pltpu.VMEM((8, C_MID), F32)),
         ("spread", pltpu.VMEM((128, 128), F32)),
         ("colors", pltpu.VMEM((4, 8, 128), F32)),
@@ -480,37 +824,74 @@
 SCRATCH_NAMES = [name for name, _ in SCRATCH]
 
 
+def widen(first_ref, second_ref, small_ref, g1, gs, g2, gh, loss):
+    for which in range(2):
+        for block in range(3):
+            at = (which * 3 + block) * C_MID
+            values = first_ref[0, at : at + C_MID, :].astype(F32)
+            g1[which, :, block * 128 : block * 128 + 128] = values
+    gs[...] = g1[1]
+    g2[0, :, 0:128] = second_ref[0, 0:C_MID, :].astype(F32)
+    g2[1, :, 0:128] = second_ref[0, C_MID : 2 * C_MID, :].astype(F32)
+    rest = second_ref[0, 2 * C_MID : 3 * C_MID, :].astype(F32)
+    g2[0, :, 128:] = rest[:, 0:64]
+    g2[1, :, 128:] = rest[:, 64:]
+    gh[:, 0:128] = small_ref[0:3, :]
+    gh[:, 128:] = small_ref[3:6, 0:64]
+    loss[...] = jnp.sum(small_ref[7:8, :], axis=1, keepdims=True) / (N_TM * N_ROW * N_COL)
+
+
 def body(features, conv_first, conv_second, shortcut_weight, head_weight, target_frames):
     vmem = pl.BlockSpec(memory_space=pltpu.VMEM)
-    g1, g2, gh, loss = pl.pallas_call(
+    flat, small = pl.pallas_call(
         kernel,
         out_shape=[
-            jax.ShapeDtypeStruct((28, C_MID, C_IN), F32),
-            jax.ShapeDtypeStruct((27, C_MID, C_MID), F32),
-            jax.ShapeDtypeStruct((8, C_MID), F32),
+            jax.ShapeDtypeStruct((2, LINES, 128), BF16),
             jax.ShapeDtypeStruct((8, 128), F32),
         ],
         in_specs=[vmem] * 6,
-        out_specs=[vmem] * 4,
+        out_specs=[vmem] * 2,
         scratch_shapes=[shape for _, shape in SCRATCH],
         compiler_params=pltpu.CompilerParams(
             collective_id=0, has_side_effects=True, vmem_limit_bytes=60 * 1024 * 1024
         ),
     )(
-        features.reshape(VOX, C_IN),
+        features,
         conv_first.transpose(0, 1, 2, 4, 3).reshape(27, C_MID, C_IN),
         conv_second.reshape(27, C_MID, C_MID),
         shortcut_weight.T,
         head_weight.T,
         target_frames.reshape(6, TH, TW),
     )
-    g1, g2, gh, loss = lax.psum((g1, g2, gh[:3], jnp.sum(loss[0])), ("tm", "row", "col"))
+    g1, gs, g2, gh, loss = pl.pallas_call(
+        widen,
+        grid=(SLOTS,),
+        out_shape=[
+            jax.ShapeDtypeStruct((27, C_MID, C_IN), F32),
+            jax.ShapeDtypeStruct((C_MID, C_IN), F32),
+            jax.ShapeDtypeStruct((27, C_MID, C_MID), F32),
+            jax.ShapeDtypeStruct((3, C_MID), F32),
+            jax.ShapeDtypeStruct((1, 1), F32),
+        ],
+        in_specs=[
+            pl.BlockSpec((1, 6 * C_MID, 128), lambda i: (i // 7, lax.rem(i, 7), 0)),
+            pl.BlockSpec((1, 3 * C_MID, 128), lambda i: (i // 7, SLOTS + lax.rem(i, 7), 0)),
+            pl.BlockSpec((8, 128), lambda i: (0, 0)),
+        ],
+        out_specs=[
+            pl.BlockSpec((2, C_MID, C_IN), lambda i: (i, 0, 0)),
+            pl.BlockSpec((C_MID, C_IN), lambda i: (0, 0)),
+            pl.BlockSpec((2, C_MID, C_MID), lambda i: (i, 0, 0)),
+            pl.BlockSpec((3, C_MID), lambda i: (0, 0)),
+            pl.BlockSpec((1, 1), lambda i: (0, 0)),
+        ],
+    )(flat, flat, small)
     return (
-        g1[:27].reshape(3, 3, 3, C_MID, C_IN).transpose(0, 1, 2, 4, 3),
+        g1.reshape(3, 3, 3, C_MID, C_IN).transpose(0, 1, 2, 4, 3),
         g2.reshape(3, 3, 3, C_MID, C_MID),
-        g1[27].T,
+        gs.T,
         gh.T,
-        loss / (N_TM * N_ROW * N_COL),
+        loss.reshape(()),
     )
 
 

time: 273 us -> 144 us (0.53)
  waiting for transfers between devices: 104 us -> 0 us
  Pallas kernels: 76.1 us -> 143 us
  blocking collectives: 64.5 us -> 0 us
  between operations: 15.8 us -> 0.64 us
  local copies, waits for them, and re-layouts: 11.7 us -> 0 us
    psum x1 -> x0, waiting for transfers between devices: 104 us -> none  [body(): lax.psum((g1, g2, gh[:3], jnp.sum(loss[0])), ('tm', 'row', 'col'))]
    pallas_call x1 -> x2, Pallas kernels: 76.1 us -> 143 us  [the longest x1 131 us: body(): pl.pallas_call(kernel, out_shape=[jax.ShapeDtypeStruct((2, LINES, 128), B...]
    psum x1 -> x0, blocking collectives: 64.5 us -> none  [body(): lax.psum((g1, g2, gh[:3], jnp.sum(loss[0])), ('tm', 'row', 'col'))]
    slice x1 -> x0, local copies, waits for them, and re-layouts: 7.46 us -> none  [body(): g1[:27].reshape(3, 3, 3, C_MID, C_IN).transpose(0, 1, 2, 4, 3)]
  transfers between devices with their start and end apart: 1 -> 0, of which waited for: 1 -> 0; matrix products, arithmetic and copies ran while one was open for 0% -> 0% of each run, Pallas kernels for 0% -> 0%
where the time goes in v2:
time: 144 us; the launch traced here: 143 us
  Pallas kernels  143 us (99%)
    pallas_call x1, Pallas kernels, body(): pl.pallas_call(kernel, out_shape=[jax.ShapeDtypeStruct((2, LINES, 128), B...  131 us
    pallas_call x1, Pallas kernels, body(): pl.pallas_call(widen, grid=(SLOTS,), out_shape=[jax.ShapeDtypeStruct((27,...  12 us

profile of v2, /device:TPU:1, one launch (start us, length us, event | category | flops | bytes accessed | tf_op | source)
XLA Modules:
  0.0 143.2 jit_solution(1133711759487134818)
XLA Ops:
  0.6 130.6 %shard_map.101 = (bf16[2,12288,128]{2,1,0:T(8,128)(2,1)}, f32[8,128]{1,0:T(8,128)}) custom-call(bf16[2,8,32,384]{3,2,1,0:T(8,128)(2,1)} %feat.1, bf16[27,192,384]{2,1,0:T(8,128)(2,1)} %bitcast.14, bf16[27,192,192]{2,1,0:T(8,128)(2,1)} %bitcast.15, bf16[192,384]{1,0:T(8,128)(2,1)} %bitcast.16, bf16[3,192]{1,0:T(4,128)(2,1)} %bitcast.18, f32[6,8,32]{2,1,0:T(8,128)} %bitcast.17), custom_call_target="tpu_custom_call" | custom-call | tf_op jit(solution)/shard_map/pallas_call | solution.py:846
  131.2 12.0 %shard_map.102 = (f32[27,192,384]{2,1,0:T(8,128)}, f32[192,384]{1,0:T(8,128)}, f32[27,192,192]{2,1,0:T(8,128)}, f32[3,192]{1,0:T(4,128)}, f32[1,1]{1,0:T(1,128)}) custom-call(bf16[2,12288,128]{2,1,0:T(8,128)(2,1)} %get-tuple-element.12.first_ref.second_ref, bf16[2,12288,128]{2,1,0:T(8,128)(2,1)} %get-tuple-element.12.first_ref.second_ref, ...), custom_call_target="tpu_custom_call" | custom-call | tf_op jit(solution)/shard_map/pallas_call | solution.py:866

commit v3 on v2

--- a/solution.py
+++ b/solution.py
@@ -26,12 +26,15 @@
 NT = (((1,), (1,)), ((), ()))
 NN = (((1,), (0,)), ((), ()))
 TN = (((0,), (0,)), ((), ()))
-PARTS, SPAN = 3, 4096
-SIZES = (1024, 256, 64)
+SMALL = 96
+LARGE = 4 * SMALL
+SPAN = 4 * LARGE
+PARTS, GROUPS = 3, 3
 AXES = ("yzx", "zxy", "xyz")
 SLOTS = 14
-LINES = PARTS * SPAN
-SECOND_AT = SLOTS * 3 * C_MID
+GROUP = PARTS * SPAN
+LINES = GROUPS * GROUP
+FILLED = SLOTS // 2 * 3 * C_MID
 SIDES = [(-1, -1), (0, -1), (1, -1), (-1, 1), (0, 1), (1, 1)]
 
 
@@ -101,9 +104,9 @@
     def start(self, edges_ref):
         chan = self.edges.shape[-1]
         self.edges[...] = edges_ref[:, :, 0:chan].astype(BF16)
-        for group in (0, 1):
-            for copy in self.copies(group):
-                copy.start()
+        near, far = self.copies(0), self.copies(1)
+        for copy in far[8:] + near + far[:8]:
+            copy.start()
 
     def arrived(self, group):
         for copy in self.copies(group):
@@ -299,121 +302,66 @@
 
 
 class Reduce:
-    def __init__(self, s, place, part, result):
-        self.s, self.part, self.result = s, part, result
+    def __init__(self, s, place, group, result):
+        self.s, self.group, self.result = s, group, result
         self.core = place[2] & 1
         self.mate = (place[0], place[1], place[2] + 1 - 2 * self.core)
-        lines = [axis_line(place, axis) for axis in AXES[part]]
-        self.at = [line[0] for line in lines]
-        self.there = [line[1] for line in lines]
-
-    def held(self, phase, chunk, half):
-        size = SIZES[phase]
-        index = lax.rem(self.at[phase] + (chunk + 4), 4)
-        base = self.part * SPAN if phase == 0 else 0
-        at = pl.multiple_of(base + index * size + half * (size // 2), 32)
-        ref = (self.s.flat, self.s.sum1.at[self.part], self.s.sum2.at[self.part])[phase]
-        return ref.at[pl.ds(at, size // 2), :]
-
-    def inbox(self, phase):
-        return (self.s.inbox0, self.s.inbox1, self.s.inbox2)[phase].at[self.part]
-
-    def stage(self, phase):
-        return (self.s.stage0, self.s.stage1, self.s.stage2)[phase].at[self.part]
-
-    def scatter_copy(self, phase, number):
-        if phase == 0 or number >= 4:
-            src = self.stage(phase).at[number if phase == 0 else number - 4]
-        else:
-            src = self.held(phase, *((2, 0), (2, 1), (1, 1), (-1, 0))[number])
-        sem = (self.part * 3 + phase) * 6 + number
+        self.lines = [[axis_line(place, axis) for axis in AXES[part]] for part in range(PARTS)]
+
+    def at(self, part, phase, step=0):
+        return lax.rem(self.lines[part][phase][0] + (step + 4), 4)
+
+    def copy(self, part, phase, stage, step, src, dst):
+        sem = ((self.group * PARTS + part) * 5 + stage) * 3 + step - 1
         return pltpu.make_async_remote_copy(
             src_ref=src,
-            dst_ref=self.inbox(phase).at[number],
-            send_sem=self.s.scatter_send.at[sem],
-            recv_sem=self.s.scatter_recv.at[sem],
-            device_id=self.there[phase](1 if number % 2 == 0 else -1),
+            dst_ref=dst,
+            send_sem=self.s.ring_send.at[sem],
+            recv_sem=self.s.ring_recv.at[sem],
+            device_id=self.lines[part][phase][1](step),
             device_id_type=MESH,
         )
 
-    def scatter_start(self, phase):
-        for number, (chunk, half) in enumerate(((2, 0), (2, 1), (1, 1), (-1, 0))):
-            if phase == 0:
-                self.stage(0)[number] = self.held(0, chunk, half)[...].astype(BF16)
-            self.scatter_copy(phase, number).start()
-
-    def scatter_middle(self, phase):
-        for number, (chunk, half) in ((4, (1, 0)), (5, (-1, 1))):
-            self.scatter_copy(phase, number - 4).wait_recv()
-            stage = self.stage(phase).at[number if phase == 0 else number - 4]
-            total = self.held(phase, chunk, half)[...] + self.inbox(phase)[number - 4].astype(F32)
-            stage[...] = total.astype(stage.dtype)
-            self.scatter_copy(phase, number).start()
-
-    def scatter_finish(self, phase):
-        for number in (2, 3, 4, 5):
-            self.scatter_copy(phase, number).wait_recv()
-        half_size = SIZES[phase] // 2
-        for half, (first, second) in ((0, (4, 3)), (1, (2, 5))):
-            total = self.held(phase, 0, half)[...] + (
-                self.inbox(phase)[first].astype(F32) + self.inbox(phase)[second].astype(F32)
-            )
-            if phase == 0:
-                self.s.sum1[self.part, half * half_size : (half + 1) * half_size, :] = total
-            elif phase == 1:
-                self.s.sum2[self.part, half * half_size : (half + 1) * half_size, :] = total
-            else:
-                self.region(2, 0, half, self.core)[...] = total.astype(BF16)
-
-    def region(self, phase, chunk, half, core):
-        size = SIZES[phase]
-        base = self.part * SPAN
-        for outer in range(phase):
-            base = base + self.at[outer] * SIZES[outer]
-        base = base + lax.rem(self.at[phase] + (chunk + 4), 4) * size
-        if half is None:
-            return self.result.at[core, pl.ds(pl.multiple_of(base, 32), size), :]
-        return self.result.at[core, pl.ds(pl.multiple_of(base + half * (size // 2), 32), size // 2), :]
-
-    def gather_copy(self, phase, number, arriving):
-        chunk, half = ((0, 0), (0, 1), (0, 1), (0, 0), (-1, 0), (1, 1))[number]
-        way = 1 if number % 2 == 0 else -1
-        block = self.region(phase, chunk - way if arriving else chunk, half, self.core)
-        sem = (self.part * 3 + phase) * 6 + number
-        return pltpu.make_async_remote_copy(
-            src_ref=block,
-            dst_ref=block,
-            send_sem=self.s.gather_send.at[sem],
-            recv_sem=self.s.gather_recv.at[sem],
-            device_id=self.there[phase](way),
-            device_id_type=MESH,
-        )
-
-    def gather_start(self, phase):
-        for number in range(4):
-            self.gather_copy(phase, number, False).start()
-        if phase == 0:
-            self.share(0).start()
-
-    def gather_middle(self, phase):
-        for number in (4, 5):
-            self.gather_copy(phase, number - 4, True).wait_recv()
-            self.gather_copy(phase, number, False).start()
-
-    def gather_finish(self, phase):
-        for number in (2, 3):
-            self.gather_copy(phase, number, True).wait_recv()
-        if phase == 0:
-            self.share(1).start()
-            self.share(-1).start()
-        for number in (4, 5):
-            self.gather_copy(phase, number, True).wait_recv()
-        if phase == 0:
-            self.share(2).start()
-
-    def share(self, chunk, arriving=False):
-        block = self.region(0, chunk, None, 1 - self.core if arriving else self.core)
-        sem = self.part * 4 + chunk % 4
+    def base(self, part):
+        return (self.group * PARTS + part) * SPAN
+
+    def lines_of(self, part, step):
+        return pl.ds(pl.multiple_of(self.base(part) + self.at(part, 0, step) * LARGE, 32), LARGE)
+
+    def region(self, part, large, small=None, core=None):
+        core = self.core if core is None else core
+        base = self.base(part) + self.at(part, 0, large) * LARGE
+        if small is None:
+            return self.result.at[core, pl.ds(pl.multiple_of(base, 32), LARGE), :]
+        base = base + self.at(part, 1, small) * SMALL
+        return self.result.at[core, pl.ds(pl.multiple_of(base, 32), SMALL), :]
+
+    def send(self, part, stage, step):
+        s, group = self.s, self.group
+        if stage == 0:
+            where = (group, part, step - 1)
+            return self.copy(part, 0, 0, step, s.stage0.at[where], s.inbox0.at[where])
+        if stage == 1:
+            src = s.sum1.at[group, part, pl.ds(pl.multiple_of(self.at(part, 1, step) * SMALL, 32), SMALL), :]
+            return self.copy(part, 1, 1, step, src, s.inbox1.at[group, part, step - 1])
+        if stage == 2:
+            block = s.last.at[group, part, self.at(part, 2)]
+            return self.copy(part, 2, 2, step, block, block)
+        block = self.region(part, 0, 0) if stage == 3 else self.region(part, 0)
+        return self.copy(part, 1 if stage == 3 else 0, stage, step, block, block)
+
+    def arrival(self, part, stage, step):
+        if stage < 2:
+            return self.send(part, stage, step)
+        if stage == 2:
+            block = self.s.last.at[self.group, part, self.at(part, 2, -step)]
+            return self.copy(part, 2, 2, step, block, block)
+        block = self.region(part, 0, -step) if stage == 3 else self.region(part, -step)
+        return self.copy(part, 1 if stage == 3 else 0, stage, step, block, block)
+
+    def share(self, part, large, arriving=False):
+        block = self.region(part, large, core=1 - self.core if arriving else None)
+        sem = (self.group * PARTS + part) * 4 + (large + 4) % 4
         return pltpu.make_async_remote_copy(
             src_ref=block,
             dst_ref=block,
@@ -423,15 +371,44 @@
             device_id_type=MESH,
         )
 
+    def run(self, stage):
+        s, group = self.s, self.group
+        for part in range(PARTS):
+            if stage > 0:
+                for step in (1, 3, 2):
+                    self.arrival(part, stage - 1, step).wait_recv()
+                    if stage == 5:
+                        self.share(part, -step).start()
+            if stage == 0:
+                for step in (2, 1, 3):
+                    s.stage0[group, part, step - 1] = s.flat[self.lines_of(part, step), :].astype(BF16)
+            elif stage == 1:
+                total = s.inbox0[group, part, 0].astype(F32) + s.inbox0[group, part, 1].astype(F32)
+                total = total + s.inbox0[group, part, 2].astype(F32)
+                s.sum1[group, part] = s.flat[self.lines_of(part, 0), :] + total
+            elif stage == 2:
+                own = s.sum1[group, part, pl.ds(pl.multiple_of(self.at(part, 1) * SMALL, 32), SMALL), :]
+                total = s.inbox1[group, part, 0] + s.inbox1[group, part, 1] + s.inbox1[group, part, 2]
+                s.last[group, part, self.at(part, 2)] = own + total
+            elif stage == 3:
+                total = s.last[group, part, 0] + s.last[group, part, 1]
+                total = total + s.last[group, part, 2] + s.last[group, part, 3]
+                self.region(part, 0, 0)[...] = total.astype(BF16)
+            if stage < 5:
+                for step in (2, 1, 3):
+                    self.send(part, stage, step).start()
+            if stage == 4:
+                self.share(part, 0).start()
+
     def settle(self):
-        for chunk in range(4):
-            self.share(chunk, True).wait_recv()
-        for phase in range(3):
-            for number in range(6):
-                self.scatter_copy(phase, number).wait_send()
-                self.gather_copy(phase, number, False).wait_send()
-        for chunk in range(4):
-            self.share(chunk).wait_send()
+        for part in range(PARTS):
+            for large in range(4):
+                self.share(part, large, True).wait_recv()
+            for stage in range(5):
+                for step in (1, 2, 3):
+                    self.send(part, stage, step).wait_send()
+            for large in range(4):
+                self.share(part, large).wait_send()
 
 
 class Small:
@@ -485,11 +462,16 @@
                 copy.wait_send()
 
 
-def kernel(feat, w1, w2, ws, head, targ, result, small_out, *scratch):
+def kernel(feat, w1_hbm, w2_hbm, ws, head, targ, result, small_out, *scratch):
     s = types.SimpleNamespace(**dict(zip(SCRATCH_NAMES, scratch)))
     t, r, c = lax.axis_index("tm"), lax.axis_index("row"), lax.axis_index("col")
     place = (t, r, c)
 
+    w1, w2 = s.w1, s.w2
+    loads = [
+        pltpu.make_async_copy(w1_hbm, w1, s.load.at[0]),
+        pltpu.make_async_copy(w2_hbm, w2, s.load.at[1]),
+    ]
     barrier = pltpu.get_barrier_semaphore()
     around = [
         (dt, dr, dc)
@@ -537,6 +519,9 @@
         frame, row = tile_rows(step)
         return feat[frame, pl.ds(row, CHUNK // TW)].reshape(CHUNK, C_IN)
 
+    for load in loads:
+        load.start()
+
     def act(rows, step):
         raw = features(step)
         frame, row = tile_rows(step)
@@ -561,6 +546,7 @@
     halo0.arrived(0)
     halo0.shift(0, s.shift0, FR)
     mates[1].start()
+    loads[0].wait()
     convolve(s.shift0, w1, s.pre, FR, 2, FR, 1, NT, False, True)
     halo0.arrived(1)
     halo0.shift(1, s.shift0, 0)
@@ -576,6 +562,7 @@
     halo1.arrived(0)
     halo1.shift(0, s.shift1, FR)
     mates[3].start()
+    loads[1].wait()
     convolve(s.shift1, w2, s.block, FR, 2, FR, 1, NN, False, True)
 
     def shortcut(rows, step):
@@ -645,8 +632,9 @@
     halo2.start(s.columns)
     s.grads[1] = s.values1[...].T.astype(BF16)
     mates[5].start()
-    parts = [Reduce(s, place, part, result) for part in range(PARTS)]
-    s.flat[LINES - C_MID :, :] = jnp.zeros((C_MID, 128), F32)
+    groups = [Reduce(s, place, group, result) for group in range(GROUPS)]
+    for group in range(GROUPS):
+        s.flat[group * GROUP + FILLED : (group + 1) * GROUP, :] = jnp.zeros((GROUP - FILLED, 128), F32)
     small.start(1, small.finish(0))
     halo2.arrived(0)
     halo2.shift(0, s.shift2, 0)
@@ -664,14 +652,14 @@
             data = s.mate1[col, pl.ds(time, FR), pl.ds(row, TH)].reshape(VOX, C_MID)
             term = term + lax.dot_general(s.mate_grads[1], data, NN, preferred_element_type=F32)
             halves.append(term.T)
-        at = pl.multiple_of(SECOND_AT + pair * (3 * C_MID), C_MID)
+        at = pl.multiple_of(2 * GROUP + pair * (3 * C_MID), C_MID)
         s.flat[pl.ds(at, C_MID), :] = halves[0][:, 0:128]
         s.flat[pl.ds(at + C_MID, C_MID), :] = halves[1][:, 0:128]
         s.flat[pl.ds(at + 2 * C_MID, C_MID), :] = jnp.concatenate([halves[0][:, 128:], halves[1][:, 128:]], axis=1)
         return carry
 
     lax.fori_loop(0, SLOTS // 2, second, 0)
-    parts[2].scatter_start(0)
+    groups[2].run(0)
     halo2.arrived(1)
     halo2.shift(1, s.shift2, FR)
     convolve(s.shift2, w2, s.back, FR, 0, FR, 1, NT, True, False)
@@ -682,7 +670,7 @@
     chunks(back_first)
     s.grads[0] = s.values1[...].T.astype(BF16)
     mates[6].start()
-    parts[2].scatter_middle(0)
+    groups[2].run(1)
     small.start(2, small.finish(1))
     for number in (0, 1, 2, 6):
         mates[number].wait_recv()
@@ -695,64 +683,31 @@
         term = lax.dot_general(s.grads[extra], data, NN, preferred_element_type=F32)
         data = s.mate0[col, pl.ds(time, FR), pl.ds(row, TH)].reshape(VOX, C_IN)
         term = term + lax.dot_general(s.mate_grads[extra], data, NN, preferred_element_type=F32)
-        at = pl.multiple_of(step * (3 * C_MID), C_MID)
+        late = (step >= SLOTS // 2).astype(jnp.int32)
+        at = pl.multiple_of(late * GROUP + (step - late * (SLOTS // 2)) * (3 * C_MID), C_MID)
         for block in range(3):
             s.flat[pl.ds(at + block * C_MID, C_MID), :] = term[:, block * 128 : block * 128 + 128]
         return carry
 
-    lax.fori_loop(0, 8, first, 0)
-    parts[0].scatter_start(0)
-    lax.fori_loop(8, SLOTS, first, 0)
-    parts[1].scatter_start(0)
+    lax.fori_loop(0, SLOTS // 2, first, 0)
+    groups[0].run(0)
+    groups[2].run(2)
+    lax.fori_loop(SLOTS // 2, SLOTS, first, 0)
+    groups[1].run(0)
+    groups[2].run(3)
     small.start(3, small.finish(2))
-    parts[2].scatter_finish(0)
-    parts[2].scatter_start(1)
-    for part in (0, 1):
-        parts[part].scatter_middle(0)
-    parts[2].scatter_middle(1)
+    groups[0].run(1)
+    groups[2].run(4)
+    groups[1].run(1)
+    groups[0].run(2)
+    groups[2].run(5)
+    groups[1].run(2)
     small_out[...] = small.finish(3)
-    for part in (0, 1):
-        parts[part].scatter_finish(0)
-        parts[part].scatter_start(1)
-    parts[2].scatter_finish(1)
-    parts[2].scatter_start(2)
-    for part in (0, 1):
-        parts[part].scatter_middle(1)
-    parts[2].scatter_middle(2)
-    for part in (0, 1):
-        parts[part].scatter_finish(1)
-        parts[part].scatter_start(2)
-    parts[2].scatter_finish(2)
-    parts[2].gather_start(2)
-    for part in (0, 1):
-        parts[part].scatter_middle(2)
-    parts[2].gather_middle(2)
-    for part in (0, 1):
-        parts[part].scatter_finish(2)
-        parts[part].gather_start(2)
-    parts[2].gather_finish(2)
-    parts[2].gather_start(1)
-    for part in (0, 1):
-        parts[part].gather_middle(2)
-    parts[2].gather_middle(1)
-    for part in (0, 1):
-        parts[part].gather_finish(2)
-        parts[part].gather_start(1)
-    parts[2].gather_finish(1)
-    parts[2].gather_start(0)
-    for part in (0, 1):
-        parts[part].gather_middle(1)
-    parts[2].gather_middle(0)
-    for part in (0, 1):
-        parts[part].gather_finish(1)
-        parts[part].gather_start(0)
-    parts[2].gather_finish(0)
-    for part in (0, 1):
-        parts[part].gather_middle(0)
-    for part in (0, 1):
-        parts[part].gather_finish(0)
-    for part in parts:
-        part.settle()
+    for stage in (3, 4, 5):
+        groups[0].run(stage)
+        groups[1].run(stage)
+    for group in groups:
+        group.settle()
     for halo in (halo0, halo1, halo2):
         halo.sent()
     for copy in x_copies + y_copies + mates:
@@ -777,6 +732,9 @@
     + halo_scratch(1, C_MID, 3)
     + halo_scratch(2, C_MID, 3)
     + [
+        ("w1", pltpu.VMEM((27, C_MID, C_IN), BF16)),
+        ("w2", pltpu.VMEM((27, C_MID, C_MID), BF16)),
+        ("load", pltpu.SemaphoreType.DMA((2,))),
         ("lines0", pltpu.VMEM((2, FR, 16, C_IN), F32)),
         ("lines1", pltpu.VMEM((2, FR, 16, C_MID), F32)),
         ("columns", pltpu.VMEM((2, FR * TH, C_IN), F32)),
@@ -791,20 +749,15 @@
         ("mate_send", pltpu.SemaphoreType.DMA((7,))),
         ("mate_recv", pltpu.SemaphoreType.DMA((7,))),
         ("flat", pltpu.VMEM((LINES, 128), F32)),
-        ("sum1", pltpu.VMEM((PARTS, SIZES[0], 128), F32)),
-        ("sum2", pltpu.VMEM((PARTS, SIZES[1], 128), F32)),
-        ("stage0", pltpu.VMEM((PARTS, 6, SIZES[0] // 2, 128), BF16)),
-        ("stage1", pltpu.VMEM((PARTS, 2, SIZES[1] // 2, 128), F32)),
-        ("stage2", pltpu.VMEM((PARTS, 2, SIZES[2] // 2, 128), F32)),
-        ("inbox0", pltpu.VMEM((PARTS, 6, SIZES[0] // 2, 128), BF16)),
-        ("inbox1", pltpu.VMEM((PARTS, 6, SIZES[1] // 2, 128), F32)),
-        ("inbox2", pltpu.VMEM((PARTS, 6, SIZES[2] // 2, 128), F32)),
-        ("scatter_send", pltpu.SemaphoreType.DMA((54,))),
-        ("scatter_recv", pltpu.SemaphoreType.DMA((54,))),
-        ("gather_send", pltpu.SemaphoreType.DMA((54,))),
-        ("gather_recv", pltpu.SemaphoreType.DMA((54,))),
-        ("share_send", pltpu.SemaphoreType.DMA((12,))),
-        ("share_recv", pltpu.SemaphoreType.DMA((12,))),
+        ("stage0", pltpu.VMEM((GROUPS, PARTS, 3, LARGE, 128), BF16)),
+        ("inbox0", pltpu.VMEM((GROUPS, PARTS, 3, LARGE, 128), BF16)),
+        ("sum1", pltpu.VMEM((GROUPS, PARTS, LARGE, 128), F32)),
+        ("inbox1", pltpu.VMEM((GROUPS, PARTS, 3, SMALL, 128), F32)),
+        ("last", pltpu.VMEM((GROUPS, PARTS, 4, SMALL, 128), F32)),
+        ("ring_send", pltpu.SemaphoreType.DMA((GROUPS * PARTS * 15,))),
+        ("ring_recv", pltpu.SemaphoreType.DMA((GROUPS * PARTS * 15,))),
+        ("share_send", pltpu.SemaphoreType.DMA((GROUPS * PARTS * 4,))),
+        ("share_recv", pltpu.SemaphoreType.DMA((GROUPS * PARTS * 4,))),
         ("small", pltpu.VMEM((4, 4, 8, 128), F32)),
         ("small_send", pltpu.SemaphoreType.DMA((12,))),
         ("small_recv", pltpu.SemaphoreType.DMA((12,))),
@@ -824,36 +777,56 @@
 SCRATCH_NAMES = [name for name, _ in SCRATCH]
 
 
-def widen(first_ref, second_ref, small_ref, g1, gs, g2, gh, loss):
-    for which in range(2):
+def widen(flat, small_ref, g1, gs, g2, gh, loss, wide1, wide2, sems):
+    copies = []
+
+    def one1(slot, carry):
+        core, step = slot // SLOTS, lax.rem(slot, SLOTS)
+        late = step // (SLOTS // 2)
+        at = pl.multiple_of(late * GROUP + (step - late * (SLOTS // 2)) * (3 * C_MID), C_MID)
         for block in range(3):
-            at = (which * 3 + block) * C_MID
-            values = first_ref[0, at : at + C_MID, :].astype(F32)
-            g1[which, :, block * 128 : block * 128 + 128] = values
-    gs[...] = g1[1]
-    g2[0, :, 0:128] = second_ref[0, 0:C_MID, :].astype(F32)
-    g2[1, :, 0:128] = second_ref[0, C_MID : 2 * C_MID, :].astype(F32)
-    rest = second_ref[0, 2 * C_MID : 3 * C_MID, :].astype(F32)
-    g2[0, :, 128:] = rest[:, 0:64]
-    g2[1, :, 128:] = rest[:, 64:]
+            rows = flat[core, pl.ds(at + block * C_MID, C_MID), :]
+            wide1[slot, :, block * 128 : block * 128 + 128] = rows.astype(F32)
+        return carry
+
+    def one2(pair, carry):
+        core, step = pair // (SLOTS // 2), lax.rem(pair, SLOTS // 2)
+        at = pl.multiple_of(2 * GROUP + step * (3 * C_MID), C_MID)
+        wide2[2 * pair, :, 0:128] = flat[core, pl.ds(at, C_MID), :].astype(F32)
+        wide2[2 * pair + 1, :, 0:128] = flat[core, pl.ds(at + C_MID, C_MID), :].astype(F32)
+        rest = flat[core, pl.ds(at + 2 * C_MID, C_MID), :].astype(F32)
+        wide2[2 * pair, :, 128:] = rest[:, 0:64]
+        wide2[2 * pair + 1, :, 128:] = rest[:, 64:]
+        return carry
+
+    for piece in range(7):
+        lax.fori_loop(4 * piece, 4 * piece + 4, one1, 0)
+        last = min(4 * piece + 4, 27)
+        rows = pl.ds(4 * piece, last - 4 * piece)
+        copies.append(pltpu.make_async_copy(wide1.at[rows], g1.at[rows], sems.at[len(copies)]))
+        copies[-1].start()
+        lax.fori_loop(2 * piece, 2 * piece + 2, one2, 0)
+        copies.append(pltpu.make_async_copy(wide2.at[rows], g2.at[rows], sems.at[len(copies)]))
+        copies[-1].start()
+    copies.append(pltpu.make_async_copy(wide1.at[27], gs, sems.at[len(copies)]))
+    copies[-1].start()
     gh[:, 0:128] = small_ref[0:3, :]
     gh[:, 128:] = small_ref[3:6, 0:64]
     loss[...] = jnp.sum(small_ref[7:8, :], axis=1, keepdims=True) / (N_TM * N_ROW * N_COL)
+    for copy in copies:
+        copy.wait()
 
 
 def body(features, conv_first, conv_second, shortcut_weight, head_weight, target_frames):
-    vmem = pl.BlockSpec(memory_space=pltpu.VMEM)
+    vmem, hbm = pl.BlockSpec(memory_space=pltpu.VMEM), pl.BlockSpec(memory_space=pl.ANY)
     flat, small = pl.pallas_call(
         kernel,
-        out_shape=[
-            jax.ShapeDtypeStruct((2, LINES, 128), BF16),
-            jax.ShapeDtypeStruct((8, 128), F32),
-        ],
-        in_specs=[vmem] * 6,
+        out_shape=[pltpu.VMEM((2, LINES, 128), BF16), pltpu.VMEM((8, 128), F32)],
+        in_specs=[vmem, hbm, hbm, vmem, vmem, vmem],
         out_specs=[vmem] * 2,
         scratch_shapes=[shape for _, shape in SCRATCH],
         compiler_params=pltpu.CompilerParams(
-            collective_id=0, has_side_effects=True, vmem_limit_bytes=60 * 1024 * 1024
+            collective_id=0, has_side_effects=True, vmem_limit_bytes=52 * 1024 * 1024
         ),
     )(
         features,
@@ -865,7 +838,6 @@
     )
     g1, gs, g2, gh, loss = pl.pallas_call(
         widen,
-        grid=(SLOTS,),
         out_shape=[
             jax.ShapeDtypeStruct((27, C_MID, C_IN), F32),
             jax.ShapeDtypeStruct((C_MID, C_IN), F32),
@@ -873,19 +845,15 @@
             jax.ShapeDtypeStruct((3, C_MID), F32),
             jax.ShapeDtypeStruct((1, 1), F32),
         ],
-        in_specs=[
-            pl.BlockSpec((1, 6 * C_MID, 128), lambda i: (i // 7, lax.rem(i, 7), 0)),
-            pl.BlockSpec((1, 3 * C_MID, 128), lambda i: (i // 7, SLOTS + lax.rem(i, 7), 0)),
-            pl.BlockSpec((8, 128), lambda i: (0, 0)),
+        in_specs=[vmem] * 2,
+        out_specs=[hbm] * 3 + [vmem] * 2,
+        scratch_shapes=[
+            pltpu.VMEM((28, C_MID, C_IN), F32),
+            pltpu.VMEM((28, C_MID, C_MID), F32),
+            pltpu.SemaphoreType.DMA((15,)),
         ],
-        out_specs=[
-            pl.BlockSpec((2, C_MID, C_IN), lambda i: (i, 0, 0)),
-            pl.BlockSpec((C_MID, C_IN), lambda i: (0, 0)),
-            pl.BlockSpec((2, C_MID, C_MID), lambda i: (i, 0, 0)),
-            pl.BlockSpec((3, C_MID), lambda i: (0, 0)),
-            pl.BlockSpec((1, 1), lambda i: (0, 0)),
-        ],
-    )(flat, flat, small)
+        compiler_params=pltpu.CompilerParams(vmem_limit_bytes=40 * 1024 * 1024),
+    )(flat, small)
     return (
         g1.reshape(3, 3, 3, C_MID, C_IN).transpose(0, 1, 2, 4, 3),
         g2.reshape(3, 3, 3, C_MID, C_MID),

time: 144 us -> 125 us (0.87)
  Pallas kernels: 143 us -> 124 us
    pallas_call x2, Pallas kernels: 143 us -> 124 us  [the longest x1 118 us: body(): pl.pallas_call(kernel, out_shape=[pltpu.VMEM((2, LINES, 128), BF16), pltp...]
where the time goes in v3:
time: 125 us; the launch traced here: 124 us
  Pallas kernels  124 us (99%)
    pallas_call x1, Pallas kernels, body(): pl.pallas_call(kernel, out_shape=[pltpu.VMEM((2, LINES, 128), BF16), pltp...  118 us
    pallas_call x1, Pallas kernels, body(): pl.pallas_call(widen, out_shape=[jax.ShapeDtypeStruct((27, C_MID, C_IN),...  5.75 us

profile of v3, /device:TPU:1, one launch (start us, length us, event | category | flops | bytes accessed | tf_op | source)
XLA Modules:
  0.0 124.5 jit_solution(13877696218612663123)
XLA Ops:
  0.6 118.1 %shard_map.101 = (bf16[2,13824,128]{2,1,0:T(8,128)(2,1)S(1)}, f32[8,128]{1,0:T(8,128)S(1)}) custom-call(bf16[2,8,32,384]{3,2,1,0:T(8,128)(2,1)} %feat.1, bf16[27,192,384]{2,1,0:T(8,128)(2,1)} %bitcast.14, bf16[27,192,192]{2,1,0:T(8,128)(2,1)} %bitcast.15, bf16[192,384]{1,0:T(8,128)(2,1)} %bitcast.16, bf16[3,192]{1,0:T(4,128)(2,1)} %bitcast.18, ...), custom_call_target="tpu_custom_call" | custom-call | tf_op jit(solution)/shard_map/pallas_call | solution.py:822
  118.7 5.8 %shard_map.102 = (f32[27,192,384]{2,1,0:T(8,128)}, f32[192,384]{1,0:T(8,128)}, f32[27,192,192]{2,1,0:T(8,128)}, f32[3,192]{1,0:T(4,128)}, f32[1,1]{1,0:T(1,128)}) custom-call(bf16[2,13824,128]{2,1,0:T(8,128)(2,1)S(1)} %get-tuple-element.12.flat, f32[8,128]{1,0:T(8,128)S(1)} %get-tuple-element.13.small_ref), custom_call_target="tpu_custom_call" | custom-call | tf_op jit(solution)/shard_map/pallas_call | solution.py:839

commit v4 on v3

--- a/solution.py
+++ b/solution.py
@@ -26,15 +26,16 @@
 NT = (((1,), (1,)), ((), ()))
 NN = (((1,), (0,)), ((), ()))
 TN = (((0,), (0,)), ((), ()))
-SMALL = 96
-LARGE = 4 * SMALL
-SPAN = 4 * LARGE
 PARTS, GROUPS = 3, 3
+SMALL = (96, 80, 96)
+LARGE = tuple(4 * size for size in SMALL)
+SPAN = tuple(4 * size for size in LARGE)
 AXES = ("yzx", "zxy", "xyz")
 SLOTS = 14
-GROUP = PARTS * SPAN
-LINES = GROUPS * GROUP
-FILLED = SLOTS // 2 * 3 * C_MID
+START = (0, PARTS * SPAN[0], PARTS * (SPAN[0] + SPAN[1]))
+LINES = PARTS * sum(SPAN)
+FIRST_FILLED, SECOND_FILLED = SLOTS * 3 * C_MID, START[2] + SLOTS // 2 * 3 * C_MID
+EARLY = 8
 SIDES = [(-1, -1), (0, -1), (1, -1), (-1, 1), (0, 1), (1, 1)]
 
 
@@ -69,58 +70,68 @@
 
 
 class Halo:
-    def __init__(self, place, ahead, own, other, rims, edges, lines, send, recv):
-        self.place, self.ahead = place, ahead
+    def __init__(self, place, ahead, chan, own, other, rims, edges, lines, send, recv):
+        self.place, self.ahead, self.chan = place, ahead, chan
+        self.packed = chan % 128 != 0
         self.tiles, self.rims, self.edges, self.lines = (own, other), rims, edges, lines
         self.send, self.recv = send, recv
 
-    def copies(self, group):
+    def copy(self, number, src, dst, dt, dr, dc):
         t, r, c = self.place
-        own, target = self.tiles[0], self.tiles[group]
-        there = wrap(t, self.ahead * group, N_TM)
-        items = []
-
-        def add(number, src, dst, dr, dc):
-            items.append(
-                pltpu.make_async_remote_copy(
-                    src_ref=src,
-                    dst_ref=dst,
-                    send_sem=self.send.at[9 * group + number],
-                    recv_sem=self.recv.at[9 * group + number],
-                    device_id=(there, wrap(r, dr, N_ROW), wrap(c, dc, N_COL)),
-                    device_id_type=MESH,
-                )
-            )
-
-        add(0, own.at[:, 1], target.at[:, 9], -1, 0)
-        add(1, own.at[:, 8], target.at[:, 0], 1, 0)
+        return pltpu.make_async_remote_copy(
+            src_ref=src,
+            dst_ref=dst,
+            send_sem=self.send.at[number],
+            recv_sem=self.recv.at[number],
+            device_id=(wrap(t, dt, N_TM), wrap(r, dr, N_ROW), wrap(c, dc, N_COL)),
+            device_id_type=MESH,
+        )
+
+    def rows(self, group, at):
+        tile = self.tiles[group]
+        return tile.at[at] if self.packed else tile.at[:, at]
+
+    def near(self):
+        items = [
+            self.copy(0, self.rows(0, 1), self.rows(0, TH + 1), 0, -1, 0),
+            self.copy(1, self.rows(0, TH), self.rows(0, 0), 0, 1, 0),
+        ]
         for number, (dr, dc) in enumerate(SIDES):
             side = 0 if dc == 1 else 1
-            add(2 + number, self.edges.at[1 - side], self.rims.at[group, side, 1 - dr], dr, dc)
-        if group == 1:
-            add(8, own.at[:, pl.ds(1, TH)], target.at[:, pl.ds(1, TH)], 0, 0)
+            items.append(self.copy(2 + number, self.edges.at[1 - side], self.rims.at[0, side, 1 - dr], 0, dr, dc))
         return items
 
+    def far_tile(self):
+        middle = pl.ds(1, TH)
+        return self.copy(8, self.rows(0, middle), self.rows(1, middle), self.ahead, 0, 0)
+
+    def far_rim(self):
+        return [
+            self.copy(9, self.rims.at[0], self.rims.at[1], self.ahead, 0, 0),
+            self.copy(10, self.rows(0, 0), self.rows(1, 0), self.ahead, 0, 0),
+            self.copy(11, self.rows(0, TH + 1), self.rows(1, TH + 1), self.ahead, 0, 0),
+        ]
+
     def start(self, edges_ref):
-        chan = self.edges.shape[-1]
-        self.edges[...] = edges_ref[:, :, 0:chan].astype(BF16)
-        near, far = self.copies(0), self.copies(1)
-        for copy in far[8:] + near + far[:8]:
+        self.far_tile().start()
+        self.edges[...] = edges_ref[:, :, 0 : self.chan].astype(BF16)
+        for copy in self.near():
             copy.start()
 
     def arrived(self, group):
-        for copy in self.copies(group):
+        for copy in self.near() if group == 0 else [self.far_tile()] + self.far_rim():
             copy.wait_recv()
+        if group == 0:
+            for copy in self.far_rim():
+                copy.start()
 
     def sent(self):
-        for group in (0, 1):
-            for copy in self.copies(group):
-                copy.wait_send()
+        for copy in self.near() + [self.far_tile()] + self.far_rim():
+            copy.wait_send()
 
     def shift(self, group, shifted, frame_at):
         t, r, c = self.place
-        tile, lines = self.tiles[group], self.lines
-        chan = tile.shape[-1]
+        tile, lines, chan = self.tiles[group], self.lines, self.chan
         for side in (0, 1):
             for frame in range(FR):
                 at = slice(frame * TH, frame * TH + TH)
@@ -135,23 +146,28 @@
         left = jnp.where(c == 0, 0.0, 1.0)
         right = jnp.where(c == N_COL - 1, 0.0, 1.0)
         column = iota((TW, chan), 0)
-
-        def one(step, carry):
-            frame, row = step // (TH + 2), lax.rem(step, TH + 2)
-            scale = live * jnp.where(row == 0, top, jnp.where(row == TH + 1, bottom, 1.0))
-            base = tile[frame, row].astype(F32) * scale
-            first = lines[0, frame, pl.ds(row, 1), :] * (scale * left)
-            last = lines[1, frame, pl.ds(row, 1), :] * (scale * right)
-            shifted[0, frame_at + frame, row] = jnp.where(column == 0, first, pltpu.roll(base, 1, 0)).astype(BF16)
-            shifted[1, frame_at + frame, row] = base.astype(BF16)
-            shifted[2, frame_at + frame, row] = jnp.where(column == TW - 1, last, pltpu.roll(base, TW - 1, 0)).astype(BF16)
-            return carry
-
-        lax.fori_loop(0, FR * (TH + 2), one, 0)
+        for frame in range(FR):
+
+            def one(row, carry, frame=frame):
+                scale = live * jnp.where(row == 0, top, jnp.where(row == TH + 1, bottom, 1.0))
+                if self.packed:
+                    base = tile[row].astype(F32)[:, frame * chan : (frame + 1) * chan] * scale
+                else:
+                    base = tile[frame, row].astype(F32) * scale
+                first = lines[0, frame, pl.ds(row, 1), :] * (scale * left)
+                last = lines[1, frame, pl.ds(row, 1), :] * (scale * right)
+                before, after = pltpu.roll(base, 1, 0), pltpu.roll(base, TW - 1, 0)
+                shifted[0, frame_at + frame, row] = jnp.where(column == 0, first, before).astype(BF16)
+                shifted[1, frame_at + frame, row] = base.astype(BF16)
+                shifted[2, frame_at + frame, row] = jnp.where(column == TW - 1, last, after).astype(BF16)
+                return carry
+
+            lax.fori_loop(0, TH + 2, one, 0)
 
 
 def convolve(shifted, weights, total, full_at, full_tap, half_at, half_out, dims, flip, first):
-    half = VOX // FR
+    half, chan = VOX // FR, shifted.shape[-1]
+    joined = chan % 128 == 0
 
     def one(row, carry):
         def tap(time, col):
@@ -159,19 +175,23 @@
                 return weights[(time * 3 + 2 - row) * 3 + 2 - col]
             return weights[(time * 3 + row) * 3 + col]
 
-        chan = shifted.shape[-1]
-        full = None
-        part = None
-        for col in range(3):
-            data = shifted[col, pl.ds(full_at, FR), pl.ds(row, TH)].reshape(VOX, chan)
-            term = lax.dot_general(data, tap(full_tap, col), dims, preferred_element_type=F32)
-            full = term if full is None else full + term
-        total[...] += full
-        for col in range(3):
-            data = shifted[col, half_at, pl.ds(row, TH)].reshape(half, chan)
-            term = lax.dot_general(data, tap(1, col), dims, preferred_element_type=F32)
-            part = term if part is None else part + term
-        total[pl.ds(half_out * half, half), :] += part
+        def data(frame, col):
+            return shifted[col, frame, pl.ds(row, TH)].reshape(half, chan)
+
+        for out in range(FR):
+            terms = [(full_at + out, full_tap, col) for col in range(3)]
+            if out == half_out:
+                terms += [(half_at, 1, col) for col in range(3)]
+            if joined:
+                values = jnp.concatenate([data(frame, col) for frame, _, col in terms], axis=1)
+                taps = jnp.concatenate([tap(time, col) for _, time, col in terms], axis=dims[0][1][0])
+                result = lax.dot_general(values, taps, dims, preferred_element_type=F32)
+            else:
+                result = None
+                for frame, time, col in terms:
+                    term = lax.dot_general(data(frame, col), tap(time, col), dims, preferred_element_type=F32)
+                    result = term if result is None else result + term
+            total[out * half : (out + 1) * half, :] += result
         return carry
 
     if first:
@@ -183,22 +203,23 @@
 
 
 def chunks(body):
-    def one(step, carry):
-        body(pl.ds(pl.multiple_of(step * CHUNK, CHUNK), CHUNK), step)
-        return carry
-
-    lax.fori_loop(0, VOX // CHUNK, one, 0)
+    for step in range(VOX // CHUNK):
+        body(slice(step * CHUNK, (step + 1) * CHUNK), step)
 
 
 def put_tile(tile, edges, step, values):
     rows = CHUNK // TW
     chan = values.shape[-1]
     for at in range(rows):
-        edges[0, pl.ds(step * rows + at, 1), 0:chan] = values[at * TW : at * TW + 1]
-        edges[1, pl.ds(step * rows + at, 1), 0:chan] = values[at * TW + TW - 1 : at * TW + TW]
-    values = values.astype(BF16)
-    frame, row = step // (TH // rows), lax.rem(step, TH // rows) * rows
-    tile[frame, pl.ds(row + 1, rows)] = values.reshape(rows, TW, values.shape[-1])
+        line = step * rows + at
+        edges[0, line : line + 1, 0:chan] = values[at * TW : at * TW + 1]
+        edges[1, line : line + 1, 0:chan] = values[at * TW + TW - 1 : at * TW + TW]
+    frame, row = divmod(step * rows, TH)
+    values = values.astype(BF16).reshape(rows, TW, chan)
+    if len(tile.shape) == 3:
+        tile[row + 1 : row + 1 + rows, :, frame * chan : (frame + 1) * chan] = values
+    else:
+        tile[frame, row + 1 : row + 1 + rows] = values
 
 
 def picture_copies(place, tile, field, send, recv):
@@ -236,19 +257,41 @@
     return jnp.dot(a, b, precision=HIGH, preferred_element_type=F32)
 
 
-def picture_loss(place, x_tile, y_tile, x_field, y_field, spread):
+def thirds(values):
+    high = values.astype(BF16).astype(F32)
+    rest = values - high
+    middle = rest.astype(BF16).astype(F32)
+    return jnp.concatenate([high, middle, rest - middle], axis=0)
+
+
+WINDOW = TH + 16
+
+
+def picture_bands(place, across, down, down_own):
+    across[...] = band(iota((128, 128), 0) - iota((128, 128), 1), True)
+    out, source = iota(down.shape, 0), iota(down.shape, 1)
+    picture = sum((out >= WINDOW * at).astype(jnp.int32) for at in range(1, 6))
+    line = out - WINDOW * picture + (place[1] * TH - 8)
+    down[...] = band(line - (source & 31), (picture == (source >> 5)) & (line >= 0) & (line < N_ROW * TH))
+    out, source = iota(down_own.shape, 0), iota(down_own.shape, 1)
+    picture = sum((source >= WINDOW * at).astype(jnp.int32) for at in range(1, 6))
+    down_own[...] = band((out & 7) + 8 - (source - WINDOW * picture), (out >> 3) == picture)
+
+
+def blurred(maps, across, down):
+    rows = maps[0].shape[0]
+    wide = high_dot(jnp.concatenate(maps, axis=0), across[...])
+    wide = jnp.concatenate([wide[m * rows : (m + 1) * rows] for m in range(len(maps))], axis=1)
+    result = high_dot(down[...], wide)
+    return [result[:, m * 128 : (m + 1) * 128] for m in range(len(maps))]
+
+
+def picture_loss(place, x_tile, y_tile, x_field, y, mean_y, square_y, bands, spread):
     t, r, c = place
-    rows = 6 * N_ROW * TH
-    x, y = canvas(place, x_tile, x_field), canvas(place, y_tile, y_field)
-    across = band(iota((128, 128), 0) - iota((128, 128), 1), True)
-    row_a, row_b = iota((rows, rows), 0), iota((rows, rows), 1)
-    down = band(row_a - row_b, (row_a >> 5) == (row_b >> 5))
-    own_a, own_b = iota((48, rows), 0), iota((48, rows), 1)
-    down_own = band((own_a & 7) + r * TH - (own_b & 31), (own_a >> 3) == (own_b >> 5))
-    wide = high_dot(jnp.concatenate([x, y, x * x, y * y, x * y], axis=0), across)
-    mean_x, mean_y, square_x, square_y, cross = [
-        high_dot(down, wide[m * rows : (m + 1) * rows]) for m in range(5)
-    ]
+    across, down, down_own = bands
+    x = canvas(place, x_tile, x_field)
+    mean_x, square_x, cross = blurred([x, x * x, x * y], across, down)
+    rows = 6 * WINDOW
     var_x = square_x - mean_x * mean_x
     var_y = square_y - mean_y * mean_y
     covar = cross - mean_x * mean_y
@@ -263,17 +306,15 @@
     )
     slope_square = -ssim / denom_b
     slope_cross = 2.0 * numer_a / denom_all
-    lane, line = iota((rows, 128), 1), iota((rows, 128), 0) & 31
+    lane, line = iota((rows, 128), 1), iota((rows, 128), 0)
+    line = line - WINDOW * sum((line >= WINDOW * at).astype(jnp.int32) for at in range(1, 6)) + (r * TH - 8)
     low = jnp.where(c == 0, TW, TW - 5)
     high = jnp.where(c == N_COL - 1, 2 * TW, 2 * TW + 5)
-    inside = (lane >= low) & (lane < high)
+    inside = (lane >= low) & (lane < high) & (line >= 0) & (line < N_ROW * TH)
     mine = (lane >= TW) & (lane < 2 * TW) & (line >= r * TH) & (line < r * TH + TH)
     loss = jnp.sum(jnp.where(mine, 1.0 - ssim, 0.0), axis=0, keepdims=True)
-    adjoint = jnp.concatenate(
-        [jnp.where(inside, slope * (-1.0 / PIX), 0.0) for slope in (slope_mean, slope_square, slope_cross)], axis=0
-    )
-    wide = high_dot(adjoint, across)
-    pulled = [high_dot(down_own, wide[m * rows : (m + 1) * rows]) for m in range(3)]
+    adjoint = [jnp.where(inside, slope * (-1.0 / PIX), 0.0) for slope in (slope_mean, slope_square, slope_cross)]
+    pulled = blurred(adjoint, across, down_own)
     x_own = pltpu.roll(x_tile[...].reshape(48, 128), TW, 1)
     y_own = pltpu.roll(y_tile[...].reshape(48, 128), TW, 1)
     lane = iota((48, 128), 1)
@@ -304,6 +345,7 @@
 class Reduce:
     def __init__(self, s, place, group, result):
         self.s, self.group, self.result = s, group, result
+        self.small, self.large = SMALL[group], LARGE[group]
         self.core = place[2] & 1
         self.mate = (place[0], place[1], place[2] + 1 - 2 * self.core)
         self.lines = [[axis_line(place, axis) for axis in AXES[part]] for part in range(PARTS)]
@@ -323,29 +365,29 @@
         )
 
     def base(self, part):
-        return (self.group * PARTS + part) * SPAN
+        return START[self.group] + part * SPAN[self.group]
 
     def lines_of(self, part, step):
-        return pl.ds(pl.multiple_of(self.base(part) + self.at(part, 0, step) * LARGE, 32), LARGE)
+        return pl.ds(pl.multiple_of(self.base(part) + self.at(part, 0, step) * self.large, 16), self.large)
 
     def region(self, part, large, small=None, core=None):
         core = self.core if core is None else core
-        base = self.base(part) + self.at(part, 0, large) * LARGE
+        base = self.base(part) + self.at(part, 0, large) * self.large
         if small is None:
-            return self.result.at[core, pl.ds(pl.multiple_of(base, 32), LARGE), :]
-        base = base + self.at(part, 1, small) * SMALL
-        return self.result.at[core, pl.ds(pl.multiple_of(base, 32), SMALL), :]
+            return self.result.at[core, pl.ds(pl.multiple_of(base, 16), self.large), :]
+        base = base + self.at(part, 1, small) * self.small
+        return self.result.at[core, pl.ds(pl.multiple_of(base, 16), self.small), :]
 
     def send(self, part, stage, step):
         s, group = self.s, self.group
         if stage == 0:
-            where = (group, part, step - 1)
+            where = (group, part, step - 1, pl.ds(0, self.large))
             return self.copy(part, 0, 0, step, s.stage0.at[where], s.inbox0.at[where])
         if stage == 1:
-            src = s.sum1.at[group, part, pl.ds(pl.multiple_of(self.at(part, 1, step) * SMALL, 32), SMALL), :]
-            return self.copy(part, 1, 1, step, src, s.inbox1.at[group, part, step - 1])
+            src = s.sum1.at[group, part, pl.ds(pl.multiple_of(self.at(part, 1, step) * self.small, 16), self.small), :]
+            return self.copy(part, 1, 1, step, src, s.inbox1.at[group, part, step - 1, pl.ds(0, self.small)])
         if stage == 2:
-            block = s.last.at[group, part, self.at(part, 2)]
+            block = s.last.at[group, part, self.at(part, 2), pl.ds(0, self.small)]
             return self.copy(part, 2, 2, step, block, block)
         block = self.region(part, 0, 0) if stage == 3 else self.region(part, 0)
         return self.copy(part, 1 if stage == 3 else 0, stage, step, block, block)
@@ -354,7 +396,7 @@
         if stage < 2:
             return self.send(part, stage, step)
         if stage == 2:
-            block = self.s.last.at[self.group, part, self.at(part, 2, -step)]
+            block = self.s.last.at[self.group, part, self.at(part, 2, -step), pl.ds(0, self.small)]
             return self.copy(part, 2, 2, step, block, block)
         block = self.region(part, 0, -step) if stage == 3 else self.region(part, -step)
         return self.copy(part, 1 if stage == 3 else 0, stage, step, block, block)
@@ -379,22 +421,22 @@
                     self.arrival(part, stage - 1, step).wait_recv()
                     if stage == 5:
                         self.share(part, -step).start()
+            large, small = pl.ds(0, self.large), pl.ds(0, self.small)
             if stage == 0:
                 for step in (2, 1, 3):
-                    s.stage0[group, part, step - 1] = s.flat[self.lines_of(part, step), :].astype(BF16)
+                    s.stage0[group, part, step - 1, large, :] = s.flat[self.lines_of(part, step), :].astype(BF16)
+                    self.send(part, 0, step).start()
             elif stage == 1:
-                total = s.inbox0[group, part, 0].astype(F32) + s.inbox0[group, part, 1].astype(F32)
-                total = total + s.inbox0[group, part, 2].astype(F32)
-                s.sum1[group, part] = s.flat[self.lines_of(part, 0), :] + total
+                total = [s.inbox0[group, part, index, large, :].astype(F32) for index in range(3)]
+                s.sum1[group, part, large, :] = s.flat[self.lines_of(part, 0), :] + (total[0] + total[1] + total[2])
             elif stage == 2:
-                own = s.sum1[group, part, pl.ds(pl.multiple_of(self.at(part, 1) * SMALL, 32), SMALL), :]
-                total = s.inbox1[group, part, 0] + s.inbox1[group, part, 1] + s.inbox1[group, part, 2]
-                s.last[group, part, self.at(part, 2)] = own + total
+                own = s.sum1[group, part, pl.ds(pl.multiple_of(self.at(part, 1) * self.small, 16), self.small), :]
+                total = [s.inbox1[group, part, index, small, :] for index in range(3)]
+                s.last[group, part, self.at(part, 2), small, :] = own + (total[0] + total[1] + total[2])
             elif stage == 3:
-                total = s.last[group, part, 0] + s.last[group, part, 1]
-                total = total + s.last[group, part, 2] + s.last[group, part, 3]
-                self.region(part, 0, 0)[...] = total.astype(BF16)
-            if stage < 5:
+                total = [s.last[group, part, index, small, :] for index in range(4)]
+                self.region(part, 0, 0)[...] = ((total[0] + total[1]) + (total[2] + total[3])).astype(BF16)
+            if 0 < stage < 5:
                 for step in (2, 1, 3):
                     self.send(part, stage, step).start()
             if stage == 4:
@@ -473,13 +515,8 @@
         pltpu.make_async_copy(w2_hbm, w2, s.load.at[1]),
     ]
     barrier = pltpu.get_barrier_semaphore()
-    around = [
-        (dt, dr, dc)
-        for dt in (-1, 0, 1)
-        for dr in (-1, 0, 1, 2)
-        for dc in (-1, 0, 1)
-        if (dt, dr, dc) != (0, 0, 0) and (dt == 0 or dr < 2)
-    ] + [(2, 0, 0), (0, 0, -2), (0, 0, 2), (0, 0, 4)]
+    around = [(0, dr, dc) for dr in (-1, 0, 1, 2) for dc in (-1, 0, 1) if (dr, dc) != (0, 0)]
+    around += [(-1, 0, 0), (1, 0, 0), (2, 0, 0), (0, 0, -2), (0, 0, 2), (0, 0, 4)]
     for dt, dr, dc in around:
         pl.semaphore_signal(
             barrier,
@@ -507,13 +544,12 @@
         to_mate(2, s.shift0.at[pl.ds(0, 3), pl.ds(0, FR)], s.mate0.at[pl.ds(0, 3), pl.ds(0, FR)]),
         to_mate(3, s.shift1.at[:, pl.ds(FR, FR)], s.mate1.at[:, pl.ds(FR, FR)]),
         to_mate(4, s.shift1.at[:, pl.ds(0, FR)], s.mate1.at[:, pl.ds(0, FR)]),
-        to_mate(5, s.grads.at[1], s.mate_grads.at[1]),
-        to_mate(6, s.grads.at[0], s.mate_grads.at[0]),
+        to_mate(5, s.grads.at[1, :, pl.ds(0, VOX)], s.grads.at[1, :, pl.ds(VOX, VOX)]),
+        to_mate(6, s.grads.at[0, :, pl.ds(0, VOX)], s.grads.at[0, :, pl.ds(VOX, VOX)]),
     ]
 
     def tile_rows(step):
-        rows = CHUNK // TW
-        return step // (TH // rows), lax.rem(step, TH // rows) * rows
+        return divmod(step * (CHUNK // TW), TH)
 
     def features(step):
         frame, row = tile_rows(step)
@@ -534,14 +570,16 @@
     s.target[:, :, 0:TW] = targ[...]
     pl.semaphore_wait(barrier, len(around))
 
-    halo0 = Halo(place, 1, s.own0, s.other0, s.rims0, s.edges0, s.lines0, s.send0, s.recv0)
-    halo1 = Halo(place, 1, s.own1, s.other1, s.rims1, s.edges1, s.lines1, s.send1, s.recv1)
-    halo2 = Halo(place, -1, s.own2, s.other2, s.rims2, s.edges2, s.lines1, s.send2, s.recv2)
+    halo0 = Halo(place, 1, C_IN, s.own0, s.other0, s.rims0, s.edges0, s.lines0, s.send0, s.recv0)
+    halo1 = Halo(place, 1, C_MID, s.own1, s.other1, s.rims1, s.edges1, s.lines1, s.send1, s.recv1)
+    halo2 = Halo(place, -1, C_MID, s.own2, s.other2, s.rims2, s.edges2, s.lines1, s.send2, s.recv2)
     halo0.start(s.columns)
     y_copies = picture_copies(place, s.target, s.y_field, s.send_y, s.recv_y)
     for copy in y_copies:
         copy.start()
     mates[0].start()
+    bands = (s.across, s.down, s.down_own)
+    picture_bands(place, *bands)
 
     halo0.arrived(0)
     halo0.shift(0, s.shift0, FR)
@@ -559,6 +597,10 @@
 
     chunks(act_first)
     halo1.start(s.columns)
+    for copy in y_copies:
+        copy.wait_recv()
+    s.y_full[...] = canvas(place, s.target, s.y_field)
+    s.y_blur[0], s.y_blur[1] = blurred([s.y_full[...], s.y_full[...] * s.y_full[...]], s.across, s.down)
     halo1.arrived(0)
     halo1.shift(0, s.shift1, FR)
     mates[3].start()
@@ -598,11 +640,11 @@
     x_copies = picture_copies(place, s.image, s.x_field, s.send_x, s.recv_x)
     for copy in x_copies:
         copy.start()
-    for copy in y_copies:
-        copy.wait_recv()
     for copy in x_copies:
         copy.wait_recv()
-    loss = picture_loss(place, s.image, s.target, s.x_field, s.y_field, s.spread)
+    loss = picture_loss(
+        place, s.image, s.target, s.x_field, s.y_full[...], s.y_blur[0], s.y_blur[1], bands, s.spread
+    )
 
     grad_head = None
     for part in range(4):
@@ -612,9 +654,12 @@
             at = (4 * part + piece) * 8
             held = s.spread[at : at + 8, :]
             color = held if piece == 0 else color + pltpu.roll(held, TW * piece, 1)
-        s.colors[part] = color
-        term = high_dot(color, s.values1[rows, :])
+        split = thirds(color)
+        s.colors[part] = jnp.concatenate([split, jnp.zeros((128 - 24, 128), F32)], axis=0).T[:, 0:24].astype(BF16)
+        term = jnp.dot(split.astype(BF16), s.values1[rows, :].astype(BF16), preferred_element_type=F32)
         grad_head = term if grad_head is None else grad_head + term
+    grad_head = grad_head[0:8] + (grad_head[8:16] + grad_head[16:24])
+    heads = jnp.concatenate([s.headf[...]] * 3, axis=0).astype(BF16)
     tail = jnp.concatenate([grad_head[:, 128:], jnp.zeros((8, 64), F32)], axis=1)
     small = Small(s, place)
     small.start(
@@ -623,18 +668,18 @@
     )
 
     def back_block(rows, step):
-        grad = lax.dot_general(s.colors[step], s.headf[...], TN, precision=HIGH, preferred_element_type=F32)
+        grad = jnp.dot(s.colors[step], heads, preferred_element_type=F32)
         values = silu_backward(s.block[rows, :], grad)
         s.values1[rows, :] = values
         put_tile(s.own2, s.columns, step, values)
 
     chunks(back_block)
     halo2.start(s.columns)
-    s.grads[1] = s.values1[...].T.astype(BF16)
+    s.grads[1, :, 0:VOX] = s.values1[...].T.astype(BF16)
     mates[5].start()
     groups = [Reduce(s, place, group, result) for group in range(GROUPS)]
-    for group in range(GROUPS):
-        s.flat[group * GROUP + FILLED : (group + 1) * GROUP, :] = jnp.zeros((GROUP - FILLED, 128), F32)
+    s.flat[FIRST_FILLED : START[2], :] = jnp.zeros((START[2] - FIRST_FILLED, 128), F32)
+    s.flat[SECOND_FILLED:LINES, :] = jnp.zeros((LINES - SECOND_FILLED, 128), F32)
     small.start(1, small.finish(0))
     halo2.arrived(0)
     halo2.shift(0, s.shift2, 0)
@@ -642,17 +687,20 @@
     for number in (3, 4, 5):
         mates[number].wait_recv()
 
+    def patches(mine, theirs, slot):
+        extra = (slot == 27).astype(jnp.int32)
+        time, row, col = slot // 9 - extra, lax.rem(slot // 3, 3) + extra, lax.rem(slot, 3) + 3 * extra
+        where = (col, pl.ds(time, FR), pl.ds(row, TH))
+        chan = mine.shape[-1]
+        return jnp.concatenate([mine[where].reshape(VOX, chan), theirs[where].reshape(VOX, chan)], axis=0)
+
     def second(pair, carry):
         halves = []
         for which in range(2):
             slot = jnp.minimum(core * SLOTS + pair * 2 + which, 26)
-            time, row, col = slot // 9, lax.rem(slot // 3, 3), lax.rem(slot, 3)
-            data = s.shift1[col, pl.ds(time, FR), pl.ds(row, TH)].reshape(VOX, C_MID)
-            term = lax.dot_general(s.grads[1], data, NN, preferred_element_type=F32)
-            data = s.mate1[col, pl.ds(time, FR), pl.ds(row, TH)].reshape(VOX, C_MID)
-            term = term + lax.dot_general(s.mate_grads[1], data, NN, preferred_element_type=F32)
-            halves.append(term.T)
-        at = pl.multiple_of(2 * GROUP + pair * (3 * C_MID), C_MID)
+            data = patches(s.shift1, s.mate1, slot)
+            halves.append(lax.dot_general(s.grads[1], data, NN, preferred_element_type=F32).T)
+        at = pl.multiple_of(START[2] + pair * (3 * C_MID), 16)
         s.flat[pl.ds(at, C_MID), :] = halves[0][:, 0:128]
         s.flat[pl.ds(at + C_MID, C_MID), :] = halves[1][:, 0:128]
         s.flat[pl.ds(at + 2 * C_MID, C_MID), :] = jnp.concatenate([halves[0][:, 128:], halves[1][:, 128:]], axis=1)
@@ -668,31 +716,38 @@
         s.values1[rows, :] = silu_backward(s.pre[rows, :], s.back[rows, :])
 
     chunks(back_first)
-    s.grads[0] = s.values1[...].T.astype(BF16)
+    s.grads[0, :, 0:VOX] = s.values1[...].T.astype(BF16)
     mates[6].start()
     groups[2].run(1)
     small.start(2, small.finish(1))
     for number in (0, 1, 2, 6):
         mates[number].wait_recv()
 
-    def first(step, carry):
+    def put_slot(step, values):
+        at = pl.multiple_of(step * (3 * C_MID), C_MID)
+        for block in range(3):
+            s.flat[pl.ds(at + block * C_MID, C_MID), :] = values[:, block * 128 : block * 128 + 128]
+
+    def first(pair, carry):
+        data = [patches(s.shift0, s.mate0, core * SLOTS + 2 * pair + which) for which in range(2)]
+        data = jnp.concatenate(data, axis=1)
+        both = lax.dot_general(s.grads[0], data, NN, preferred_element_type=F32)
+        put_slot(2 * pair, both[:, 0:C_IN])
+        put_slot(2 * pair + 1, both[:, C_IN:])
+        return carry
+
+    def first_alone(step):
         slot = core * SLOTS + step
-        extra = (slot == 27).astype(jnp.int32)
-        time, row, col = slot // 9 - extra, lax.rem(slot // 3, 3) + extra, lax.rem(slot, 3) + 3 * extra
-        data = s.shift0[col, pl.ds(time, FR), pl.ds(row, TH)].reshape(VOX, C_IN)
-        term = lax.dot_general(s.grads[extra], data, NN, preferred_element_type=F32)
-        data = s.mate0[col, pl.ds(time, FR), pl.ds(row, TH)].reshape(VOX, C_IN)
-        term = term + lax.dot_general(s.mate_grads[extra], data, NN, preferred_element_type=F32)
-        late = (step >= SLOTS // 2).astype(jnp.int32)
-        at = pl.multiple_of(late * GROUP + (step - late * (SLOTS // 2)) * (3 * C_MID), C_MID)
-        for block in range(3):
-            s.flat[pl.ds(at + block * C_MID, C_MID), :] = term[:, block * 128 : block * 128 + 128]
-        return carry
-
-    lax.fori_loop(0, SLOTS // 2, first, 0)
+        data = patches(s.shift0, s.mate0, slot)
+        grads = s.grads[(slot == 27).astype(jnp.int32)]
+        put_slot(step, lax.dot_general(grads, data, NN, preferred_element_type=F32))
+
+    lax.fori_loop(0, EARLY // 2, first, 0)
     groups[0].run(0)
     groups[2].run(2)
-    lax.fori_loop(SLOTS // 2, SLOTS, first, 0)
+    lax.fori_loop(EARLY // 2, SLOTS // 2 - 1, first, 0)
+    first_alone(SLOTS - 2)
+    first_alone(SLOTS - 1)
     groups[1].run(0)
     groups[2].run(3)
     small.start(3, small.finish(2))
@@ -700,12 +755,15 @@
     groups[2].run(4)
     groups[1].run(1)
     groups[0].run(2)
-    groups[2].run(5)
     groups[1].run(2)
     small_out[...] = small.finish(3)
-    for stage in (3, 4, 5):
-        groups[0].run(stage)
-        groups[1].run(stage)
+    groups[0].run(3)
+    groups[1].run(3)
+    groups[0].run(4)
+    groups[2].run(5)
+    groups[1].run(4)
+    groups[0].run(5)
+    groups[1].run(5)
     for group in groups:
         group.settle()
     for halo in (halo0, halo1, halo2):
@@ -716,14 +774,15 @@
 
 
 def halo_scratch(number, chan, copies):
+    tile = (FR, TH + 2, TW, chan) if chan % 128 == 0 else (TH + 2, TW, FR * chan)
     return [
-        (f"own{number}", pltpu.VMEM((FR, TH + 2, TW, chan), BF16)),
-        (f"other{number}", pltpu.VMEM((FR, TH + 2, TW, chan), BF16)),
+        (f"own{number}", pltpu.VMEM(tile, BF16)),
+        (f"other{number}", pltpu.VMEM(tile, BF16)),
         (f"rims{number}", pltpu.VMEM((2, 2, 3, FR * TH, chan), BF16)),
         (f"edges{number}", pltpu.VMEM((2, FR * TH, chan), BF16)),
         (f"shift{number}", pltpu.VMEM((copies, 2 * FR, TH + 2, TW, chan), BF16)),
-        (f"send{number}", pltpu.SemaphoreType.DMA((18,))),
-        (f"recv{number}", pltpu.SemaphoreType.DMA((18,))),
+        (f"send{number}", pltpu.SemaphoreType.DMA((12,))),
+        (f"recv{number}", pltpu.SemaphoreType.DMA((12,))),
     ]
 
 
@@ -742,18 +801,17 @@
         ("pre", pltpu.VMEM((VOX, C_MID), F32)),
         ("block", pltpu.VMEM((VOX, C_MID), F32)),
         ("back", pltpu.VMEM((VOX, C_MID), F32)),
-        ("grads", pltpu.VMEM((2, C_MID, VOX), BF16)),
-        ("mate_grads", pltpu.VMEM((2, C_MID, VOX), BF16)),
+        ("grads", pltpu.VMEM((2, C_MID, 2 * VOX), BF16)),
         ("mate0", pltpu.VMEM((4, 2 * FR, TH + 2, TW, C_IN), BF16)),
         ("mate1", pltpu.VMEM((3, 2 * FR, TH + 2, TW, C_MID), BF16)),
         ("mate_send", pltpu.SemaphoreType.DMA((7,))),
         ("mate_recv", pltpu.SemaphoreType.DMA((7,))),
         ("flat", pltpu.VMEM((LINES, 128), F32)),
-        ("stage0", pltpu.VMEM((GROUPS, PARTS, 3, LARGE, 128), BF16)),
-        ("inbox0", pltpu.VMEM((GROUPS, PARTS, 3, LARGE, 128), BF16)),
-        ("sum1", pltpu.VMEM((GROUPS, PARTS, LARGE, 128), F32)),
-        ("inbox1", pltpu.VMEM((GROUPS, PARTS, 3, SMALL, 128), F32)),
-        ("last", pltpu.VMEM((GROUPS, PARTS, 4, SMALL, 128), F32)),
+        ("stage0", pltpu.VMEM((GROUPS, PARTS, 3, max(LARGE), 128), BF16)),
+        ("inbox0", pltpu.VMEM((GROUPS, PARTS, 3, max(LARGE), 128), BF16)),
+        ("sum1", pltpu.VMEM((GROUPS, PARTS, max(LARGE), 128), F32)),
+        ("inbox1", pltpu.VMEM((GROUPS, PARTS, 3, max(SMALL), 128), F32)),
+        ("last", pltpu.VMEM((GROUPS, PARTS, 4, max(SMALL), 128), F32)),
         ("ring_send", pltpu.SemaphoreType.DMA((GROUPS * PARTS * 15,))),
         ("ring_recv", pltpu.SemaphoreType.DMA((GROUPS * PARTS * 15,))),
         ("share_send", pltpu.SemaphoreType.DMA((GROUPS * PARTS * 4,))),
@@ -763,11 +821,16 @@
         ("small_recv", pltpu.SemaphoreType.DMA((12,))),
         ("headf", pltpu.VMEM((8, C_MID), F32)),
         ("spread", pltpu.VMEM((128, 128), F32)),
-        ("colors", pltpu.VMEM((4, 8, 128), F32)),
+        ("colors", pltpu.VMEM((4, 128, 24), BF16)),
         ("image", pltpu.VMEM((6, TH, 128), F32)),
         ("target", pltpu.VMEM((6, TH, 128), F32)),
         ("x_field", pltpu.VMEM((3, 6, N_ROW * TH, 128), F32)),
         ("y_field", pltpu.VMEM((3, 6, N_ROW * TH, 128), F32)),
+        ("across", pltpu.VMEM((128, 128), F32)),
+        ("down", pltpu.VMEM((6 * WINDOW, 6 * N_ROW * TH), F32)),
+        ("down_own", pltpu.VMEM((6 * TH, 6 * WINDOW), F32)),
+        ("y_full", pltpu.VMEM((6 * N_ROW * TH, 128), F32)),
+        ("y_blur", pltpu.VMEM((2, 6 * WINDOW, 128), F32)),
         ("send_x", pltpu.SemaphoreType.DMA((11,))),
         ("recv_x", pltpu.SemaphoreType.DMA((11,))),
         ("send_y", pltpu.SemaphoreType.DMA((11,))),
@@ -782,8 +845,7 @@
 
     def one1(slot, carry):
         core, step = slot // SLOTS, lax.rem(slot, SLOTS)
-        late = step // (SLOTS // 2)
-        at = pl.multiple_of(late * GROUP + (step - late * (SLOTS // 2)) * (3 * C_MID), C_MID)
+        at = pl.multiple_of(step * (3 * C_MID), C_MID)
         for block in range(3):
             rows = flat[core, pl.ds(at + block * C_MID, C_MID), :]
             wide1[slot, :, block * 128 : block * 128 + 128] = rows.astype(F32)
@@ -791,7 +853,7 @@
 
     def one2(pair, carry):
         core, step = pair // (SLOTS // 2), lax.rem(pair, SLOTS // 2)
-        at = pl.multiple_of(2 * GROUP + step * (3 * C_MID), C_MID)
+        at = pl.multiple_of(START[2] + step * (3 * C_MID), 16)
         wide2[2 * pair, :, 0:128] = flat[core, pl.ds(at, C_MID), :].astype(F32)
         wide2[2 * pair + 1, :, 0:128] = flat[core, pl.ds(at + C_MID, C_MID), :].astype(F32)
         rest = flat[core, pl.ds(at + 2 * C_MID, C_MID), :].astype(F32)

time: 125 us -> 114 us (0.912)
  Pallas kernels: 124 us -> 114 us
    pallas_call x1, Pallas kernels: 118 us -> 108 us  [body(): pl.pallas_call(kernel, out_shape=[pltpu.VMEM((2, LINES, 128), BF16), pltp...]
where the time goes in v4:
time: 114 us
  Pallas kernels  114 us (100%)
    pallas_call x1, Pallas kernels, body(): pl.pallas_call(kernel, out_shape=[pltpu.VMEM((2, LINES, 128), BF16), pltp...  108 us
    pallas_call x1, Pallas kernels, body(): pl.pallas_call(widen, out_shape=[jax.ShapeDtypeStruct((27, C_MID, C_IN),...  5.71 us

profile of v4, /device:TPU:1, one launch (start us, length us, event | category | flops | bytes accessed | tf_op | source)
XLA Modules:
  0.0 114.2 jit_solution(2353677332311103042)
XLA Ops:
  0.6 107.8 %shard_map.101 = (bf16[2,13056,128]{2,1,0:T(8,128)(2,1)S(1)}, f32[8,128]{1,0:T(8,128)S(1)}) custom-call(bf16[2,8,32,384]{3,2,1,0:T(8,128)(2,1)} %feat.1, bf16[27,192,384]{2,1,0:T(8,128)(2,1)} %bitcast.14, bf16[27,192,192]{2,1,0:T(8,128)(2,1)} %bitcast.15, bf16[192,384]{1,0:T(8,128)(2,1)} %bitcast.16, bf16[3,192]{1,0:T(4,128)(2,1)} %bitcast.18, ...), custom_call_target="tpu_custom_call" | custom-call | tf_op jit(solution)/shard_map/pallas_call | solution.py:884
  108.5 5.7 %shard_map.102 = (f32[27,192,384]{2,1,0:T(8,128)}, f32[192,384]{1,0:T(8,128)}, f32[27,192,192]{2,1,0:T(8,128)}, f32[3,192]{1,0:T(4,128)}, f32[1,1]{1,0:T(1,128)}) custom-call(bf16[2,13056,128]{2,1,0:T(8,128)(2,1)S(1)} %get-tuple-element.12.flat, f32[8,128]{1,0:T(8,128)S(1)} %get-tuple-element.13.small_ref), custom_call_target="tpu_custom_call" | custom-call | tf_op jit(solution)/shard_map/pallas_call | solution.py:901

commit v5 on v4

--- a/solution.py
+++ b/solution.py
@@ -27,14 +27,14 @@
 NN = (((1,), (0,)), ((), ()))
 TN = (((0,), (0,)), ((), ()))
 PARTS, GROUPS = 3, 3
-SMALL = (96, 80, 96)
+SMALL = (96, 80, 80)
 LARGE = tuple(4 * size for size in SMALL)
 SPAN = tuple(4 * size for size in LARGE)
 AXES = ("yzx", "zxy", "xyz")
 SLOTS = 14
 START = (0, PARTS * SPAN[0], PARTS * (SPAN[0] + SPAN[1]))
 LINES = PARTS * sum(SPAN)
-FIRST_FILLED, SECOND_FILLED = SLOTS * 3 * C_MID, START[2] + SLOTS // 2 * 3 * C_MID
+FIRST_FILLED = SLOTS * 3 * C_MID
 EARLY = 8
 SIDES = [(-1, -1), (0, -1), (1, -1), (-1, 1), (0, 1), (1, 1)]
 
@@ -63,6 +63,12 @@
     gate = 1.0 / (1.0 + jnp.exp(-unit))
     slope = grad * (gate * (1.0 + unit * (1.0 - gate)))
     return inverse * (slope - unit * jnp.mean(slope * unit, axis=-1, keepdims=True))
+
+
+def rest_at(pair):
+    last = SLOTS // 2 - 1
+    at = jnp.where(pair == last, FIRST_FILLED, START[2] + pair * (3 * C_MID) + 2 * C_MID)
+    return pl.multiple_of(at, 16)
 
 
 def wrap(index, step, count):
@@ -101,16 +107,15 @@
             items.append(self.copy(2 + number, self.edges.at[1 - side], self.rims.at[0, side, 1 - dr], 0, dr, dc))
         return items
 
+    def far_rows(self, number, at):
+        return self.copy(number, self.rows(0, at), self.rows(1, at), self.ahead, 0, 0)
+
     def far_tile(self):
-        middle = pl.ds(1, TH)
-        return self.copy(8, self.rows(0, middle), self.rows(1, middle), self.ahead, 0, 0)
+        return self.far_rows(8, pl.ds(1, TH))
 
     def far_rim(self):
-        return [
-            self.copy(9, self.rims.at[0], self.rims.at[1], self.ahead, 0, 0),
-            self.copy(10, self.rows(0, 0), self.rows(1, 0), self.ahead, 0, 0),
-            self.copy(11, self.rows(0, TH + 1), self.rows(1, TH + 1), self.ahead, 0, 0),
-        ]
+        rims = self.copy(9, self.rims.at[0], self.rims.at[1], self.ahead, 0, 0)
+        return [rims, self.far_rows(10, 0), self.far_rows(11, TH + 1)]
 
     def start(self, edges_ref):
         self.far_tile().start()
@@ -165,7 +170,7 @@
             lax.fori_loop(0, TH + 2, one, 0)
 
 
-def convolve(shifted, weights, total, full_at, full_tap, half_at, half_out, dims, flip, first):
+def convolve(shifted, weights, total, sources, dims, flip, first):
     half, chan = VOX // FR, shifted.shape[-1]
     joined = chan % 128 == 0
 
@@ -179,9 +184,9 @@
             return shifted[col, frame, pl.ds(row, TH)].reshape(half, chan)
 
         for out in range(FR):
-            terms = [(full_at + out, full_tap, col) for col in range(3)]
-            if out == half_out:
-                terms += [(half_at, 1, col) for col in range(3)]
+            terms = [(frame, time, col) for frame, time in sources[out] for col in range(3)]
+            if not terms:
+                continue
             if joined:
                 values = jnp.concatenate([data(frame, col) for frame, _, col in terms], axis=1)
                 taps = jnp.concatenate([tap(time, col) for _, time, col in terms], axis=dims[0][1][0])
@@ -244,13 +249,30 @@
     return items
 
 
-def canvas(place, tile, field):
+def pack_pictures(tile, packed):
+    for group in range(2):
+        total = tile[4 * group]
+        for number in range(4 * group + 1, min(4 * group + 4, 6)):
+            total = total + pltpu.roll(tile[number], TW * (number % 4), 1)
+        packed[group] = total
+
+
+def canvas(place, packed, field):
     t, r, c = place
-    field[1, :, pl.ds(pl.multiple_of(r * TH, TH), TH), :] = tile[...]
-    flat = [field[side].reshape(6 * N_ROW * TH, 128) for side in range(3)]
-    left = flat[0] * jnp.where(c == 0, 0.0, 1.0)
-    right = flat[2] * jnp.where(c == N_COL - 1, 0.0, 1.0)
-    return left + pltpu.roll(flat[1], TW, 1) + pltpu.roll(right, 2 * TW, 1)
+    field[1, :, pl.ds(pl.multiple_of(r * TH, TH), TH), :] = packed[...]
+    lane = iota((N_ROW * TH, 128), 1)
+    low = jnp.where(c == 0, TW, 0)
+    high = jnp.where(c == N_COL - 1, 2 * TW, 3 * TW)
+    pictures = []
+    for number in range(6):
+        group, place_in = divmod(number, 4)
+        total = jnp.zeros((N_ROW * TH, 128), F32)
+        for side in range(3):
+            turn = (TW * (side - place_in)) % 128
+            moved = pltpu.roll(field[side, group], turn, 1) if turn else field[side, group]
+            total = jnp.where((lane >= TW * side) & (lane < TW * side + TW), moved, total)
+        pictures.append(jnp.where((lane >= low) & (lane < high), total, 0.0))
+    return jnp.concatenate(pictures, axis=0)
 
 
 def high_dot(a, b):
@@ -286,10 +308,10 @@
     return [result[:, m * 128 : (m + 1) * 128] for m in range(len(maps))]
 
 
-def picture_loss(place, x_tile, y_tile, x_field, y, mean_y, square_y, bands, spread):
+def picture_loss(place, x_tile, y_tile, x_packed, x_field, y, mean_y, square_y, bands, spread):
     t, r, c = place
     across, down, down_own = bands
-    x = canvas(place, x_tile, x_field)
+    x = canvas(place, x_packed, x_field)
     mean_x, square_x, cross = blurred([x, x * x, x * y], across, down)
     rows = 6 * WINDOW
     var_x = square_x - mean_x * mean_x
@@ -415,6 +437,9 @@
 
     def run(self, stage):
         s, group = self.s, self.group
+        if stage == 5:
+            for earlier in range(4):
+                self.left(earlier)
         for part in range(PARTS):
             if stage > 0:
                 for step in (1, 3, 2):
@@ -442,13 +467,16 @@
             if stage == 4:
                 self.share(part, 0).start()
 
+    def left(self, stage):
+        for part in range(PARTS):
+            for step in (1, 2, 3):
+                self.send(part, stage, step).wait_send()
+
     def settle(self):
+        self.left(4)
         for part in range(PARTS):
             for large in range(4):
                 self.share(part, large, True).wait_recv()
-            for stage in range(5):
-                for step in (1, 2, 3):
-                    self.send(part, stage, step).wait_send()
             for large in range(4):
                 self.share(part, large).wait_send()
 
@@ -568,28 +596,26 @@
     chunks(act)
     s.target[...] = jnp.zeros(s.target.shape, F32)
     s.target[:, :, 0:TW] = targ[...]
+    pack_pictures(s.target, s.y_packed)
     pl.semaphore_wait(barrier, len(around))
 
     halo0 = Halo(place, 1, C_IN, s.own0, s.other0, s.rims0, s.edges0, s.lines0, s.send0, s.recv0)
     halo1 = Halo(place, 1, C_MID, s.own1, s.other1, s.rims1, s.edges1, s.lines1, s.send1, s.recv1)
     halo2 = Halo(place, -1, C_MID, s.own2, s.other2, s.rims2, s.edges2, s.lines1, s.send2, s.recv2)
     halo0.start(s.columns)
-    y_copies = picture_copies(place, s.target, s.y_field, s.send_y, s.recv_y)
+    y_copies = picture_copies(place, s.y_packed, s.y_field, s.send_y, s.recv_y)
     for copy in y_copies:
         copy.start()
-    mates[0].start()
     bands = (s.across, s.down, s.down_own)
     picture_bands(place, *bands)
 
     halo0.arrived(0)
     halo0.shift(0, s.shift0, FR)
-    mates[1].start()
     loads[0].wait()
-    convolve(s.shift0, w1, s.pre, FR, 2, FR, 1, NT, False, True)
+    convolve(s.shift0, w1, s.pre, ([(2, 2)], [(3, 2), (2, 1)]), NT, False, True)
     halo0.arrived(1)
     halo0.shift(1, s.shift0, 0)
-    mates[2].start()
-    convolve(s.shift0, w1, s.pre, 0, 0, 1, 0, NT, False, False)
+    convolve(s.shift0, w1, s.pre, ([(0, 0), (1, 1)], [(1, 0)]), NT, False, False)
 
     def act_first(rows, step):
         values = silu_forward(s.pre[rows, :])
@@ -597,15 +623,16 @@
 
     chunks(act_first)
     halo1.start(s.columns)
+    for number in (0, 1, 2):
+        mates[number].start()
     for copy in y_copies:
         copy.wait_recv()
-    s.y_full[...] = canvas(place, s.target, s.y_field)
+    s.y_full[...] = canvas(place, s.y_packed, s.y_field)
     s.y_blur[0], s.y_blur[1] = blurred([s.y_full[...], s.y_full[...] * s.y_full[...]], s.across, s.down)
     halo1.arrived(0)
     halo1.shift(0, s.shift1, FR)
-    mates[3].start()
     loads[1].wait()
-    convolve(s.shift1, w2, s.block, FR, 2, FR, 1, NN, False, True)
+    convolve(s.shift1, w2, s.block, ([(2, 2)], [(3, 2), (2, 1)]), NN, False, True)
 
     def shortcut(rows, step):
         s.block[rows, :] += lax.dot_general(features(step), ws[...], NT, preferred_element_type=F32)
@@ -613,8 +640,7 @@
     chunks(shortcut)
     halo1.arrived(1)
     halo1.shift(1, s.shift1, 0)
-    mates[4].start()
-    convolve(s.shift1, w2, s.block, 0, 0, 1, 0, NN, False, False)
+    convolve(s.shift1, w2, s.block, ([(0, 0), (1, 1)], [(1, 0)]), NN, False, False)
 
     s.headf[...] = jnp.zeros(s.headf.shape, F32)
     s.headf[0:3, :] = head[...].astype(F32)
@@ -637,13 +663,16 @@
         for frame in range(FR):
             s.image[color * FR + frame] = s.spread[pl.ds(frame * 64 + color, TH, stride=8), :]
 
-    x_copies = picture_copies(place, s.image, s.x_field, s.send_x, s.recv_x)
+    pack_pictures(s.image, s.x_packed)
+    x_copies = picture_copies(place, s.x_packed, s.x_field, s.send_x, s.recv_x)
     for copy in x_copies:
         copy.start()
+    for number in (3, 4):
+        mates[number].start()
     for copy in x_copies:
         copy.wait_recv()
     loss = picture_loss(
-        place, s.image, s.target, s.x_field, s.y_full[...], s.y_blur[0], s.y_blur[1], bands, s.spread
+        place, s.image, s.target, s.x_packed, s.x_field, s.y_full[...], s.y_blur[0], s.y_blur[1], bands, s.spread
     )
 
     grad_head = None
@@ -678,12 +707,8 @@
     s.grads[1, :, 0:VOX] = s.values1[...].T.astype(BF16)
     mates[5].start()
     groups = [Reduce(s, place, group, result) for group in range(GROUPS)]
-    s.flat[FIRST_FILLED : START[2], :] = jnp.zeros((START[2] - FIRST_FILLED, 128), F32)
-    s.flat[SECOND_FILLED:LINES, :] = jnp.zeros((LINES - SECOND_FILLED, 128), F32)
+    s.flat[FIRST_FILLED + C_MID : START[2], :] = jnp.zeros((START[2] - FIRST_FILLED - C_MID, 128), F32)
     small.start(1, small.finish(0))
-    halo2.arrived(0)
-    halo2.shift(0, s.shift2, 0)
-    convolve(s.shift2, w2, s.back, 0, 2, 1, 0, NT, True, True)
     for number in (3, 4, 5):
         mates[number].wait_recv()
 
@@ -703,14 +728,18 @@
         at = pl.multiple_of(START[2] + pair * (3 * C_MID), 16)
         s.flat[pl.ds(at, C_MID), :] = halves[0][:, 0:128]
         s.flat[pl.ds(at + C_MID, C_MID), :] = halves[1][:, 0:128]
-        s.flat[pl.ds(at + 2 * C_MID, C_MID), :] = jnp.concatenate([halves[0][:, 128:], halves[1][:, 128:]], axis=1)
+        s.flat[pl.ds(rest_at(pair), C_MID), :] = jnp.concatenate([halves[0][:, 128:], halves[1][:, 128:]], axis=1)
         return carry
 
-    lax.fori_loop(0, SLOTS // 2, second, 0)
+    lax.fori_loop(0, 3, second, 0)
+    halo2.arrived(0)
+    lax.fori_loop(3, SLOTS // 2, second, 0)
     groups[2].run(0)
+    halo2.shift(0, s.shift2, 0)
+    convolve(s.shift2, w2, s.back, ([(0, 2), (1, 1)], [(1, 2)]), NT, True, True)
     halo2.arrived(1)
     halo2.shift(1, s.shift2, FR)
-    convolve(s.shift2, w2, s.back, FR, 0, FR, 1, NT, True, False)
+    convolve(s.shift2, w2, s.back, ([(2, 0)], [(3, 0), (2, 1)]), NT, True, False)
 
     def back_first(rows, step):
         s.values1[rows, :] = silu_backward(s.pre[rows, :], s.back[rows, :])
@@ -744,33 +773,34 @@
 
     lax.fori_loop(0, EARLY // 2, first, 0)
     groups[0].run(0)
-    groups[2].run(2)
     lax.fori_loop(EARLY // 2, SLOTS // 2 - 1, first, 0)
     first_alone(SLOTS - 2)
     first_alone(SLOTS - 1)
     groups[1].run(0)
+    groups[0].run(1)
+    groups[2].run(2)
+    groups[1].run(1)
+    small.start(3, small.finish(2))
+    groups[0].run(2)
     groups[2].run(3)
-    small.start(3, small.finish(2))
-    groups[0].run(1)
+    groups[1].run(2)
+    groups[0].run(3)
+    small_out[...] = small.finish(3)
     groups[2].run(4)
-    groups[1].run(1)
-    groups[0].run(2)
-    groups[1].run(2)
-    small_out[...] = small.finish(3)
-    groups[0].run(3)
     groups[1].run(3)
     groups[0].run(4)
-    groups[2].run(5)
     groups[1].run(4)
-    groups[0].run(5)
-    groups[1].run(5)
-    for group in groups:
-        group.settle()
     for halo in (halo0, halo1, halo2):
         halo.sent()
     for copy in x_copies + y_copies + mates:
         copy.wait_send()
     small.settle()
+    groups[0].run(5)
+    groups[2].run(5)
+    groups[0].settle()
+    groups[2].settle()
+    groups[1].run(5)
+    groups[1].settle()
 
 
 def halo_scratch(number, chan, copies):
@@ -824,8 +854,10 @@
         ("colors", pltpu.VMEM((4, 128, 24), BF16)),
         ("image", pltpu.VMEM((6, TH, 128), F32)),
         ("target", pltpu.VMEM((6, TH, 128), F32)),
-        ("x_field", pltpu.VMEM((3, 6, N_ROW * TH, 128), F32)),
-        ("y_field", pltpu.VMEM((3, 6, N_ROW * TH, 128), F32)),
+        ("x_packed", pltpu.VMEM((2, TH, 128), F32)),
+        ("y_packed", pltpu.VMEM((2, TH, 128), F32)),
+        ("x_field", pltpu.VMEM((3, 2, N_ROW * TH, 128), F32)),
+        ("y_field", pltpu.VMEM((3, 2, N_ROW * TH, 128), F32)),
         ("across", pltpu.VMEM((128, 128), F32)),
         ("down", pltpu.VMEM((6 * WINDOW, 6 * N_ROW * TH), F32)),
         ("down_own", pltpu.VMEM((6 * TH, 6 * WINDOW), F32)),
@@ -856,7 +888,7 @@
         at = pl.multiple_of(START[2] + step * (3 * C_MID), 16)
         wide2[2 * pair, :, 0:128] = flat[core, pl.ds(at, C_MID), :].astype(F32)
         wide2[2 * pair + 1, :, 0:128] = flat[core, pl.ds(at + C_MID, C_MID), :].astype(F32)
-        rest = flat[core, pl.ds(at + 2 * C_MID, C_MID), :].astype(F32)
+        rest = flat[core, pl.ds(rest_at(step), C_MID), :].astype(F32)
         wide2[2 * pair, :, 128:] = rest[:, 0:64]
         wide2[2 * pair + 1, :, 128:] = rest[:, 64:]
         return carry

time: 114 us -> 107 us (0.939)
  Pallas kernels: 114 us -> 106 us
    pallas_call x1, Pallas kernels: 108 us -> 100 us  [body(): pl.pallas_call(kernel, out_shape=[pltpu.VMEM((2, LINES, 128), BF16), pltp...]
where the time goes in v5:
time: 107 us
  Pallas kernels  106 us (99%)
    pallas_call x1, Pallas kernels, body(): pl.pallas_call(kernel, out_shape=[pltpu.VMEM((2, LINES, 128), BF16), pltp...  100 us
    pallas_call x1, Pallas kernels, body(): pl.pallas_call(widen, out_shape=[jax.ShapeDtypeStruct((27, C_MID, C_IN),...  5.71 us

profile of v5, /device:TPU:1, one launch (start us, length us, event | category | flops | bytes accessed | tf_op | source)
XLA Modules:
  0.0 106.8 jit_solution(9540318330071277222)
XLA Ops:
  0.6 100.5 %shard_map.101 = (bf16[2,12288,128]{2,1,0:T(8,128)(2,1)S(1)}, f32[8,128]{1,0:T(8,128)S(1)}) custom-call(bf16[2,8,32,384]{3,2,1,0:T(8,128)(2,1)} %feat.1, bf16[27,192,384]{2,1,0:T(8,128)(2,1)} %bitcast.14, bf16[27,192,192]{2,1,0:T(8,128)(2,1)} %bitcast.15, bf16[192,384]{1,0:T(8,128)(2,1)} %bitcast.16, bf16[3,192]{1,0:T(4,128)(2,1)} %bitcast.18, ...), custom_call_target="tpu_custom_call" | custom-call | tf_op jit(solution)/shard_map/pallas_call | solution.py:916
  101.1 5.7 %shard_map.102 = (f32[27,192,384]{2,1,0:T(8,128)}, f32[192,384]{1,0:T(8,128)}, f32[27,192,192]{2,1,0:T(8,128)}, f32[3,192]{1,0:T(4,128)}, f32[1,1]{1,0:T(1,128)}) custom-call(bf16[2,12288,128]{2,1,0:T(8,128)(2,1)S(1)} %get-tuple-element.12.flat, f32[8,128]{1,0:T(8,128)S(1)} %get-tuple-element.13.small_ref), custom_call_target="tpu_custom_call" | custom-call | tf_op jit(solution)/shard_map/pallas_call | solution.py:933

commit v6 on v5

--- a/solution.py
+++ b/solution.py
@@ -12,6 +12,7 @@
 MESH = pl.DeviceIdType.MESH
 F32, BF16 = jnp.float32, jnp.bfloat16
 HIGH = lax.Precision.HIGHEST
+LAST = BF16
 EPSILON = 1e-06
 HUBER_BETA = 0.05
 SSIM_CONST_A = 0.0004
@@ -406,8 +407,8 @@
             where = (group, part, step - 1, pl.ds(0, self.large))
             return self.copy(part, 0, 0, step, s.stage0.at[where], s.inbox0.at[where])
         if stage == 1:
-            src = s.sum1.at[group, part, pl.ds(pl.multiple_of(self.at(part, 1, step) * self.small, 16), self.small), :]
-            return self.copy(part, 1, 1, step, src, s.inbox1.at[group, part, step - 1, pl.ds(0, self.small)])
+            where = (group, part, step - 1, pl.ds(0, self.small))
+            return self.copy(part, 1, 1, step, s.stage1.at[where], s.inbox1.at[where])
         if stage == 2:
             block = s.last.at[group, part, self.at(part, 2), pl.ds(0, self.small)]
             return self.copy(part, 2, 2, step, block, block)
@@ -454,12 +455,15 @@
             elif stage == 1:
                 total = [s.inbox0[group, part, index, large, :].astype(F32) for index in range(3)]
                 s.sum1[group, part, large, :] = s.flat[self.lines_of(part, 0), :] + (total[0] + total[1] + total[2])
+                for step in (2, 1, 3):
+                    at = pl.ds(pl.multiple_of(self.at(part, 1, step) * self.small, 16), self.small)
+                    s.stage1[group, part, step - 1, small, :] = s.sum1[group, part, at, :].astype(BF16)
             elif stage == 2:
                 own = s.sum1[group, part, pl.ds(pl.multiple_of(self.at(part, 1) * self.small, 16), self.small), :]
-                total = [s.inbox1[group, part, index, small, :] for index in range(3)]
-                s.last[group, part, self.at(part, 2), small, :] = own + (total[0] + total[1] + total[2])
+                total = [s.inbox1[group, part, index, small, :].astype(F32) for index in range(3)]
+                s.last[group, part, self.at(part, 2), small, :] = (own + (total[0] + total[1] + total[2])).astype(LAST)
             elif stage == 3:
-                total = [s.last[group, part, index, small, :] for index in range(4)]
+                total = [s.last[group, part, index, small, :].astype(F32) for index in range(4)]
                 self.region(part, 0, 0)[...] = ((total[0] + total[1]) + (total[2] + total[3])).astype(BF16)
             if 0 < stage < 5:
                 for step in (2, 1, 3):
@@ -532,16 +536,19 @@
                 copy.wait_send()
 
 
-def kernel(feat, w1_hbm, w2_hbm, ws, head, targ, result, small_out, *scratch):
+def kernel(feat_hbm, w1_hbm, w2_hbm, ws_hbm, head, targ, result, small_out, *scratch):
     s = types.SimpleNamespace(**dict(zip(SCRATCH_NAMES, scratch)))
     t, r, c = lax.axis_index("tm"), lax.axis_index("row"), lax.axis_index("col")
     place = (t, r, c)
 
-    w1, w2 = s.w1, s.w2
+    feat, w1, w2, ws = s.feat, s.w1, s.w2, s.ws
     loads = [
         pltpu.make_async_copy(w1_hbm, w1, s.load.at[0]),
         pltpu.make_async_copy(w2_hbm, w2, s.load.at[1]),
+        pltpu.make_async_copy(feat_hbm, feat, s.load.at[2]),
+        pltpu.make_async_copy(ws_hbm, ws, s.load.at[3]),
     ]
+    loads[2].start()
     barrier = pltpu.get_barrier_semaphore()
     around = [(0, dr, dc) for dr in (-1, 0, 1, 2) for dc in (-1, 0, 1) if (dr, dc) != (0, 0)]
     around += [(-1, 0, 0), (1, 0, 0), (2, 0, 0), (0, 0, -2), (0, 0, 2), (0, 0, 4)]
@@ -583,8 +590,9 @@
         frame, row = tile_rows(step)
         return feat[frame, pl.ds(row, CHUNK // TW)].reshape(CHUNK, C_IN)
 
-    for load in loads:
-        load.start()
+    for number in (0, 1, 3):
+        loads[number].start()
+    loads[2].wait()
 
     def act(rows, step):
         raw = features(step)
@@ -632,6 +640,7 @@
     halo1.arrived(0)
     halo1.shift(0, s.shift1, FR)
     loads[1].wait()
+    loads[3].wait()
     convolve(s.shift1, w2, s.block, ([(2, 2)], [(3, 2), (2, 1)]), NN, False, True)
 
     def shortcut(rows, step):
@@ -823,7 +832,9 @@
     + [
         ("w1", pltpu.VMEM((27, C_MID, C_IN), BF16)),
         ("w2", pltpu.VMEM((27, C_MID, C_MID), BF16)),
-        ("load", pltpu.SemaphoreType.DMA((2,))),
+        ("feat", pltpu.VMEM((FR, TH, TW, C_IN), BF16)),
+        ("ws", pltpu.VMEM((C_MID, C_IN), BF16)),
+        ("load", pltpu.SemaphoreType.DMA((4,))),
         ("lines0", pltpu.VMEM((2, FR, 16, C_IN), F32)),
         ("lines1", pltpu.VMEM((2, FR, 16, C_MID), F32)),
         ("columns", pltpu.VMEM((2, FR * TH, C_IN), F32)),
@@ -840,8 +851,9 @@
         ("stage0", pltpu.VMEM((GROUPS, PARTS, 3, max(LARGE), 128), BF16)),
         ("inbox0", pltpu.VMEM((GROUPS, PARTS, 3, max(LARGE), 128), BF16)),
         ("sum1", pltpu.VMEM((GROUPS, PARTS, max(LARGE), 128), F32)),
-        ("inbox1", pltpu.VMEM((GROUPS, PARTS, 3, max(SMALL), 128), F32)),
-        ("last", pltpu.VMEM((GROUPS, PARTS, 4, max(SMALL), 128), F32)),
+        ("stage1", pltpu.VMEM((GROUPS, PARTS, 3, max(SMALL), 128), BF16)),
+        ("inbox1", pltpu.VMEM((GROUPS, PARTS, 3, max(SMALL), 128), BF16)),
+        ("last", pltpu.VMEM((GROUPS, PARTS, 4, max(SMALL), 128), LAST)),
         ("ring_send", pltpu.SemaphoreType.DMA((GROUPS * PARTS * 15,))),
         ("ring_recv", pltpu.SemaphoreType.DMA((GROUPS * PARTS * 15,))),
         ("share_send", pltpu.SemaphoreType.DMA((GROUPS * PARTS * 4,))),
@@ -893,13 +905,13 @@
         wide2[2 * pair + 1, :, 128:] = rest[:, 64:]
         return carry
 
-    for piece in range(7):
-        lax.fori_loop(4 * piece, 4 * piece + 4, one1, 0)
-        last = min(4 * piece + 4, 27)
-        rows = pl.ds(4 * piece, last - 4 * piece)
+    cuts = (0, 2, 6, 12, 18, 24, 28)
+    for low, high in zip(cuts[:-1], cuts[1:]):
+        rows = pl.ds(low, min(high, 27) - low)
+        lax.fori_loop(low, high, one1, 0)
         copies.append(pltpu.make_async_copy(wide1.at[rows], g1.at[rows], sems.at[len(copies)]))
         copies[-1].start()
-        lax.fori_loop(2 * piece, 2 * piece + 2, one2, 0)
+        lax.fori_loop(low // 2, high // 2, one2, 0)
         copies.append(pltpu.make_async_copy(wide2.at[rows], g2.at[rows], sems.at[len(copies)]))
         copies[-1].start()
     copies.append(pltpu.make_async_copy(wide1.at[27], gs, sems.at[len(copies)]))
@@ -916,7 +928,7 @@
     flat, small = pl.pallas_call(
         kernel,
         out_shape=[pltpu.VMEM((2, LINES, 128), BF16), pltpu.VMEM((8, 128), F32)],
-        in_specs=[vmem, hbm, hbm, vmem, vmem, vmem],
+        in_specs=[hbm, hbm, hbm, hbm, vmem, vmem],
         out_specs=[vmem] * 2,
         scratch_shapes=[shape for _, shape in SCRATCH],
         compiler_params=pltpu.CompilerParams(

time: 107 us -> 105 us (0.981)
    pallas_call x1, Pallas kernels: 100 us -> 98.9 us  [body(): pl.pallas_call(kernel, out_shape=[pltpu.VMEM((2, LINES, 128), BF16), pltp...]
where the time goes in v6:
time: 105 us
  Pallas kernels  105 us (100%)
    pallas_call x1, Pallas kernels, body(): pl.pallas_call(kernel, out_shape=[pltpu.VMEM((2, LINES, 128), BF16), pltp...  98.9 us
    pallas_call x1, Pallas kernels, body(): pl.pallas_call(widen, out_shape=[jax.ShapeDtypeStruct((27, C_MID, C_IN),...  5.63 us

profile of v6, /device:TPU:1, one launch (start us, length us, event | category | flops | bytes accessed | tf_op | source)
XLA Modules:
  0.0 105.2 jit_solution(17701911871531729937)
XLA Ops:
  0.6 98.9 %shard_map.101 = (bf16[2,12288,128]{2,1,0:T(8,128)(2,1)S(1)}, f32[8,128]{1,0:T(8,128)S(1)}) custom-call(bf16[2,8,32,384]{3,2,1,0:T(8,128)(2,1)} %feat_hbm.1, bf16[27,192,384]{2,1,0:T(8,128)(2,1)} %bitcast.14, bf16[27,192,192]{2,1,0:T(8,128)(2,1)} %bitcast.15, bf16[192,384]{1,0:T(8,128)(2,1)} %bitcast.16, bf16[3,192]{1,0:T(4,128)(2,1)} %bitcast.18, ...), custom_call_target="tpu_custom_call" | custom-call | tf_op jit(solution)/shard_map/pallas_call | solution.py:928
  99.5 5.6 %shard_map.102 = (f32[27,192,384]{2,1,0:T(8,128)}, f32[192,384]{1,0:T(8,128)}, f32[27,192,192]{2,1,0:T(8,128)}, f32[3,192]{1,0:T(4,128)}, f32[1,1]{1,0:T(1,128)}) custom-call(bf16[2,12288,128]{2,1,0:T(8,128)(2,1)S(1)} %get-tuple-element.12.flat, f32[8,128]{1,0:T(8,128)S(1)} %get-tuple-element.13.small_ref), custom_call_target="tpu_custom_call" | custom-call | tf_op jit(solution)/shard_map/pallas_call | solution.py:945

commit v7 on v6

--- a/solution.py
+++ b/solution.py
@@ -740,9 +740,9 @@
         s.flat[pl.ds(rest_at(pair), C_MID), :] = jnp.concatenate([halves[0][:, 128:], halves[1][:, 128:]], axis=1)
         return carry
 
-    lax.fori_loop(0, 3, second, 0)
+    lax.fori_loop(0, 2, second, 0)
     halo2.arrived(0)
-    lax.fori_loop(3, SLOTS // 2, second, 0)
+    lax.fori_loop(2, SLOTS // 2, second, 0)
     groups[2].run(0)
     halo2.shift(0, s.shift2, 0)
     convolve(s.shift2, w2, s.back, ([(0, 2), (1, 1)], [(1, 2)]), NT, True, True)

time: 105 us -> 105 us (level)
  no operation moved by 1% of the time
where the time goes in v7:
time: 105 us
  Pallas kernels  104 us (99%)
    pallas_call x1, Pallas kernels, body(): pl.pallas_call(kernel, out_shape=[pltpu.VMEM((2, LINES, 128), BF16), pltp...  98.3 us
    pallas_call x1, Pallas kernels, body(): pl.pallas_call(widen, out_shape=[jax.ShapeDtypeStruct((27, C_MID, C_IN),...  5.63 us

profile of v7, /device:TPU:1, one launch (start us, length us, event | category | flops | bytes accessed | tf_op | source)
XLA Modules:
  0.0 104.6 jit_solution(6625463216733672106)
XLA Ops:
  0.6 98.3 %shard_map.101 = (bf16[2,12288,128]{2,1,0:T(8,128)(2,1)S(1)}, f32[8,128]{1,0:T(8,128)S(1)}) custom-call(bf16[2,8,32,384]{3,2,1,0:T(8,128)(2,1)} %feat_hbm.1, bf16[27,192,384]{2,1,0:T(8,128)(2,1)} %bitcast.14, bf16[27,192,192]{2,1,0:T(8,128)(2,1)} %bitcast.15, bf16[192,384]{1,0:T(8,128)(2,1)} %bitcast.16, bf16[3,192]{1,0:T(4,128)(2,1)} %bitcast.18, ...), custom_call_target="tpu_custom_call" | custom-call | tf_op jit(solution)/shard_map/pallas_call | solution.py:928
  98.9 5.6 %shard_map.102 = (f32[27,192,384]{2,1,0:T(8,128)}, f32[192,384]{1,0:T(8,128)}, f32[27,192,192]{2,1,0:T(8,128)}, f32[3,192]{1,0:T(4,128)}, f32[1,1]{1,0:T(1,128)}) custom-call(bf16[2,12288,128]{2,1,0:T(8,128)(2,1)S(1)} %get-tuple-element.12.flat, f32[8,128]{1,0:T(8,128)S(1)} %get-tuple-element.13.small_ref), custom_call_target="tpu_custom_call" | custom-call | tf_op jit(solution)/shard_map/pallas_call | solution.py:945

commit v8 on v7

--- a/solution.py
+++ b/solution.py
@@ -862,7 +862,7 @@
         ("small_send", pltpu.SemaphoreType.DMA((12,))),
         ("small_recv", pltpu.SemaphoreType.DMA((12,))),
         ("headf", pltpu.VMEM((8, C_MID), F32)),
-        ("spread", pltpu.VMEM((128, 128), F32)),
+        ("spread", pltpu.VMEM((136, 128), F32)),
         ("colors", pltpu.VMEM((4, 128, 24), BF16)),
         ("image", pltpu.VMEM((6, TH, 128), F32)),
         ("target", pltpu.VMEM((6, TH, 128), F32)),

time: 105 us -> 105 us (level)
  no operation moved by 1% of the time
where the time goes in v8:
time: 105 us
  Pallas kernels  104 us (99%)
    pallas_call x1, Pallas kernels, body(): pl.pallas_call(kernel, out_shape=[pltpu.VMEM((2, LINES, 128), BF16), pltp...  98.3 us
    pallas_call x1, Pallas kernels, body(): pl.pallas_call(widen, out_shape=[jax.ShapeDtypeStruct((27, C_MID, C_IN),...  5.63 us

profile of v8, /device:TPU:1, one launch (start us, length us, event | category | flops | bytes accessed | tf_op | source)
XLA Modules:
  0.0 104.6 jit_solution(10091728616518660235)
XLA Ops:
  0.6 98.3 %shard_map.101 = (bf16[2,12288,128]{2,1,0:T(8,128)(2,1)S(1)}, f32[8,128]{1,0:T(8,128)S(1)}) custom-call(bf16[2,8,32,384]{3,2,1,0:T(8,128)(2,1)} %feat_hbm.1, bf16[27,192,384]{2,1,0:T(8,128)(2,1)} %bitcast.14, bf16[27,192,192]{2,1,0:T(8,128)(2,1)} %bitcast.15, bf16[192,384]{1,0:T(8,128)(2,1)} %bitcast.16, bf16[3,192]{1,0:T(4,128)(2,1)} %bitcast.18, ...), custom_call_target="tpu_custom_call" | custom-call | tf_op jit(solution)/shard_map/pallas_call | solution.py:928
  98.9 5.6 %shard_map.102 = (f32[27,192,384]{2,1,0:T(8,128)}, f32[192,384]{1,0:T(8,128)}, f32[27,192,192]{2,1,0:T(8,128)}, f32[3,192]{1,0:T(4,128)}, f32[1,1]{1,0:T(1,128)}) custom-call(bf16[2,12288,128]{2,1,0:T(8,128)(2,1)S(1)} %get-tuple-element.12.flat, f32[8,128]{1,0:T(8,128)S(1)} %get-tuple-element.13.small_ref), custom_call_target="tpu_custom_call" | custom-call | tf_op jit(solution)/shard_map/pallas_call | solution.py:945
